TPU v7x, 512 devices: a whole 4x8x8 slice. The times are simulated.
512 devices in a mesh: dp: 8 (over y), node: 8 (over x, core), local: 8 (over z).
Axes of the slice: x: 4, y: 8, z: 8, core: 2. Of those that a mesh axis runs over, the one named last changes fastest.
Arguments:
- tokens: bfloat16 [4096, 3584], P(('dp', 'node', 'local')), may hold values from -6 to 6
- grad_out: bfloat16 [4096, 3584], P(('dp', 'node', 'local')), may hold values from -6 to 6
- router_gates: bfloat16 [4096, 4], P(('dp', 'node', 'local')), may hold values from 0.19921875 to 1
- groups: int32 [4096, 4], P(('dp', 'node', 'local')), may hold values from 0 to 7, all different within a row; in each aligned block of 8 rows (0 to 7, 8 to 15, ...) at most 6 rows name the same one
- w_gate: bfloat16 [8, 3584, 1024], P('node', 'dp', 'local'), may hold values from -0.09375 to 0.09375
- w_up: bfloat16 [8, 3584, 1024], P('node', 'dp', 'local'), may hold values from -0.09375 to 0.09375
- w_down: bfloat16 [8, 1024, 3584], P('node', 'local', 'dp'), may hold values from -0.1875 to 0.1875
Outputs:
- grad_tokens: bfloat16 [4096, 3584], P(('dp', 'node', 'local'))
- grad_gates: bfloat16 [4096, 4], P(('dp', 'node', 'local'))
- grad_gate: bfloat16 [8, 3584, 1024], P('node', None, 'local')
- grad_up: bfloat16 [8, 3584, 1024], P('node', None, 'local')
- grad_down: bfloat16 [8, 1024, 3584], P('node', 'local')
Inputs may be any that keep to these rules, and one draw needn't show every extreme that they name: Each token names 4 different node groups. Among the 8 tokens of one device no group is named by more than 6 tokens, a bound that some block reaches.
All inputs are finite; a program needn't handle non-finite values.
Results may differ from a plain program's by a relative error of at most 0.017.
Values may be sent and summed in bfloat16 or wider, within the bound.
No kernel may reach another device: no remote copies, remote signals or barrier semaphores. Data moves between devices by JAX's collectives and lax.ppermute only.
A program may use at most 64 MiB of HBM per device.

v0:
```python
import jax
import jax.numpy as jnp
from jax import lax
from jax.sharding import PartitionSpec as P


def backprop(rows_in, rows_upstream, rows_weight, gate_mat, up_mat, down_mat):
    sources, capacity, model_width = rows_in.shape
    inputs = rows_in.reshape(sources * capacity, model_width)
    upstream = rows_upstream.reshape(sources * capacity, model_width)
    weight = rows_weight.reshape(sources * capacity).astype(jnp.float32)
    pre_gate = jnp.dot(inputs, gate_mat, preferred_element_type=jnp.float32)
    pre_up = jnp.dot(inputs, up_mat, preferred_element_type=jnp.float32)
    sigmoid_gate = jax.nn.sigmoid(pre_gate)
    activated = (pre_gate * sigmoid_gate * pre_up).astype(jnp.bfloat16)
    scaled = (weight[:, None] * upstream.astype(jnp.float32)).astype(jnp.bfloat16)
    shard_out = jnp.dot(activated, down_mat, preferred_element_type=jnp.float32)
    gate_part = jnp.sum(upstream.astype(jnp.float32) * shard_out, axis=1)
    grad_act = jnp.dot(scaled, down_mat.T, preferred_element_type=jnp.float32)
    gate_back = (grad_act * pre_up * sigmoid_gate * (1.0 + pre_gate * (1.0 - sigmoid_gate))).astype(
        jnp.bfloat16
    )
    up_back = (grad_act * pre_gate * sigmoid_gate).astype(jnp.bfloat16)
    input_part = jnp.dot(gate_back, gate_mat.T, preferred_element_type=jnp.float32)
    input_part = input_part + jnp.dot(up_back, up_mat.T, preferred_element_type=jnp.float32)
    term_gate = jnp.dot(inputs.T, gate_back, preferred_element_type=jnp.float32)
    term_up = jnp.dot(inputs.T, up_back, preferred_element_type=jnp.float32)
    term_down = jnp.dot(activated.T, scaled, preferred_element_type=jnp.float32)
    return (
        input_part.reshape(sources, capacity, model_width),
        gate_part.reshape(sources, capacity),
        (term_gate, term_up, term_down),
    )


def shards(tokens, grad_out, router_gates, groups, w_gate, w_up, w_down):
    node_count = lax.axis_size("node")
    local_count = lax.axis_size("local")
    token_count, model_width = tokens.shape
    top_count = groups.shape[1]
    capacity = max(2, 3 * token_count * top_count // (2 * node_count))
    group_hits = (
        groups[:, :, None] == jnp.arange(node_count, dtype=jnp.int32)[None, None, :]
    ).astype(jnp.float32)
    chosen = jnp.sum(group_hits, axis=1)
    earlier = jnp.tril(jnp.ones((token_count, token_count), jnp.float32), -1)
    position = jnp.dot(earlier, chosen, precision=lax.Precision.HIGHEST)
    slot_ids = jnp.arange(capacity, dtype=jnp.float32)
    slot_table = (position[:, :, None] == slot_ids[None, None, :]).astype(jnp.float32) * chosen[
        :, :, None
    ]
    select_float = jnp.transpose(slot_table, (1, 2, 0))
    select = select_float.astype(jnp.bfloat16)
    weight_table = jnp.sum(group_hits * router_gates.astype(jnp.float32)[:, :, None], axis=1)
    send_rows = jnp.einsum(
        "nct,td->ncd", select, tokens, preferred_element_type=jnp.float32
    ).astype(jnp.bfloat16)
    send_upstream = jnp.einsum(
        "nct,td->ncd", select, grad_out, preferred_element_type=jnp.float32
    ).astype(jnp.bfloat16)
    send_weight = jnp.einsum(
        "nct,tn->nc", select_float, weight_table, precision=lax.Precision.HIGHEST
    ).astype(jnp.bfloat16)
    gate_full, up_full = (
        lax.all_gather(w_gate, "dp", axis=1, tiled=True),
        lax.all_gather(w_up, "dp", axis=1, tiled=True),
    )
    down_full = lax.all_gather(w_down, "dp", axis=2, tiled=True)
    gate_mat = gate_full[0]
    up_mat = up_full[0]
    down_mat = down_full[0]
    copies = node_count * local_count
    wide_rows = jnp.broadcast_to(
        send_rows[:, None], (node_count, local_count, capacity, model_width)
    ).reshape(copies, capacity, model_width)
    wide_upstream = jnp.broadcast_to(
        send_upstream[:, None], (node_count, local_count, capacity, model_width)
    ).reshape(copies, capacity, model_width)
    wide_weight = jnp.broadcast_to(
        send_weight[:, None], (node_count, local_count, capacity)
    ).reshape(copies, capacity)
    flat_rows, flat_upstream, flat_weight = (
        lax.all_to_all(wide_rows, ("node", "local"), split_axis=0, concat_axis=0, tiled=True),
        lax.all_to_all(wide_upstream, ("node", "local"), split_axis=0, concat_axis=0, tiled=True),
        lax.all_to_all(wide_weight, ("node", "local"), split_axis=0, concat_axis=0, tiled=True),
    )
    input_part, gate_part, weight_terms = backprop(
        flat_rows, flat_upstream, flat_weight, gate_mat, up_mat, down_mat
    )
    back_input, back_gate = (
        lax.all_to_all(
            input_part.astype(jnp.bfloat16),
            ("node", "local"),
            split_axis=0,
            concat_axis=0,
            tiled=True,
        ),
        lax.all_to_all(
            gate_part.astype(jnp.bfloat16),
            ("node", "local"),
            split_axis=0,
            concat_axis=0,
            tiled=True,
        ),
    )
    returned = jnp.sum(
        back_input.reshape(node_count, local_count, capacity, model_width).astype(jnp.float32),
        axis=1,
    ).astype(jnp.bfloat16)
    returned_gate = jnp.sum(
        back_gate.reshape(node_count, local_count, capacity).astype(jnp.float32), axis=1
    ).astype(jnp.bfloat16)
    summed_gate, summed_up, summed_down = (
        lax.psum(weight_terms[0].astype(jnp.bfloat16), "dp").astype(jnp.float32),
        lax.psum(weight_terms[1].astype(jnp.bfloat16), "dp").astype(jnp.float32),
        lax.psum(weight_terms[2].astype(jnp.bfloat16), "dp").astype(jnp.float32),
    )
    grad_tokens = jnp.einsum(
        "nct,ncd->td", select, returned, preferred_element_type=jnp.float32
    ).astype(jnp.bfloat16)
    gate_by_group = jnp.einsum(
        "nct,nc->tn",
        select_float,
        returned_gate.astype(jnp.float32),
        precision=lax.Precision.HIGHEST,
    )
    grad_gates = jnp.sum(group_hits * gate_by_group[:, None, :], axis=2).astype(jnp.bfloat16)
    return (
        grad_tokens,
        grad_gates,
        summed_gate.astype(jnp.bfloat16)[None],
        summed_up.astype(jnp.bfloat16)[None],
        summed_down.astype(jnp.bfloat16)[None],
    )


def solution(mesh):
    placed = (
        P(("dp", "node", "local"), None),
        P(("dp", "node", "local"), None),
        P(("dp", "node", "local"), None),
        P(("dp", "node", "local"), None),
        P("node", "dp", "local"),
        P("node", "dp", "local"),
        P("node", "local", "dp"),
    )
    return jax.shard_map(
        shards,
        mesh=mesh,
        in_specs=placed,
        out_specs=(
            P(("dp", "node", "local"), None),
            P(("dp", "node", "local"), None),
            P("node", None, "local"),
            P("node", None, "local"),
            P("node", "local", None),
        ),
        check_vma=False,
    )
```

profile of v0, /device:TPU:2, one launch (start us, length us, event | category | flops | bytes accessed | tf_op | source)
XLA Modules:
  0.0 397.7 jit_solution(3847429184197204834)
XLA Ops:
  8.6 2.1 broadcast_in_dim.22
  10.7 14.2 %all-to-all-start.2 = ((bf16[64,6,3584]{2,1,0:T(8,128)(2,1)}), bf16[64,6,3584]{2,1,0:T(8,128)(2,1)}, u32[]{:S(2)}, u32[]{:S(2)}) async-start(bf16[64,6,3584]{2,1,0:T(8,128)(2,1)} %bitcast.66), calls=%async_computation.2 | async-start | bytes 7340032 | tf_op jit(solution)/shard_map/all_to_all | solution.py:83
  25.3 82.4 %all-to-all-done.2 = bf16[64,6,3584]{2,1,0:T(8,128)(2,1)} async-done(((bf16[64,6,3584]{2,1,0:T(8,128)(2,1)}), bf16[64,6,3584]{2,1,0:T(8,128)(2,1)}, u32[]{:S(2)}, u32[]{:S(2)}) %all-to-all-start.2) | async-done | bytes 2752544 | tf_op jit(solution)/shard_map/all_to_all | solution.py:83
  107.7 2.1 broadcast_in_dim.21
  109.7 8.5 %all-to-all-start.1 = ((bf16[64,6,3584]{2,1,0:T(8,128)(2,1)}), bf16[64,6,3584]{2,1,0:T(8,128)(2,1)}, u32[]{:S(2)}, u32[]{:S(2)}) async-start(bf16[64,6,3584]{2,1,0:T(8,128)(2,1)} %bitcast.65), calls=%async_computation.1 | async-start | bytes 7340032 | tf_op jit(solution)/shard_map/all_to_all | solution.py:84
  118.2 30.0 %all_gather.11 = bf16[1,3584,128]{2,1,0:T(8,128)(2,1)} all-gather(bf16[1,448,128]{2,1,0:T(8,128)(2,1)S(1)} %copy-done.5), channel_id=1, replica_groups=mesh['dp'=8,'node'=8,'local'=8] {'dp'}, dimensions={1}, use_global_device_ids=true | all-gather | bytes 1032192 | tf_op jit(solution)/shard_map/all_gather | solution.py:65
  148.3 28.6 %all_gather.10 = bf16[1,3584,128]{2,1,0:T(8,128)(2,1)} all-gather(bf16[1,448,128]{2,1,0:T(8,128)(2,1)S(1)} %copy-done.6), channel_id=1, replica_groups=mesh['dp'=8,'node'=8,'local'=8] {'dp'}, dimensions={1}, use_global_device_ids=true | all-gather | bytes 1032192 | tf_op jit(solution)/shard_map/all_gather | solution.py:66
  176.9 28.4 %all_gather.9 = bf16[1,128,3584]{1,2,0:T(8,128)(2,1)} all-gather(bf16[1,128,448]{1,2,0:T(8,128)(2,1)S(1)} %copy-done.7), channel_id=1, replica_groups=mesh['dp'=8,'node'=8,'local'=8] {'dp'}, dimensions={2}, use_global_device_ids=true | all-gather | bytes 1032192 | tf_op jit(solution)/shard_map/all_gather | solution.py:68
  205.2 4.0 reshape.77
  209.2 2.1 fusion.9
  212.3 6.0 %reshape.81 = f32[384,3584]{1,0:T(8,128)} reshape(bf16[64,6,3584]{2,1,0:T(8,128)(2,1)} %all-to-all-done.1) | data formatting | bytes 8257536 | tf_op jit(solution)/shard_map/convert_element_type | solution.py:16
  218.2 3.9 fusion.6
  222.9 10.2 %all-to-all-start.4 = ((bf16[64,1,6]{2,1,0:T(2,128)(2,1)}), bf16[64,1,6]{2,1,0:T(2,128)(2,1)S(1)}, u32[]{:S(2)}, u32[]{:S(2)}) async-start(bf16[64,1,6]{2,1,0:T(2,128)(2,1)} %convert_element_type.138), calls=%async_computation.4 | async-start | bytes 65536 | tf_op jit(solution)/shard_map/all_to_all | solution.py:98
  233.1 8.6 %all-to-all-done.4 = bf16[64,1,6]{2,1,0:T(2,128)(2,1)S(1)} async-done(((bf16[64,1,6]{2,1,0:T(2,128)(2,1)}), bf16[64,1,6]{2,1,0:T(2,128)(2,1)S(1)}, u32[]{:S(2)}, u32[]{:S(2)}) %all-to-all-start.4) | async-done | bytes 800 | tf_op jit(solution)/shard_map/all_to_all | solution.py:98
  243.0 13.4 %all_to_all.30 = bf16[64,1,6]{2,1,0:T(2,128)(2,1)S(1)} all-to-all(bf16[64,1,6]{2,1,0:T(2,128)(2,1)S(1)} %copy.49), channel_id=1, replica_groups=mesh['dp'=8,'node'=8,'local'=8] {'node','local'}, dimensions={0} | all-to-all | bytes 1536 | tf_op jit(solution)/shard_map/all_to_all | solution.py:85
  256.4 4.7 %multiply_convert_fusion = bf16[64,6,3584]{2,1,0:T(8,128)(2,1)} fusion(f32[64,6]{1,0:T(8,128)S(1)} %bitcast.67, bf16[64,6,3584]{2,1,0:T(8,128)(2,1)} %all-to-all-done.1), kind=kLoop, calls=%fused_computation | loop fusion | flops 4128768 | bytes 5506560 | tf_op jit(solution)/shard_map/convert_element_type | solution.py:16
  261.2 5.5 %convert_element_type.116 = bf16[384,3584]{1,0:T(8,128)(2,1)} reshape(bf16[64,6,3584]{2,1,0:T(8,128)(2,1)} %multiply_convert_fusion) | data formatting | bytes 5505024 | tf_op jit(solution)/shard_map/convert_element_type | solution.py:16
  266.6 3.0 multiply_convert_fusion.4
  269.6 0.9 fusion.7
  270.8 2.4 fusion
  273.2 5.4 %convert_element_type.121 = bf16[64,6,3584]{2,1,0:T(8,128)(2,1)} reshape(bf16[384,3584]{1,0:T(8,128)(2,1)} %fusion) | data formatting | bytes 5505024 | tf_op jit(solution)/shard_map/convert_element_type | solution.py:92
  278.6 6.4 %all-to-all-start.3 = ((bf16[64,6,3584]{2,1,0:T(8,128)(2,1)}), bf16[64,6,3584]{2,1,0:T(8,128)(2,1)}, u32[]{:S(2)}, u32[]{:S(2)}) async-start(bf16[64,6,3584]{2,1,0:T(8,128)(2,1)} %convert_element_type.121), calls=%async_computation.3 | async-start | bytes 7340032 | tf_op jit(solution)/shard_map/all_to_all | solution.py:91
  285.3 1.8 fusion.2
  287.2 1.8 fusion.1
  289.0 4.2 %fusion.3 = bf16[1,128,3584]{2,1,0:T(8,128)(2,1)} fusion(bf16[384,128]{1,0:T(8,128)(2,1)S(1)} %get-tuple-element.12, f32[384,3584]{1,0:T(8,128)} %reshape.81, f32[384]{0:T(512)S(1)} %reshape.82), kind=kOutput, calls=%fused_computation.10 | convolution fusion | flops 355532800 | bytes 6522368 | tf_op jit(solution)/shard_map/dot_general | solution.py:28
  293.2 74.6 %all-to-all-done.3 = bf16[64,6,3584]{2,1,0:T(8,128)(2,1)} async-done(((bf16[64,6,3584]{2,1,0:T(8,128)(2,1)}), bf16[64,6,3584]{2,1,0:T(8,128)(2,1)}, u32[]{:S(2)}, u32[]{:S(2)}) %all-to-all-start.3) | async-done | bytes 2752544 | tf_op jit(solution)/shard_map/all_to_all | solution.py:91
  367.9 2.8 bitcast_reduce_fusion
  370.7 0.9 fusion.4
  371.6 13.9 %all-reduce.3.cloned.1.call-done = (bf16[1,3584,128]{2,1,0:T(8,128)(2,1)}, bf16[1,3584,128]{2,1,0:T(8,128)(2,1)}, bf16[1,128,3584]{2,1,0:T(8,128)(2,1)}) async-done(((bf16[1,3584,128]{2,1,0:T(8,128)(2,1)}, bf16[1,3584,128]{2,1,0:T(8,128)(2,1)}, bf16[1,128,3584]{2,1,0:T(8,128)(2,1)}), (bf16[1,3584,128]{2,1,0:T(8,128)(2,1)}, bf16[1,3584,128]{2,1,0:T(8,128)(2,1)}, ...) | async-done | bytes 2752528 | tf_op jit(solution)/shard_map/psum | solution.py:114
  385.5 2.2 copy.78
  387.8 2.2 copy.79
  389.9 0.9 copy.80
  (48 shorter events, 5.4 us)
Async XLA Ops:
  7.2 1.0 copy-start
  10.7 14.2 %copy-start.8 = (bf16[8,3584]{1,0:T(8,128)(2,1)S(1)}, bf16[8,3584]{1,0:T(8,128)(2,1)}, u32[]{:S(2)}) copy-start(bf16[8,3584]{1,0:T(8,128)(2,1)} %param.8) | copy-start | bytes 172036
  10.7 97.0 %all-to-all-start.2 = ((bf16[64,6,3584]{2,1,0:T(8,128)(2,1)}), bf16[64,6,3584]{2,1,0:T(8,128)(2,1)}, u32[]{:S(2)}, u32[]{:S(2)}) async-start(bf16[64,6,3584]{2,1,0:T(8,128)(2,1)} %bitcast.66), calls=%async_computation.2 | async-start | bytes 7340032 | tf_op jit(solution)/shard_map/all_to_all | solution.py:83
  109.7 8.5 %copy-start.5 = (bf16[1,448,128]{2,1,0:T(8,128)(2,1)S(1)}, bf16[1,448,128]{2,1,0:T(8,128)(2,1)}, u32[]{:S(2)}) copy-start(bf16[1,448,128]{2,1,0:T(8,128)(2,1)} %param.11) | copy-start | bytes 344068
  109.7 38.5 %copy-start.6 = (bf16[1,448,128]{2,1,0:T(8,128)(2,1)S(1)}, bf16[1,448,128]{2,1,0:T(8,128)(2,1)}, u32[]{:S(2)}) copy-start(bf16[1,448,128]{2,1,0:T(8,128)(2,1)} %param.12) | copy-start | bytes 344068
  109.7 67.1 %copy-start.7 = (bf16[1,128,448]{1,2,0:T(8,128)(2,1)S(1)}, bf16[1,128,448]{1,2,0:T(8,128)(2,1)}, u32[]{:S(2)}) copy-start(bf16[1,128,448]{1,2,0:T(8,128)(2,1)} %param.13) | copy-start | bytes 344068
  109.7 102.5 %all-to-all-start.1 = ((bf16[64,6,3584]{2,1,0:T(8,128)(2,1)}), bf16[64,6,3584]{2,1,0:T(8,128)(2,1)}, u32[]{:S(2)}, u32[]{:S(2)}) async-start(bf16[64,6,3584]{2,1,0:T(8,128)(2,1)} %bitcast.65), calls=%async_computation.1 | async-start | bytes 7340032 | tf_op jit(solution)/shard_map/all_to_all | solution.py:84
  209.2 2.1 copy-start.2
  218.2 14.8 %copy-start.10 = (bf16[8,4]{0,1:T(4,128)(2,1)S(1)}, bf16[8,4]{0,1:T(4,128)(2,1)}, u32[]{:S(2)}) copy-start(bf16[8,4]{0,1:T(4,128)(2,1)} %param.9) | copy-start | bytes 196
  218.2 23.7 %copy-start.9 = (s32[8,4]{0,1:T(4,128)S(1)}, s32[8,4]{0,1:T(4,128)}, u32[]{:S(2)}) copy-start(s32[8,4]{0,1:T(4,128)} %param.10) | copy-start | bytes 388
  222.9 18.8 %all-to-all-start.4 = ((bf16[64,1,6]{2,1,0:T(2,128)(2,1)}), bf16[64,1,6]{2,1,0:T(2,128)(2,1)S(1)}, u32[]{:S(2)}, u32[]{:S(2)}) async-start(bf16[64,1,6]{2,1,0:T(2,128)(2,1)} %convert_element_type.138), calls=%async_computation.4 | async-start | bytes 65536 | tf_op jit(solution)/shard_map/all_to_all | solution.py:98
  266.6 3.0 copy-start.1
  269.6 1.2 copy-start.3
  278.6 89.3 %all-to-all-start.3 = ((bf16[64,6,3584]{2,1,0:T(8,128)(2,1)}), bf16[64,6,3584]{2,1,0:T(8,128)(2,1)}, u32[]{:S(2)}, u32[]{:S(2)}) async-start(bf16[64,6,3584]{2,1,0:T(8,128)(2,1)} %convert_element_type.121), calls=%async_computation.3 | async-start | bytes 7340032 | tf_op jit(solution)/shard_map/all_to_all | solution.py:91
  285.0 100.5 %all-reduce.3.cloned.1.call-start = ((), (), s32[]{:S(2)}) async-start(), calls=%async_computation.5 | async-start | bytes 5505024 | tf_op jit(solution)/shard_map/psum | solution.py:114
  385.5 4.4 %copy-start.4 = (bf16[1,128,3584]{2,1,0:T(8,128)(2,1)S(1)}, bf16[1,128,3584]{2,1,0:T(8,128)(2,1)}, u32[]{:S(2)}) copy-start(bf16[1,128,3584]{2,1,0:T(8,128)(2,1)} %get-tuple-element.18) | copy-start | bytes 2752516
Sparse Core Ops, SparseCore 0:
  293.4 92.1 all-reduce.2
where the time goes:
time: 399 us; the launch traced here: 398 us
  waiting for transfers between devices  180 us (45%)
  blocking collectives  100 us (25%)
  starting transfers between devices  39.3 us (10%)
  local copies, waits for them, and re-layouts  32.2 us (8%)
  matrix products  22.7 us (6%)
  between operations  14.3 us (4%)
  other arithmetic  9.3 us (2%)
    all_to_all x1, waiting for transfers between devices, shards(): lax.all_to_all(wide_rows, ('node', 'local'), split_axis=0, concat_axis=0,...  82.4 us
    all_to_all x1, waiting for transfers between devices, shards(): lax.all_to_all(input_part.astype(jnp.bfloat16), ('node', 'local'), split_...  74.6 us
    all_gather x1, blocking collectives, shards(): lax.all_gather(w_gate, 'dp', axis=1, tiled=True)  30 us
    all_gather x1, blocking collectives, shards(): lax.all_gather(w_up, 'dp', axis=1, tiled=True)  28.6 us
    all_gather x1, blocking collectives, shards(): down_full = lax.all_gather(w_down, 'dp', axis=2, tiled=True)  28.4 us
    all_to_all x1, starting transfers between devices, shards(): lax.all_to_all(wide_rows, ('node', 'local'), split_axis=0, concat_axis=0,...  14.2 us
    psum x1, waiting for transfers between devices, shards(): lax.psum(weight_terms[0].astype(jnp.bfloat16), 'dp').astype(jnp.float32)  13.9 us
    all_to_all x1, blocking collectives, shards(): lax.all_to_all(wide_weight, ('node', 'local'), split_axis=0, concat_axis=...  13.4 us
  transfers between devices with their start and end apart: 5, of which 4 were waited for; matrix products, arithmetic and copies ran while one was open for 5% of the time, Pallas kernels for 0%

commit v1 on v0

v1 whole, which is shorter than its diff:
```python
import functools

import jax
import jax.numpy as jnp
from jax import lax
from jax.experimental import pallas as pl
from jax.experimental.pallas import tpu as pltpu
from jax.sharding import PartitionSpec as P

LANES = 128
STEP = 512


def gradients_kernel(n_own, n_other, z_ref, sel_ref, w_hbm, *refs):
    own = refs[:n_own]
    other = refs[n_own : n_own + n_other]
    grads_ref, back_ref, part_ref, rows, weights, sems = refs[n_own + n_other :]
    half = rows.shape[0] // 2
    width = (rows.shape[1] - LANES) // 2
    block = own[0].shape[0]
    places = half // block
    here = z_ref[0]
    copies = [pltpu.make_async_copy(w_hbm, weights, sems.at[0])]
    offsets = ring_offsets(places)
    count = 0
    for base, group in ((0, own), (half, other)):
        index = 0
        for ref in group:
            for piece in range(ref.shape[0] // block):
                slot = lax.rem(here + (offsets[index] + places), places)
                start = pl.multiple_of(base + slot * block, block)
                copies.append(
                    pltpu.make_async_copy(
                        ref.at[pl.ds(piece * block, block)],
                        rows.at[pl.ds(start, block)],
                        sems.at[1 + count],
                    )
                )
                index += 1
                count += 1
    for copy in copies:
        copy.start()
    for copy in copies:
        copy.wait()

    def project(step, total):
        span = pl.ds(pl.multiple_of(step * STEP, STEP), STEP)
        return total + jnp.dot(
            rows[:, span], weights[span, : 2 * LANES], preferred_element_type=jnp.float32
        )

    def project_back(step, total):
        span = pl.ds(pl.multiple_of(step * STEP, STEP), STEP)
        shifted = pl.ds(pl.multiple_of(width + step * STEP, STEP), STEP)
        return total + jnp.dot(
            rows[:, shifted], weights[span, 2 * LANES :], preferred_element_type=jnp.float32
        )

    steps = width // STEP
    pre = lax.fori_loop(0, steps, project, jnp.zeros((2 * half, 2 * LANES), jnp.float32))
    raw = lax.fori_loop(0, steps, project_back, jnp.zeros((2 * half, LANES), jnp.float32))
    pre_gate, pre_up = pre[:, :LANES], pre[:, LANES:]
    sel = sel_ref[0:1, :]
    weight = jnp.sum(rows[:, 2 * width :].astype(jnp.float32) * sel, axis=1, keepdims=True)
    sigmoid = jax.nn.sigmoid(pre_gate)
    activated = (pre_gate * sigmoid * pre_up).astype(jnp.bfloat16).astype(jnp.float32)
    part_ref[...] = (jnp.sum(activated * raw, axis=1, keepdims=True) * sel).astype(jnp.bfloat16)
    grad_act = raw * weight
    back_gate = grad_act * pre_up * sigmoid * (1.0 + pre_gate * (1.0 - sigmoid))
    back_up = grad_act * pre_gate * sigmoid
    back = jnp.concatenate([back_gate, back_up], axis=1)
    back_ref[...] = back.astype(jnp.bfloat16)
    back_t = back.T.astype(jnp.bfloat16)
    activated_t = (activated * weight).T.astype(jnp.bfloat16)

    def terms(step, carry):
        span = pl.ds(pl.multiple_of(step * STEP, STEP), STEP)
        shifted = pl.ds(pl.multiple_of(width + step * STEP, STEP), STEP)
        grads_ref[: 2 * LANES, span] = jnp.dot(
            back_t, rows[:, span], preferred_element_type=jnp.float32
        ).astype(jnp.bfloat16)
        grads_ref[2 * LANES :, span] = jnp.dot(
            activated_t, rows[:, shifted], preferred_element_type=jnp.float32
        ).astype(jnp.bfloat16)
        return carry

    lax.fori_loop(0, steps, terms, 0)


def input_kernel(back_ref, part_ref, w_ref, own_ref, other_ref):
    half = own_ref.shape[0]
    width = own_ref.shape[1] - LANES

    def step_of(step, carry):
        span = pl.ds(pl.multiple_of(step * STEP, STEP), STEP)
        out = lax.dot_general(
            back_ref[...],
            w_ref[span, : 2 * LANES],
            (((1,), (1,)), ((), ())),
            preferred_element_type=jnp.float32,
        ).astype(jnp.bfloat16)
        own_ref[:, span] = out[:half]
        other_ref[:, span] = out[half:]
        return carry

    lax.fori_loop(0, width // STEP, step_of, 0)
    own_ref[:, width:] = part_ref[:half]
    other_ref[:, width:] = part_ref[half:]


def unpack_kernel(sum_ref, gate_ref, up_ref, down_ref):
    gate_ref[0] = sum_ref[:LANES, :].astype(jnp.float32).T.astype(jnp.bfloat16)
    up_ref[0] = sum_ref[LANES : 2 * LANES, :].astype(jnp.float32).T.astype(jnp.bfloat16)
    down_ref[0] = sum_ref[2 * LANES :, :]


def ring_offsets(places):
    offsets = [0]
    for hop in range(1, places // 2 + 1):
        offsets.append(-hop)
        if hop < places - hop:
            offsets.append(hop)
    return offsets


def params():
    return pltpu.CompilerParams(vmem_limit_bytes=48 * 1024 * 1024)


def shards(tokens, grad_out, router_gates, groups, w_gate, w_up, w_down):
    nodes = lax.axis_size("node")
    places = lax.axis_size("local")
    count, width = tokens.shape
    columns = nodes // 2
    node = lax.axis_index("node")
    place = lax.axis_index("local")
    wide = 2 * width + LANES

    lanes = jnp.arange(LANES, dtype=jnp.int32)
    hits = groups[:, :, None] == lanes[None, None, :]
    table = jnp.sum(
        jnp.where(hits, router_gates.astype(jnp.float32)[:, :, None], 0.0), axis=1
    ).astype(jnp.bfloat16)
    mine = jnp.concatenate([tokens, grad_out, table], axis=1)
    packed = jnp.concatenate([w_gate[0], w_up[0], w_down[0].T], axis=1)
    weights = lax.all_gather(packed, "dp", axis=0, tiled=True)

    same_core = [[2 * x + core for x in range(columns)] for core in range(2)]
    block = lax.all_gather(mine, "node", axis=0, tiled=True, axis_index_groups=same_core)
    up = [(i, (i + 1) % places) for i in range(places)]
    down = [(i, (i - 1) % places) for i in range(places)]
    cores = [(i, i ^ 1) for i in range(nodes)]
    rising = falling = block
    own = [block]
    for hop in range(1, places // 2 + 1):
        rising = lax.ppermute(rising, "local", up)
        own.append(rising)
        if hop < places - hop:
            falling = lax.ppermute(falling, "local", down)
            own.append(falling)
    other = [
        lax.ppermute(jnp.concatenate(own[a:b], axis=0), "node", cores)
        for a, b in ((0, 3), (3, 5), (5, len(own)))
    ]

    half = places * columns * count
    sel = jnp.broadcast_to((lanes == node).astype(jnp.float32)[None], (8, LANES))
    vmem = pl.BlockSpec(memory_space=pltpu.VMEM)
    anywhere = pl.BlockSpec(memory_space=pl.ANY)
    grads, back, part = pl.pallas_call(
        functools.partial(gradients_kernel, len(own), len(other)),
        out_shape=(
            jax.ShapeDtypeStruct((3 * LANES, width), jnp.bfloat16),
            jax.ShapeDtypeStruct((2 * half, 2 * LANES), jnp.bfloat16),
            jax.ShapeDtypeStruct((2 * half, LANES), jnp.bfloat16),
        ),
        in_specs=[pl.BlockSpec(memory_space=pltpu.SMEM), vmem]
        + [anywhere] * (1 + len(own) + len(other)),
        out_specs=(vmem, vmem, vmem),
        scratch_shapes=[
            pltpu.VMEM((2 * half, wide), jnp.bfloat16),
            pltpu.VMEM((width, 3 * LANES), jnp.bfloat16),
            pltpu.SemaphoreType.DMA((1 + 2 * places,)),
        ],
        compiler_params=params(),
        name="gradients",
    )(place.astype(jnp.int32)[None], sel, weights, *own, *other)

    summed = lax.psum(grads, "dp")

    part_own, part_other = pl.pallas_call(
        input_kernel,
        out_shape=(
            jax.ShapeDtypeStruct((half, width + LANES), jnp.bfloat16),
            jax.ShapeDtypeStruct((half, width + LANES), jnp.bfloat16),
        ),
        in_specs=[vmem, vmem, vmem],
        out_specs=(vmem, vmem),
        compiler_params=params(),
        name="input_part",
    )(back, part, weights)
    arrived = lax.ppermute(part_other, "node", cores)
    chip = (part_own.astype(jnp.float32) + arrived.astype(jnp.float32)).astype(jnp.bfloat16)
    by_place = lax.all_to_all(
        chip.reshape(places, columns * count, width + LANES), "local", 0, 0, tiled=True
    )
    column = jnp.sum(by_place.astype(jnp.float32), axis=0).astype(jnp.bfloat16)
    by_column = lax.all_to_all(
        column.reshape(columns, count, width + LANES),
        "node",
        0,
        0,
        tiled=True,
        axis_index_groups=same_core,
    )
    total = jnp.sum(by_column.astype(jnp.float32), axis=0)
    grad_tokens = total[:, :width].astype(jnp.bfloat16)
    grad_gates = jnp.sum(jnp.where(hits, total[:, None, width:], 0.0), axis=2).astype(jnp.bfloat16)

    grad_gate, grad_up, grad_down = pl.pallas_call(
        unpack_kernel,
        out_shape=(
            jax.ShapeDtypeStruct((1, width, LANES), jnp.bfloat16),
            jax.ShapeDtypeStruct((1, width, LANES), jnp.bfloat16),
            jax.ShapeDtypeStruct((1, LANES, width), jnp.bfloat16),
        ),
        in_specs=[vmem],
        out_specs=(vmem, vmem, vmem),
        compiler_params=params(),
        name="unpack",
    )(summed)
    return grad_tokens, grad_gates, grad_gate, grad_up, grad_down


def solution(mesh):
    placed = (
        P(("dp", "node", "local"), None),
        P(("dp", "node", "local"), None),
        P(("dp", "node", "local"), None),
        P(("dp", "node", "local"), None),
        P("node", "dp", "local"),
        P("node", "dp", "local"),
        P("node", "local", "dp"),
    )
    return jax.shard_map(
        shards,
        mesh=mesh,
        in_specs=placed,
        out_specs=(
            P(("dp", "node", "local"), None),
            P(("dp", "node", "local"), None),
            P("node", None, "local"),
            P("node", None, "local"),
            P("node", "local", None),
        ),
        check_vma=False,
    )
```

time: 399 us -> 227 us (0.57)
  blocking collectives: 100 us -> 15.4 us
  waiting for transfers between devices: 180 us -> 117 us
  local copies, waits for them, and re-layouts: 32.2 us -> 3.44 us
  matrix products: 22.7 us -> 0 us
  Pallas kernels: 0 us -> 19.5 us
  starting transfers between devices: 39.3 us -> 45.3 us
    all_to_all x4 -> x2, waiting for transfers between devices: 166 us -> 46.8 us  [the longest x1 46.8 us: shards(): lax.all_to_all(chip.reshape(places, columns * count, width + LANES), 'loc...]
    all_gather x3 -> x1, blocking collectives: 87 us -> 15.4 us  [shards(): lax.all_gather(mine, 'node', axis=0, tiled=True, axis_index_groups=same_c...]
    ppermute x0 -> x11, starting transfers between devices: none -> 36.2 us  [the longest x3 19.8 us: shards(): falling = lax.ppermute(falling, 'local', down)]
    psum x1, waiting for transfers between devices: 13.9 us -> 45.1 us  [shards(): summed = lax.psum(grads, 'dp')]
    all_to_all x4 -> x2, starting transfers between devices: 39.3 us -> 9.01 us  [the longest x1 4.63 us: shards(): lax.all_to_all(column.reshape(columns, count, width + LANES), 'node', 0,...]
    ppermute x0 -> x11, waiting for transfers between devices: none -> 24.8 us  [the longest x4 16.7 us: shards(): rising = lax.ppermute(rising, 'local', up)]
    dot_general x13 -> x0, matrix products: 22.7 us -> none  [the longest x1 4.21 us: backprop(): term_down = jnp.dot(activated.T, scaled, preferred_element_type=jnp.float32)]
    pallas_call x0 -> x3, Pallas kernels: none -> 19.5 us  [the longest x1 13.6 us: shards(): pl.pallas_call(functools.partial(gradients_kernel, len(own), len(other)),...]
  transfers between devices with their start and end apart: 5 -> 15, of which waited for: 4 -> 10; matrix products, arithmetic and copies ran while one was open for 5% -> 3% of each run, Pallas kernels for 0% -> 1%
where the time goes in v1:
time: 227 us; the launch traced here: 226 us
  waiting for transfers between devices  117 us (52%)
  starting transfers between devices  45.3 us (20%)
  Pallas kernels  19.5 us (9%)
  blocking collectives  15.4 us (7%)
  between operations  14.2 us (6%)
  other arithmetic  11.1 us (5%)
  local copies, waits for them, and re-layouts  3.44 us (2%)
    all_to_all x1, waiting for transfers between devices, shards(): lax.all_to_all(chip.reshape(places, columns * count, width + LANES), 'loc...  46.8 us
    psum x1, waiting for transfers between devices, shards(): summed = lax.psum(grads, 'dp')  45.1 us
    ppermute x3, starting transfers between devices, shards(): falling = lax.ppermute(falling, 'local', down)  19.8 us
    ppermute x4, waiting for transfers between devices, shards(): rising = lax.ppermute(rising, 'local', up)  16.7 us
    all_gather x1, blocking collectives, shards(): lax.all_gather(mine, 'node', axis=0, tiled=True, axis_index_groups=same_c...  15.4 us
    pallas_call x1, Pallas kernels, shards(): pl.pallas_call(functools.partial(gradients_kernel, len(own), len(other)),...  13.6 us
    ppermute x4, starting transfers between devices, shards(): rising = lax.ppermute(rising, 'local', up)  7.97 us
    ppermute x3, starting transfers between devices, shards(): lax.ppermute(jnp.concatenate(own[a:b], axis=0), 'node', cores)  6.21 us
  transfers between devices with their start and end apart: 15, of which 10 were waited for; matrix products, arithmetic and copies ran while one was open for 3% of the time, Pallas kernels for 1%

profile of v1, /device:TPU:2, one launch (start us, length us, event | category | flops | bytes accessed | tf_op | source)
XLA Modules:
  0.0 226.3 jit_solution(5978344909002932040)
XLA Ops:
  9.5 15.4 %all_gather.7.refs_0_ = bf16[32,7296]{1,0:T(8,128)(2,1)S(1)} all-gather(bf16[8,7296]{1,0:T(8,128)(2,1)S(1)} %pad_maximum_fusion.4), channel_id=1, replica_groups={{0,16,32,48},{8,24,40,56},{1,17,33,49},{9,25,41,57},{2,18,34,50},{10,26..., dimensions={0}, use_global_device_ids=true | all-gather | bytes 583680 | tf_op jit(solution)/shard_map/all_gather | solution.py:149
  24.9 2.2 collective-permute-start
  27.1 1.8 pad_maximum_fusion.3
  28.9 8.6 %collective-permute-start.1 = (bf16[32,7296]{1,0:T(8,128)(2,1)S(1)}, bf16[32,7296]{1,0:T(8,128)(2,1)S(1)}, u32[]{:S(2)}, u32[]{:S(2)}) collective-permute-start(bf16[32,7296]{1,0:T(8,128)(2,1)S(1)} %all_gather.7.refs_0_), channel_id=1, source_target_pairs={{0,7},{1,0},{2,1},{3,2},{4,3},{5,4},{6,5},{7,6},{8,15},{9,8},{10,9... | collective-permute-start | bytes 1400840 | tf_op jit(solution)/shard_map/ppermute | solution.py:159
  37.5 3.4 %collective-permute-done.refs_1_ = bf16[32,7296]{1,0:T(8,128)(2,1)S(1)} collective-permute-done((bf16[32,7296]{1,0:T(8,128)(2,1)S(1)}, bf16[32,7296]{1,0:T(8,128)(2,1)S(1)}, u32[]{:S(2)}, u32[]{:S(2)}) %collective-permute-start) | collective-permute-done | bytes 466976 | tf_op jit(solution)/shard_map/ppermute | solution.py:156
  41.0 1.9 collective-permute-start.2
  42.9 1.1 collective-permute-done.1.refs_2_
  44.0 5.6 %collective-permute-start.3 = (bf16[32,7296]{1,0:T(8,128)(2,1)S(1)}, bf16[32,7296]{1,0:T(8,128)(2,1)S(1)}, u32[]{:S(2)}, u32[]{:S(2)}) collective-permute-start(bf16[32,7296]{1,0:T(8,128)(2,1)S(1)} %collective-permute-done.1.refs_2_), channel_id=1, source_target_pairs={{0,7},{1,0},{2,1},{3,2},{4,3},{5,4},{6,5},{7,6},{8,15},{9,8},{10,9... | collective-permute-start | bytes 1400840 | tf_op jit(solution)/shard_map/ppermute | solution.py:159
  49.6 3.1 %collective-permute-done.2.refs_3_ = bf16[32,7296]{1,0:T(8,128)(2,1)S(1)} collective-permute-done((bf16[32,7296]{1,0:T(8,128)(2,1)S(1)}, bf16[32,7296]{1,0:T(8,128)(2,1)S(1)}, u32[]{:S(2)}, u32[]{:S(2)}) %collective-permute-start.2) | collective-permute-done | bytes 466976 | tf_op jit(solution)/shard_map/ppermute | solution.py:156
  52.6 1.9 collective-permute-start.4
  54.6 1.1 collective-permute-done.3.refs_4_
  55.6 5.6 %collective-permute-start.5 = (bf16[32,7296]{1,0:T(8,128)(2,1)S(1)}, bf16[32,7296]{1,0:T(8,128)(2,1)S(1)}, u32[]{:S(2)}, u32[]{:S(2)}) collective-permute-start(bf16[32,7296]{1,0:T(8,128)(2,1)S(1)} %collective-permute-done.3.refs_4_), channel_id=1, source_target_pairs={{0,7},{1,0},{2,1},{3,2},{4,3},{5,4},{6,5},{7,6},{8,15},{9,8},{10,9... | collective-permute-start | bytes 1400840 | tf_op jit(solution)/shard_map/ppermute | solution.py:159
  61.2 3.6 %collective-permute-done.4.refs_5_ = bf16[32,7296]{1,0:T(8,128)(2,1)S(1)} collective-permute-done((bf16[32,7296]{1,0:T(8,128)(2,1)S(1)}, bf16[32,7296]{1,0:T(8,128)(2,1)S(1)}, u32[]{:S(2)}, u32[]{:S(2)}) %collective-permute-start.4) | collective-permute-done | bytes 466976 | tf_op jit(solution)/shard_map/ppermute | solution.py:156
  64.8 1.9 collective-permute-start.6
  66.7 1.2 pad_maximum_fusion
  67.9 1.9 collective-permute-start.7
  69.9 6.6 %collective-permute-done.6.refs_7_ = bf16[32,7296]{1,0:T(8,128)(2,1)S(1)} collective-permute-done((bf16[32,7296]{1,0:T(8,128)(2,1)S(1)}, bf16[32,7296]{1,0:T(8,128)(2,1)S(1)}, u32[]{:S(2)}, u32[]{:S(2)}) %collective-permute-start.6) | collective-permute-done | bytes 466976 | tf_op jit(solution)/shard_map/ppermute | solution.py:156
  76.5 1.3 pad_maximum_fusion.1
  77.7 1.9 collective-permute-start.9
  80.7 2.4 %collective-permute-start.8 = (bf16[64,7296]{1,0:T(8,128)(2,1)}, bf16[64,7296]{1,0:T(8,128)(2,1)}, u32[]{:S(2)}, u32[]{:S(2)}) collective-permute-start(bf16[64,7296]{1,0:T(8,128)(2,1)} %pad_maximum_fusion.2), channel_id=1, source_target_pairs={{0,8},{8,0},{16,24},{24,16},{32,40},{40,32},{48,56},{56,48},{1,9},... | collective-permute-start | bytes 2801672 | tf_op jit(solution)/shard_map/ppermute | solution.py:162
  83.1 2.4 %collective-permute-done.8.refs_9_ = bf16[64,7296]{1,0:T(8,128)(2,1)} collective-permute-done((bf16[64,7296]{1,0:T(8,128)(2,1)}, bf16[64,7296]{1,0:T(8,128)(2,1)}, u32[]{:S(2)}, u32[]{:S(2)}) %collective-permute-start.8) | collective-permute-done | bytes 933920 | tf_op jit(solution)/shard_map/ppermute | solution.py:162
  86.5 13.6 %gradients.1 = (bf16[384,3584]{1,0:T(8,128)(2,1)}, bf16[512,256]{1,0:T(8,128)(2,1)S(1)}, bf16[512,128]{1,0:T(8,128)(2,1)S(1)}) custom-call(s32[1]{0:T(128)} %bitcast.z_ref, f32[8,128]{1,0:T(8,128)S(1)} %broadcast_in_dim.36.sel_ref, bf16[3584,384]{1,0:T(8,128)(2,1)} %all-gather.2.cloned.1.call-done.w_hbm.w_ref, bf16[32,7296]{1,0:T(8,128)(2,1)S(1)} %all_gather.7.refs_0_, ...), custom_call_target="tpu_custom_call" | custom-call | tf_op jit(solution)/shard_map/gradients/pallas_call | solution.py:170
  100.1 4.1 %input_part.1 = (bf16[256,3712]{1,0:T(8,128)(2,1)S(1)}, bf16[256,3712]{1,0:T(8,128)(2,1)S(1)}) custom-call(bf16[512,256]{1,0:T(8,128)(2,1)S(1)} %get-tuple-element.13.back_ref, bf16[512,128]{1,0:T(8,128)(2,1)S(1)} %get-tuple-element.14.part_ref, bf16[3584,384]{1,0:T(8,128)(2,1)} %all-gather.2.cloned.1.call-done.w_hbm.w_ref), custom_call_target="tpu_custom_call" | custom-call | tf_op jit(solution)/shard_map/input_part/pallas_call | solution.py:191
  104.2 2.3 %collective-permute-start.10 = (bf16[256,3712]{1,0:T(8,128)(2,1)S(1)}, bf16[256,3712]{1,0:T(8,128)(2,1)S(1)}, u32[]{:S(2)}, u32[]{:S(2)}) collective-permute-start(bf16[256,3712]{1,0:T(8,128)(2,1)S(1)} %get-tuple-element.16), channel_id=1, source_target_pairs={{0,8},{8,0},{16,24},{24,16},{32,40},{40,32},{48,56},{56,48},{1,9},... | collective-permute-start | bytes 5701640 | tf_op jit(solution)/shard_map/ppermute | solution.py:202
  106.5 3.5 %collective-permute-done.10 = bf16[256,3712]{1,0:T(8,128)(2,1)S(1)} collective-permute-done((bf16[256,3712]{1,0:T(8,128)(2,1)S(1)}, bf16[256,3712]{1,0:T(8,128)(2,1)S(1)}, u32[]{:S(2)}, u32[]{:S(2)}) %collective-permute-start.10) | collective-permute-done | bytes 1900576 | tf_op jit(solution)/shard_map/ppermute | solution.py:202
  110.0 1.8 add_convert_fusion
  111.8 4.4 %all-to-all-start = ((bf16[8,32,3712]{2,1,0:T(8,128)(2,1)}), bf16[8,32,3712]{2,1,0:T(8,128)(2,1)S(1)}, u32[]{:S(2)}, u32[]{:S(2)}) async-start(bf16[8,32,3712]{2,1,0:T(8,128)(2,1)} %bitcast.8), calls=%async_computation | async-start | bytes 3801088 | tf_op jit(solution)/shard_map/all_to_all | solution.py:204
  116.9 46.8 %all-to-all-done = bf16[8,32,3712]{2,1,0:T(8,128)(2,1)S(1)} async-done(((bf16[8,32,3712]{2,1,0:T(8,128)(2,1)}), bf16[8,32,3712]{2,1,0:T(8,128)(2,1)S(1)}, u32[]{:S(2)}, u32[]{:S(2)}) %all-to-all-start) | async-done | bytes 1900576 | tf_op jit(solution)/shard_map/all_to_all | solution.py:204
  164.7 4.6 %all-to-all-start.1 = ((bf16[4,8,3712]{2,1,0:T(8,128)(2,1)}), bf16[4,8,3712]{2,1,0:T(8,128)(2,1)S(1)}, u32[]{:S(2)}, u32[]{:S(2)}) async-start(bf16[4,8,3712]{2,1,0:T(8,128)(2,1)} %bitcast.6), calls=%async_computation.1 | async-start | bytes 475136 | tf_op jit(solution)/shard_map/all_to_all | solution.py:208
  169.3 45.1 %all-reduce.2.cloned.1.call-done.sum_ref = bf16[384,3584]{1,0:T(8,128)(2,1)} async-done(((bf16[384,3584]{1,0:T(8,128)(2,1)}), bf16[384,3584]{1,0:T(8,128)(2,1)}) %all-reduce.2.cloned.1.call-update) | async-done | bytes 2752528 | tf_op jit(solution)/shard_map/psum | solution.py:189
  214.4 1.8 copy-done
  216.2 1.8 unpack.1
  (27 shorter events, 7.5 us)
Async XLA Ops:
  7.2 78.4 %all-gather.2.cloned.1.call-start = ((), (), s32[]{:S(2)}) async-start(), calls=%async_computation.2 | async-start | bytes 3096576 | tf_op jit(solution)/shard_map/all_gather | solution.py:146
  24.9 16.1 %collective-permute-start = (bf16[32,7296]{1,0:T(8,128)(2,1)S(1)}, bf16[32,7296]{1,0:T(8,128)(2,1)S(1)}, u32[]{:S(2)}, u32[]{:S(2)}) collective-permute-start(bf16[32,7296]{1,0:T(8,128)(2,1)S(1)} %all_gather.7.refs_0_), channel_id=1, source_target_pairs={{0,1},{1,2},{2,3},{3,4},{4,5},{5,6},{6,7},{7,0},{8,9},{9,10},{10,1... | collective-permute-start | bytes 1400840 | tf_op jit(solution)/shard_map/ppermute | solution.py:156
  28.9 15.0 %collective-permute-start.1 = (bf16[32,7296]{1,0:T(8,128)(2,1)S(1)}, bf16[32,7296]{1,0:T(8,128)(2,1)S(1)}, u32[]{:S(2)}, u32[]{:S(2)}) collective-permute-start(bf16[32,7296]{1,0:T(8,128)(2,1)S(1)} %all_gather.7.refs_0_), channel_id=1, source_target_pairs={{0,7},{1,0},{2,1},{3,2},{4,3},{5,4},{6,5},{7,6},{8,15},{9,8},{10,9... | collective-permute-start | bytes 1400840 | tf_op jit(solution)/shard_map/ppermute | solution.py:159
  41.0 11.7 %collective-permute-start.2 = (bf16[32,7296]{1,0:T(8,128)(2,1)S(1)}, bf16[32,7296]{1,0:T(8,128)(2,1)S(1)}, u32[]{:S(2)}, u32[]{:S(2)}) collective-permute-start(bf16[32,7296]{1,0:T(8,128)(2,1)S(1)} %collective-permute-done.refs_1_), channel_id=1, source_target_pairs={{0,1},{1,2},{2,3},{3,4},{4,5},{5,6},{6,7},{7,0},{8,9},{9,10},{10,1... | collective-permute-start | bytes 1400840 | tf_op jit(solution)/shard_map/ppermute | solution.py:156
  44.0 11.7 %collective-permute-start.3 = (bf16[32,7296]{1,0:T(8,128)(2,1)S(1)}, bf16[32,7296]{1,0:T(8,128)(2,1)S(1)}, u32[]{:S(2)}, u32[]{:S(2)}) collective-permute-start(bf16[32,7296]{1,0:T(8,128)(2,1)S(1)} %collective-permute-done.1.refs_2_), channel_id=1, source_target_pairs={{0,7},{1,0},{2,1},{3,2},{4,3},{5,4},{6,5},{7,6},{8,15},{9,8},{10,9... | collective-permute-start | bytes 1400840 | tf_op jit(solution)/shard_map/ppermute | solution.py:159
  52.6 12.2 %collective-permute-start.4 = (bf16[32,7296]{1,0:T(8,128)(2,1)S(1)}, bf16[32,7296]{1,0:T(8,128)(2,1)S(1)}, u32[]{:S(2)}, u32[]{:S(2)}) collective-permute-start(bf16[32,7296]{1,0:T(8,128)(2,1)S(1)} %collective-permute-done.2.refs_3_), channel_id=1, source_target_pairs={{0,1},{1,2},{2,3},{3,4},{4,5},{5,6},{6,7},{7,0},{8,9},{9,10},{10,1... | collective-permute-start | bytes 1400840 | tf_op jit(solution)/shard_map/ppermute | solution.py:156
  55.6 14.2 %collective-permute-start.5 = (bf16[32,7296]{1,0:T(8,128)(2,1)S(1)}, bf16[32,7296]{1,0:T(8,128)(2,1)S(1)}, u32[]{:S(2)}, u32[]{:S(2)}) collective-permute-start(bf16[32,7296]{1,0:T(8,128)(2,1)S(1)} %collective-permute-done.3.refs_4_), channel_id=1, source_target_pairs={{0,7},{1,0},{2,1},{3,2},{4,3},{5,4},{6,5},{7,6},{8,15},{9,8},{10,9... | collective-permute-start | bytes 1400840 | tf_op jit(solution)/shard_map/ppermute | solution.py:159
  64.8 11.7 %collective-permute-start.6 = (bf16[32,7296]{1,0:T(8,128)(2,1)S(1)}, bf16[32,7296]{1,0:T(8,128)(2,1)S(1)}, u32[]{:S(2)}, u32[]{:S(2)}) collective-permute-start(bf16[32,7296]{1,0:T(8,128)(2,1)S(1)} %collective-permute-done.4.refs_5_), channel_id=1, source_target_pairs={{0,1},{1,2},{2,3},{3,4},{4,5},{5,6},{6,7},{7,0},{8,9},{9,10},{10,1... | collective-permute-start | bytes 1400840 | tf_op jit(solution)/shard_map/ppermute | solution.py:156
  67.9 17.6 %collective-permute-start.7 = (bf16[96,7296]{1,0:T(8,128)(2,1)}, bf16[96,7296]{1,0:T(8,128)(2,1)}, u32[]{:S(2)}, u32[]{:S(2)}) collective-permute-start(bf16[96,7296]{1,0:T(8,128)(2,1)} %pad_maximum_fusion), channel_id=1, source_target_pairs={{0,8},{8,0},{16,24},{24,16},{32,40},{40,32},{48,56},{56,48},{1,9},... | collective-permute-start | bytes 4202504 | tf_op jit(solution)/shard_map/ppermute | solution.py:162
  76.5 4.2 %copy-start.1 = (bf16[32,7296]{1,0:T(8,128)(2,1)}, bf16[32,7296]{1,0:T(8,128)(2,1)S(1)}, u32[]{:S(2)}) copy-start(bf16[32,7296]{1,0:T(8,128)(2,1)S(1)} %collective-permute-done.6.refs_7_) | copy-start | bytes 1400836
  77.7 7.8 %collective-permute-start.9 = (bf16[96,7296]{1,0:T(8,128)(2,1)}, bf16[96,7296]{1,0:T(8,128)(2,1)}, u32[]{:S(2)}, u32[]{:S(2)}) collective-permute-start(bf16[96,7296]{1,0:T(8,128)(2,1)} %pad_maximum_fusion.1), channel_id=1, source_target_pairs={{0,8},{8,0},{16,24},{24,16},{32,40},{40,32},{48,56},{56,48},{1,9},... | collective-permute-start | bytes 4202504 | tf_op jit(solution)/shard_map/ppermute | solution.py:162
  80.7 4.8 %collective-permute-start.8 = (bf16[64,7296]{1,0:T(8,128)(2,1)}, bf16[64,7296]{1,0:T(8,128)(2,1)}, u32[]{:S(2)}, u32[]{:S(2)}) collective-permute-start(bf16[64,7296]{1,0:T(8,128)(2,1)} %pad_maximum_fusion.2), channel_id=1, source_target_pairs={{0,8},{8,0},{16,24},{24,16},{32,40},{40,32},{48,56},{56,48},{1,9},... | collective-permute-start | bytes 2801672 | tf_op jit(solution)/shard_map/ppermute | solution.py:162
  85.5 1.0 copy-start.2
  104.2 5.8 %collective-permute-start.10 = (bf16[256,3712]{1,0:T(8,128)(2,1)S(1)}, bf16[256,3712]{1,0:T(8,128)(2,1)S(1)}, u32[]{:S(2)}, u32[]{:S(2)}) collective-permute-start(bf16[256,3712]{1,0:T(8,128)(2,1)S(1)} %get-tuple-element.16), channel_id=1, source_target_pairs={{0,8},{8,0},{16,24},{24,16},{32,40},{40,32},{48,56},{56,48},{1,9},... | collective-permute-start | bytes 5701640 | tf_op jit(solution)/shard_map/ppermute | solution.py:202
  111.8 51.9 %all-to-all-start = ((bf16[8,32,3712]{2,1,0:T(8,128)(2,1)}), bf16[8,32,3712]{2,1,0:T(8,128)(2,1)S(1)}, u32[]{:S(2)}, u32[]{:S(2)}) async-start(bf16[8,32,3712]{2,1,0:T(8,128)(2,1)} %bitcast.8), calls=%async_computation | async-start | bytes 3801088 | tf_op jit(solution)/shard_map/all_to_all | solution.py:204
  116.2 98.2 %all-reduce.2.cloned.1.call-start = ((), (), s32[]{:S(2)}) async-start(), calls=%async_computation.3 | async-start | bytes 5505024 | tf_op jit(solution)/shard_map/psum | solution.py:189
  164.7 54.0 %copy-start.3 = (s32[8,4]{0,1:T(4,128)S(1)}, s32[8,4]{0,1:T(4,128)}, u32[]{:S(2)}) copy-start(s32[8,4]{0,1:T(4,128)} %param.10) | copy-start | bytes 388
  164.7 53.3 %all-to-all-start.1 = ((bf16[4,8,3712]{2,1,0:T(8,128)(2,1)}), bf16[4,8,3712]{2,1,0:T(8,128)(2,1)S(1)}, u32[]{:S(2)}, u32[]{:S(2)}) async-start(bf16[4,8,3712]{2,1,0:T(8,128)(2,1)} %bitcast.6), calls=%async_computation.1 | async-start | bytes 475136 | tf_op jit(solution)/shard_map/all_to_all | solution.py:208
  214.4 1.8 copy-start
Sparse Core Ops, SparseCore 0:
  29.1 49.0 all-gather.1
  119.4 94.9 all-reduce.1

commit v2 on v1

--- a/solution.py
+++ b/solution.py
@@ -8,39 +8,34 @@
 from jax.sharding import PartitionSpec as P
 
 LANES = 128
-STEP = 512
-
-
-def gradients_kernel(n_own, n_other, z_ref, sel_ref, w_hbm, *refs):
-    own = refs[:n_own]
-    other = refs[n_own : n_own + n_other]
-    grads_ref, back_ref, part_ref, rows, weights, sems = refs[n_own + n_other :]
+STEP = 1792
+
+
+def gradients_kernel(plan, z_ref, sel_ref, w_hbm, *refs):
+    blocks = refs[: len(plan)]
+    grads_hbm, back_ref, part_ref, rows, weights, grads, sems = refs[len(plan) :]
     half = rows.shape[0] // 2
     width = (rows.shape[1] - LANES) // 2
-    block = own[0].shape[0]
-    places = half // block
-    here = z_ref[0]
-    copies = [pltpu.make_async_copy(w_hbm, weights, sems.at[0])]
-    offsets = ring_offsets(places)
-    count = 0
-    for base, group in ((0, own), (half, other)):
-        index = 0
-        for ref in group:
-            for piece in range(ref.shape[0] // block):
-                slot = lax.rem(here + (offsets[index] + places), places)
-                start = pl.multiple_of(base + slot * block, block)
-                copies.append(
-                    pltpu.make_async_copy(
-                        ref.at[pl.ds(piece * block, block)],
-                        rows.at[pl.ds(start, block)],
-                        sems.at[1 + count],
-                    )
+    here, towards = z_ref[0], z_ref[1]
+    size = blocks[0].shape[0]
+    places = half // size
+    early = [pltpu.make_async_copy(w_hbm, weights, sems.at[0])]
+    late = []
+    for source, (hop, which) in zip(blocks, plan):
+        slot = lax.rem(here + towards * hop + places, places)
+        target = rows.at[pl.ds(pl.multiple_of(which * half + slot * size, size), size)]
+        count = len(early)
+        for group, first, columns in ((early, 0, width), (late, width, width + LANES)):
+            group.append(
+                pltpu.make_async_copy(
+                    source.at[:, pl.ds(first, columns)],
+                    target.at[:, pl.ds(first, columns)],
+                    sems.at[count + (2 * places if first else 0)],
                 )
-                index += 1
-                count += 1
-    for copy in copies:
+            )
+    for copy in early + late:
         copy.start()
-    for copy in copies:
+    for copy in early:
         copy.wait()
 
     def project(step, total):
@@ -58,6 +53,8 @@
 
     steps = width // STEP
     pre = lax.fori_loop(0, steps, project, jnp.zeros((2 * half, 2 * LANES), jnp.float32))
+    for copy in late:
+        copy.wait()
     raw = lax.fori_loop(0, steps, project_back, jnp.zeros((2 * half, LANES), jnp.float32))
     pre_gate, pre_up = pre[:, :LANES], pre[:, LANES:]
     sel = sel_ref[0:1, :]
@@ -73,18 +70,25 @@
     back_t = back.T.astype(jnp.bfloat16)
     activated_t = (activated * weight).T.astype(jnp.bfloat16)
 
-    def terms(step, carry):
-        span = pl.ds(pl.multiple_of(step * STEP, STEP), STEP)
-        shifted = pl.ds(pl.multiple_of(width + step * STEP, STEP), STEP)
-        grads_ref[: 2 * LANES, span] = jnp.dot(
+    outgoing = []
+    for step in range(steps):
+        span = pl.ds(step * STEP, STEP)
+        grads[: 2 * LANES, span] = jnp.dot(
             back_t, rows[:, span], preferred_element_type=jnp.float32
         ).astype(jnp.bfloat16)
-        grads_ref[2 * LANES :, span] = jnp.dot(
-            activated_t, rows[:, shifted], preferred_element_type=jnp.float32
+        grads[2 * LANES :, span] = jnp.dot(
+            activated_t,
+            rows[:, pl.ds(width + step * STEP, STEP)],
+            preferred_element_type=jnp.float32,
         ).astype(jnp.bfloat16)
-        return carry
-
-    lax.fori_loop(0, steps, terms, 0)
+        outgoing.append(
+            pltpu.make_async_copy(
+                grads.at[:, span], grads_hbm.at[:, span], sems.at[4 * places + 1 + step]
+            )
+        )
+        outgoing[-1].start()
+    for copy in outgoing:
+        copy.wait()
 
 
 def input_kernel(back_ref, part_ref, w_ref, own_ref, other_ref):
@@ -114,15 +118,6 @@
     down_ref[0] = sum_ref[2 * LANES :, :]
 
 
-def ring_offsets(places):
-    offsets = [0]
-    for hop in range(1, places // 2 + 1):
-        offsets.append(-hop)
-        if hop < places - hop:
-            offsets.append(hop)
-    return offsets
-
-
 def params():
     return pltpu.CompilerParams(vmem_limit_bytes=48 * 1024 * 1024)
 
@@ -147,46 +142,47 @@
 
     same_core = [[2 * x + core for x in range(columns)] for core in range(2)]
     block = lax.all_gather(mine, "node", axis=0, tiled=True, axis_index_groups=same_core)
-    up = [(i, (i + 1) % places) for i in range(places)]
-    down = [(i, (i - 1) % places) for i in range(places)]
     cores = [(i, i ^ 1) for i in range(nodes)]
-    rising = falling = block
-    own = [block]
+    ring = [
+        (n * places + z, n * places + (z + 1 - 2 * (n % 2)) % places)
+        for n in range(nodes)
+        for z in range(places)
+    ]
+    swap = lambda piece: lax.ppermute(piece, "node", cores)
+    chains = [block, swap(block)]
+    blocks, plan = list(chains), [(0, 0), (0, 1)]
     for hop in range(1, places // 2 + 1):
-        rising = lax.ppermute(rising, "local", up)
-        own.append(rising)
-        if hop < places - hop:
-            falling = lax.ppermute(falling, "local", down)
-            own.append(falling)
-    other = [
-        lax.ppermute(jnp.concatenate(own[a:b], axis=0), "node", cores)
-        for a, b in ((0, 3), (3, 5), (5, len(own)))
-    ]
-
-    half = places * columns * count
+        for which in range(1 if 2 * hop == places else 2):
+            chains[which] = lax.ppermute(chains[which], ("node", "local"), ring)
+            blocks += [chains[which], swap(chains[which])]
+            plan += [(hop, which), (-hop, 1 - which)]
+
+    half = places * block.shape[0]
+    core = lax.rem(node, 2)
+    where = jnp.stack([place, 2 * core - 1]).astype(jnp.int32)
     sel = jnp.broadcast_to((lanes == node).astype(jnp.float32)[None], (8, LANES))
     vmem = pl.BlockSpec(memory_space=pltpu.VMEM)
     anywhere = pl.BlockSpec(memory_space=pl.ANY)
     grads, back, part = pl.pallas_call(
-        functools.partial(gradients_kernel, len(own), len(other)),
+        functools.partial(gradients_kernel, plan),
         out_shape=(
             jax.ShapeDtypeStruct((3 * LANES, width), jnp.bfloat16),
             jax.ShapeDtypeStruct((2 * half, 2 * LANES), jnp.bfloat16),
             jax.ShapeDtypeStruct((2 * half, LANES), jnp.bfloat16),
         ),
-        in_specs=[pl.BlockSpec(memory_space=pltpu.SMEM), vmem]
-        + [anywhere] * (1 + len(own) + len(other)),
-        out_specs=(vmem, vmem, vmem),
+        in_specs=[pl.BlockSpec(memory_space=pltpu.SMEM), vmem] + [anywhere] * (1 + len(blocks)),
+        out_specs=(anywhere, vmem, vmem),
         scratch_shapes=[
             pltpu.VMEM((2 * half, wide), jnp.bfloat16),
             pltpu.VMEM((width, 3 * LANES), jnp.bfloat16),
-            pltpu.SemaphoreType.DMA((1 + 2 * places,)),
+            pltpu.VMEM((3 * LANES, width), jnp.bfloat16),
+            pltpu.SemaphoreType.DMA((4 * places + 1 + width // STEP,)),
         ],
         compiler_params=params(),
         name="gradients",
-    )(place.astype(jnp.int32)[None], sel, weights, *own, *other)
-
-    summed = lax.psum(grads, "dp")
+    )(where, sel, weights, *blocks)
+
+    share = lax.psum_scatter(grads, "dp", scatter_dimension=0, tiled=True)
 
     part_own, part_other = pl.pallas_call(
         input_kernel,
@@ -201,10 +197,16 @@
     )(back, part, weights)
     arrived = lax.ppermute(part_other, "node", cores)
     chip = (part_own.astype(jnp.float32) + arrived.astype(jnp.float32)).astype(jnp.bfloat16)
-    by_place = lax.all_to_all(
-        chip.reshape(places, columns * count, width + LANES), "local", 0, 0, tiled=True
-    )
-    column = jnp.sum(by_place.astype(jnp.float32), axis=0).astype(jnp.bfloat16)
+    chip = chip.reshape(places, columns * count, width + LANES)
+    cut = width // 2
+    first = lax.all_to_all(chip[:, :, :cut], "local", 0, 0, tiled=True)
+    share, first, rest = lax.optimization_barrier((share, first, chip[:, :, cut:]))
+    summed = lax.all_gather(share, "dp", axis=0, tiled=True)
+    rest = lax.all_to_all(rest, "local", 0, 0, tiled=True)
+    column = jnp.concatenate(
+        [jnp.sum(part.astype(jnp.float32), axis=0).astype(jnp.bfloat16) for part in (first, rest)],
+        axis=1,
+    )
     by_column = lax.all_to_all(
         column.reshape(columns, count, width + LANES),
         "node",

time: 227 us -> 204 us (0.90)
  waiting for transfers between devices: 117 us -> 86.8 us
  blocking collectives: 15.4 us -> 25 us
  local copies, waits for them, and re-layouts: 3.44 us -> 9.56 us
  Pallas kernels: 19.5 us -> 13.9 us
  other arithmetic: 11.1 us -> 5.63 us
  starting transfers between devices: 45.3 us -> 47.7 us
    psum x1 -> x0, waiting for transfers between devices: 45.1 us -> none  [shards(): summed = lax.psum(grads, 'dp')]
    all_to_all x0 -> x1, blocking collectives: none -> 9.62 us  [shards(): lax.all_to_all(column.reshape(columns, count, width + LANES), 'node', 0,...]
    all_gather x0 -> x1, waiting for transfers between devices: none -> 5.47 us  [shards(): summed = lax.all_gather(share, 'dp', axis=0, tiled=True)]
    pallas_call x1, Pallas kernels: 13.6 us -> 8.96 us  [shards(): pl.pallas_call(functools.partial(gradients_kernel, plan), out_shape=(jax....]
    unnamed x8 -> x16, local copies, waits for them, and re-layouts: 2.8 us -> 6.88 us
    reduce_scatter x0 -> x1, waiting for transfers between devices: none -> 3.74 us  [shards(): share = lax.psum_scatter(grads, 'dp', scatter_dimension=0, tiled=True)]
    ppermute x10 -> x15, waiting for transfers between devices: 21.3 us -> 25 us  [the longest x7 22.9 us: shards(): chains[which] = lax.ppermute(chains[which], ('node', 'local'), ring)]
    concatenate x3 -> x0, other arithmetic: 3.49 us -> none  [shards(): jnp.concatenate(own[a:b], axis=0)]
  transfers between devices with their start and end apart: 15 -> 21, of which waited for: 10 -> 11; matrix products, arithmetic and copies ran while one was open for 3% -> 3% of each run, Pallas kernels for 1% -> 2%
where the time goes in v2:
time: 204 us; the launch traced here: 203 us
  waiting for transfers between devices  86.8 us (43%)
  starting transfers between devices  47.7 us (23%)
  blocking collectives  25 us (12%)
  between operations  14 us (7%)
  Pallas kernels  13.9 us (7%)
  local copies, waits for them, and re-layouts  9.56 us (5%)
  other arithmetic  5.63 us (3%)
    all_to_all x1, waiting for transfers between devices, shards(): first = lax.all_to_all(chip[:, :, :cut], 'local', 0, 0, tiled=True)  25.1 us
    all_to_all x1, waiting for transfers between devices, shards(): rest = lax.all_to_all(rest, 'local', 0, 0, tiled=True)  23.7 us
    ppermute x7, waiting for transfers between devices, shards(): chains[which] = lax.ppermute(chains[which], ('node', 'local'), ring)  22.9 us
    ppermute x8, starting transfers between devices, shards(): swap = lambda piece: lax.ppermute(piece, 'node', cores)  19.5 us
    all_gather x1, blocking collectives, shards(): lax.all_gather(mine, 'node', axis=0, tiled=True, axis_index_groups=same_c...  15.4 us
    ppermute x7, starting transfers between devices, shards(): chains[which] = lax.ppermute(chains[which], ('node', 'local'), ring)  13.7 us
    all_to_all x1, blocking collectives, shards(): lax.all_to_all(column.reshape(columns, count, width + LANES), 'node', 0,...  9.62 us
    pallas_call x1, Pallas kernels, shards(): pl.pallas_call(functools.partial(gradients_kernel, plan), out_shape=(jax....  8.96 us
  transfers between devices with their start and end apart: 21, of which 11 were waited for; matrix products, arithmetic and copies ran while one was open for 3% of the time, Pallas kernels for 2%

profile of v2, /device:TPU:2, one launch (start us, length us, event | category | flops | bytes accessed | tf_op | source)
XLA Modules:
  0.0 202.6 jit_solution(10766753359533271694)
XLA Ops:
  11.4 15.4 %all_gather.10.refs_0_ = bf16[32,7296]{1,0:T(8,128)(2,1)S(1)} all-gather(bf16[8,7296]{1,0:T(8,128)(2,1)S(1)} %pad_maximum_fusion.1), channel_id=1, replica_groups={{0,16,32,48},{8,24,40,56},{1,17,33,49},{9,25,41,57},{2,18,34,50},{10,26..., dimensions={0}, use_global_device_ids=true | all-gather | bytes 583680 | tf_op jit(solution)/shard_map/all_gather | solution.py:144
  26.7 2.2 %collective-permute-start.1 = (bf16[32,7296]{1,0:T(8,128)(2,1)S(1)}, bf16[32,7296]{1,0:T(8,128)(2,1)S(1)}, u32[]{:S(2)}, u32[]{:S(2)}) collective-permute-start(bf16[32,7296]{1,0:T(8,128)(2,1)S(1)} %all_gather.10.refs_0_), channel_id=1, source_target_pairs={{0,1},{1,2},{2,3},{3,4},{4,5},{5,6},{6,7},{7,0},{8,15},{9,8},{10,9... | collective-permute-start | bytes 1400840 | tf_op jit(solution)/shard_map/ppermute | solution.py:156
  29.0 4.6 %collective-permute-start = (bf16[32,7296]{1,0:T(8,128)(2,1)S(1)}, bf16[32,7296]{1,0:T(8,128)(2,1)S(1)}, u32[]{:S(2)}, u32[]{:S(2)}) collective-permute-start(bf16[32,7296]{1,0:T(8,128)(2,1)S(1)} %all_gather.10.refs_0_), channel_id=1, source_target_pairs={{0,8},{8,0},{16,24},{24,16},{32,40},{40,32},{48,56},{56,48},{1,9},... | collective-permute-start | bytes 1400840 | tf_op jit(solution)/shard_map/ppermute | solution.py:151
  33.6 8.6 %collective-permute-done.1.refs_2_ = bf16[32,7296]{1,0:T(8,128)(2,1)S(1)} collective-permute-done((bf16[32,7296]{1,0:T(8,128)(2,1)S(1)}, bf16[32,7296]{1,0:T(8,128)(2,1)S(1)}, u32[]{:S(2)}, u32[]{:S(2)}) %collective-permute-start.1) | collective-permute-done | bytes 466976 | tf_op jit(solution)/shard_map/ppermute | solution.py:156
  42.2 1.9 collective-permute-start.5
  44.1 1.9 collective-permute-start.3
  46.1 7.8 %collective-permute-done.5.refs_6_ = bf16[32,7296]{1,0:T(8,128)(2,1)S(1)} collective-permute-done((bf16[32,7296]{1,0:T(8,128)(2,1)S(1)}, bf16[32,7296]{1,0:T(8,128)(2,1)S(1)}, u32[]{:S(2)}, u32[]{:S(2)}) %collective-permute-start.5) | collective-permute-done | bytes 466976 | tf_op jit(solution)/shard_map/ppermute | solution.py:156
  53.9 1.9 collective-permute-start.9
  55.8 3.1 %collective-permute-done.3.refs_4_ = bf16[32,7296]{1,0:T(8,128)(2,1)S(1)} collective-permute-done((bf16[32,7296]{1,0:T(8,128)(2,1)S(1)}, bf16[32,7296]{1,0:T(8,128)(2,1)S(1)}, u32[]{:S(2)}, u32[]{:S(2)}) %collective-permute-start.3) | collective-permute-done | bytes 466976 | tf_op jit(solution)/shard_map/ppermute | solution.py:156
  58.9 1.9 collective-permute-start.7
  60.8 1.9 collective-permute-start.2
  62.7 2.4 %collective-permute-start.6 = (bf16[32,7296]{1,0:T(8,128)(2,1)S(1)}, bf16[32,7296]{1,0:T(8,128)(2,1)S(1)}, u32[]{:S(2)}, u32[]{:S(2)}) collective-permute-start(bf16[32,7296]{1,0:T(8,128)(2,1)S(1)} %collective-permute-done.5.refs_6_), channel_id=1, source_target_pairs={{0,8},{8,0},{16,24},{24,16},{32,40},{40,32},{48,56},{56,48},{1,9},... | collective-permute-start | bytes 1400840 | tf_op jit(solution)/shard_map/ppermute | solution.py:151
  65.5 1.9 collective-permute-start.13
  67.4 3.1 %collective-permute-done.7.refs_8_ = bf16[32,7296]{1,0:T(8,128)(2,1)S(1)} collective-permute-done((bf16[32,7296]{1,0:T(8,128)(2,1)S(1)}, bf16[32,7296]{1,0:T(8,128)(2,1)S(1)}, u32[]{:S(2)}, u32[]{:S(2)}) %collective-permute-start.7) | collective-permute-done | bytes 466976 | tf_op jit(solution)/shard_map/ppermute | solution.py:156
  70.5 1.9 collective-permute-start.11
  72.4 1.9 collective-permute-start.4
  75.2 2.4 %collective-permute-start.10 = (bf16[32,7296]{1,0:T(8,128)(2,1)S(1)}, bf16[32,7296]{1,0:T(8,128)(2,1)}, u32[]{:S(2)}, u32[]{:S(2)}) collective-permute-start(bf16[32,7296]{1,0:T(8,128)(2,1)S(1)} %collective-permute-done.9.refs_10_), channel_id=1, source_target_pairs={{0,8},{8,0},{16,24},{24,16},{32,40},{40,32},{48,56},{56,48},{1,9},... | collective-permute-start | bytes 1400840 | tf_op jit(solution)/shard_map/ppermute | solution.py:151
  78.3 1.9 collective-permute-start.8
  80.3 2.4 %collective-permute-start.14 = (bf16[32,7296]{1,0:T(8,128)(2,1)}, bf16[32,7296]{1,0:T(8,128)(2,1)}, u32[]{:S(2)}, u32[]{:S(2)}) collective-permute-start(bf16[32,7296]{1,0:T(8,128)(2,1)} %collective-permute-done.13.refs_14_), channel_id=1, source_target_pairs={{0,8},{8,0},{16,24},{24,16},{32,40},{40,32},{48,56},{56,48},{1,9},... | collective-permute-start | bytes 1400840 | tf_op jit(solution)/shard_map/ppermute | solution.py:151
  82.7 1.9 collective-permute-start.12
  84.7 2.0 collective-permute-done.12.refs_13_
  88.8 9.0 %gradients.1 = (bf16[384,3584]{1,0:T(8,128)(2,1)}, bf16[512,256]{1,0:T(8,128)(2,1)S(1)}, bf16[512,128]{1,0:T(8,128)(2,1)S(1)}) custom-call(s32[2]{0:T(128)S(1)} %pad_add_fusion.z_ref, f32[8,128]{1,0:T(8,128)S(1)} %broadcast_in_dim.32.sel_ref, bf16[3584,384]{1,0:T(8,128)(2,1)} %all-gather.3.cloned.1.call-done.w_hbm.w_ref, ...), custom_call_target="tpu_custom_call" | custom-call | tf_op jit(solution)/shard_map/gradients/pallas_call | solution.py:166
  99.3 3.2 %input_part.1 = (bf16[256,3712]{1,0:T(8,128)(2,1)S(1)}, bf16[256,3712]{1,0:T(8,128)(2,1)S(1)}) custom-call(bf16[512,256]{1,0:T(8,128)(2,1)S(1)} %get-tuple-element.17.back_ref, bf16[512,128]{1,0:T(8,128)(2,1)S(1)} %copy-done.6, bf16[3584,384]{1,0:T(8,128)(2,1)} %all-gather.3.cloned.1.call-done.w_hbm.w_ref), custom_call_target="tpu_custom_call" | custom-call | tf_op jit(solution)/shard_map/input_part/pallas_call | solution.py:187
  102.5 2.0 %collective-permute-start.15 = (bf16[256,3712]{1,0:T(8,128)(2,1)S(1)}, bf16[256,3712]{1,0:T(8,128)(2,1)S(1)}, u32[]{:S(2)}, u32[]{:S(2)}) collective-permute-start(bf16[256,3712]{1,0:T(8,128)(2,1)S(1)} %get-tuple-element.20), channel_id=1, source_target_pairs={{0,8},{8,0},{16,24},{24,16},{32,40},{40,32},{48,56},{56,48},{1,9},... | collective-permute-start | bytes 5701640 | tf_op jit(solution)/shard_map/ppermute | solution.py:198
  104.5 3.7 %collective-permute-done.15 = bf16[256,3712]{1,0:T(8,128)(2,1)S(1)} collective-permute-done((bf16[256,3712]{1,0:T(8,128)(2,1)S(1)}, bf16[256,3712]{1,0:T(8,128)(2,1)S(1)}, u32[]{:S(2)}, u32[]{:S(2)}) %collective-permute-start.15) | collective-permute-done | bytes 1900576 | tf_op jit(solution)/shard_map/ppermute | solution.py:198
  109.7 5.0 %all-to-all-start = ((bf16[8,32,1792]{2,1,0:T(8,128)(2,1)}), bf16[8,32,1792]{2,1,0:T(8,128)(2,1)S(1)}, u32[]{:S(2)}, u32[]{:S(2)}) async-start(bf16[8,32,1792]{2,1,0:T(8,128)(2,1)} %slice.17), calls=%async_computation.1 | async-start | bytes 1835008 | tf_op jit(solution)/shard_map/all_to_all | solution.py:202
  115.8 25.1 %all-to-all-done = bf16[8,32,1792]{2,1,0:T(8,128)(2,1)S(1)} async-done(((bf16[8,32,1792]{2,1,0:T(8,128)(2,1)}), bf16[8,32,1792]{2,1,0:T(8,128)(2,1)S(1)}, u32[]{:S(2)}, u32[]{:S(2)}) %all-to-all-start) | async-done | bytes 917536 | tf_op jit(solution)/shard_map/all_to_all | solution.py:202
  141.0 3.7 %reduce-scatter.2.cloned.1.call-done = bf16[48,3584]{1,0:T(8,128)(2,1)} async-done(((bf16[384,3584]{1,0:T(8,128)(2,1)}), bf16[48,3584]{1,0:T(8,128)(2,1)}) %reduce-scatter.2.cloned.1.call-update) | async-done | bytes 344080 | tf_op jit(solution)/shard_map/reduce_scatter | solution.py:185
  144.7 7.3 %all-to-all-start.1 = ((bf16[8,32,1920]{2,1,0:T(8,128)(2,1)}), bf16[8,32,1920]{2,1,0:T(8,128)(2,1)S(1)}, u32[]{:S(2)}, u32[]{:S(2)}) async-start(bf16[8,32,1920]{2,1,0:T(8,128)(2,1)} %slice.18), calls=%async_computation.2 | async-start | bytes 1966080 | tf_op jit(solution)/shard_map/all_to_all | solution.py:205
  152.1 23.7 %all-to-all-done.1 = bf16[8,32,1920]{2,1,0:T(8,128)(2,1)S(1)} async-done(((bf16[8,32,1920]{2,1,0:T(8,128)(2,1)}), bf16[8,32,1920]{2,1,0:T(8,128)(2,1)S(1)}, u32[]{:S(2)}, u32[]{:S(2)}) %all-to-all-start.1) | async-done | bytes 983072 | tf_op jit(solution)/shard_map/all_to_all | solution.py:205
  176.0 9.6 %all_to_all.15 = bf16[4,8,3712]{2,1,0:T(8,128)(2,1)S(1)} all-to-all(bf16[4,8,3712]{2,1,0:T(8,128)(2,1)S(1)} %maximum_bitcast_fusion), channel_id=1, replica_groups={{0,16,32,48},{8,24,40,56},{1,17,33,49},{9,25,41,57},{2,18,34,50},{10,26..., dimensions={0} | all-to-all | bytes 475136 | tf_op jit(solution)/shard_map/all_to_all | solution.py:210
  187.0 5.5 %all-gather.5.cloned.1.call-done.sum_ref = bf16[384,3584]{1,0:T(8,128)(2,1)} async-done(((bf16[48,3584]{1,0:T(8,128)(2,1)}), bf16[384,3584]{1,0:T(8,128)(2,1)}) %all-gather.5.cloned.1.call-update) | async-done | bytes 2752528 | tf_op jit(solution)/shard_map/all_gather | solution.py:204
  (51 shorter events, 17.6 us)
Async XLA Ops:
  7.2 79.6 %all-gather.3.cloned.1.call-start = ((), (), s32[]{:S(2)}) async-start(), calls=%async_computation.4 | async-start | bytes 3096576 | tf_op jit(solution)/shard_map/all_gather | solution.py:141
  9.0 135.7 %reduce-scatter.2.cloned.1.call-start = ((), (), s32[]{:S(2)}) async-start(), calls=%async_computation.5 | async-start | bytes 3096576 | tf_op jit(solution)/shard_map/reduce_scatter | solution.py:185
  26.7 15.4 %collective-permute-start.1 = (bf16[32,7296]{1,0:T(8,128)(2,1)S(1)}, bf16[32,7296]{1,0:T(8,128)(2,1)S(1)}, u32[]{:S(2)}, u32[]{:S(2)}) collective-permute-start(bf16[32,7296]{1,0:T(8,128)(2,1)S(1)} %all_gather.10.refs_0_), channel_id=1, source_target_pairs={{0,1},{1,2},{2,3},{3,4},{4,5},{5,6},{6,7},{7,0},{8,15},{9,8},{10,9... | collective-permute-start | bytes 1400840 | tf_op jit(solution)/shard_map/ppermute | solution.py:156
  29.0 15.1 %collective-permute-start = (bf16[32,7296]{1,0:T(8,128)(2,1)S(1)}, bf16[32,7296]{1,0:T(8,128)(2,1)S(1)}, u32[]{:S(2)}, u32[]{:S(2)}) collective-permute-start(bf16[32,7296]{1,0:T(8,128)(2,1)S(1)} %all_gather.10.refs_0_), channel_id=1, source_target_pairs={{0,8},{8,0},{16,24},{24,16},{32,40},{40,32},{48,56},{56,48},{1,9},... | collective-permute-start | bytes 1400840 | tf_op jit(solution)/shard_map/ppermute | solution.py:151
  42.2 11.7 %collective-permute-start.5 = (bf16[32,7296]{1,0:T(8,128)(2,1)S(1)}, bf16[32,7296]{1,0:T(8,128)(2,1)S(1)}, u32[]{:S(2)}, u32[]{:S(2)}) collective-permute-start(bf16[32,7296]{1,0:T(8,128)(2,1)S(1)} %collective-permute-done.1.refs_2_), channel_id=1, source_target_pairs={{0,1},{1,2},{2,3},{3,4},{4,5},{5,6},{6,7},{7,0},{8,15},{9,8},{10,9... | collective-permute-start | bytes 1400840 | tf_op jit(solution)/shard_map/ppermute | solution.py:156
  44.1 14.7 %collective-permute-start.3 = (bf16[32,7296]{1,0:T(8,128)(2,1)S(1)}, bf16[32,7296]{1,0:T(8,128)(2,1)S(1)}, u32[]{:S(2)}, u32[]{:S(2)}) collective-permute-start(bf16[32,7296]{1,0:T(8,128)(2,1)S(1)} %collective-permute-done.refs_1_), channel_id=1, source_target_pairs={{0,1},{1,2},{2,3},{3,4},{4,5},{5,6},{6,7},{7,0},{8,15},{9,8},{10,9... | collective-permute-start | bytes 1400840 | tf_op jit(solution)/shard_map/ppermute | solution.py:156
  53.9 11.7 %collective-permute-start.9 = (bf16[32,7296]{1,0:T(8,128)(2,1)S(1)}, bf16[32,7296]{1,0:T(8,128)(2,1)S(1)}, u32[]{:S(2)}, u32[]{:S(2)}) collective-permute-start(bf16[32,7296]{1,0:T(8,128)(2,1)S(1)} %collective-permute-done.5.refs_6_), channel_id=1, source_target_pairs={{0,1},{1,2},{2,3},{3,4},{4,5},{5,6},{6,7},{7,0},{8,15},{9,8},{10,9... | collective-permute-start | bytes 1400840 | tf_op jit(solution)/shard_map/ppermute | solution.py:156
  58.9 11.7 %collective-permute-start.7 = (bf16[32,7296]{1,0:T(8,128)(2,1)S(1)}, bf16[32,7296]{1,0:T(8,128)(2,1)S(1)}, u32[]{:S(2)}, u32[]{:S(2)}) collective-permute-start(bf16[32,7296]{1,0:T(8,128)(2,1)S(1)} %collective-permute-done.3.refs_4_), channel_id=1, source_target_pairs={{0,1},{1,2},{2,3},{3,4},{4,5},{5,6},{6,7},{7,0},{8,15},{9,8},{10,9... | collective-permute-start | bytes 1400840 | tf_op jit(solution)/shard_map/ppermute | solution.py:156
  60.8 13.6 %collective-permute-start.2 = (bf16[32,7296]{1,0:T(8,128)(2,1)S(1)}, bf16[32,7296]{1,0:T(8,128)(2,1)S(1)}, u32[]{:S(2)}, u32[]{:S(2)}) collective-permute-start(bf16[32,7296]{1,0:T(8,128)(2,1)S(1)} %collective-permute-done.1.refs_2_), channel_id=1, source_target_pairs={{0,8},{8,0},{16,24},{24,16},{32,40},{40,32},{48,56},{56,48},{1,9},... | collective-permute-start | bytes 1400840 | tf_op jit(solution)/shard_map/ppermute | solution.py:151
  62.7 14.9 %collective-permute-start.6 = (bf16[32,7296]{1,0:T(8,128)(2,1)S(1)}, bf16[32,7296]{1,0:T(8,128)(2,1)S(1)}, u32[]{:S(2)}, u32[]{:S(2)}) collective-permute-start(bf16[32,7296]{1,0:T(8,128)(2,1)S(1)} %collective-permute-done.5.refs_6_), channel_id=1, source_target_pairs={{0,8},{8,0},{16,24},{24,16},{32,40},{40,32},{48,56},{56,48},{1,9},... | collective-permute-start | bytes 1400840 | tf_op jit(solution)/shard_map/ppermute | solution.py:151
  65.5 14.7 %collective-permute-start.13 = (bf16[32,7296]{1,0:T(8,128)(2,1)S(1)}, bf16[32,7296]{1,0:T(8,128)(2,1)}, u32[]{:S(2)}, u32[]{:S(2)}) collective-permute-start(bf16[32,7296]{1,0:T(8,128)(2,1)S(1)} %collective-permute-done.9.refs_10_), channel_id=1, source_target_pairs={{0,1},{1,2},{2,3},{3,4},{4,5},{5,6},{6,7},{7,0},{8,15},{9,8},{10,9... | collective-permute-start | bytes 1400840 | tf_op jit(solution)/shard_map/ppermute | solution.py:156
  70.5 12.2 %collective-permute-start.11 = (bf16[32,7296]{1,0:T(8,128)(2,1)S(1)}, bf16[32,7296]{1,0:T(8,128)(2,1)}, u32[]{:S(2)}, u32[]{:S(2)}) collective-permute-start(bf16[32,7296]{1,0:T(8,128)(2,1)S(1)} %collective-permute-done.7.refs_8_), channel_id=1, source_target_pairs={{0,1},{1,2},{2,3},{3,4},{4,5},{5,6},{6,7},{7,0},{8,15},{9,8},{10,9... | collective-permute-start | bytes 1400840 | tf_op jit(solution)/shard_map/ppermute | solution.py:156
  72.4 12.3 %collective-permute-start.4 = (bf16[32,7296]{1,0:T(8,128)(2,1)S(1)}, bf16[32,7296]{1,0:T(8,128)(2,1)}, u32[]{:S(2)}, u32[]{:S(2)}) collective-permute-start(bf16[32,7296]{1,0:T(8,128)(2,1)S(1)} %collective-permute-done.3.refs_4_), channel_id=1, source_target_pairs={{0,8},{8,0},{16,24},{24,16},{32,40},{40,32},{48,56},{56,48},{1,9},... | collective-permute-start | bytes 1400840 | tf_op jit(solution)/shard_map/ppermute | solution.py:151
  74.4 0.8 copy-start.1
  75.2 9.6 %collective-permute-start.10 = (bf16[32,7296]{1,0:T(8,128)(2,1)S(1)}, bf16[32,7296]{1,0:T(8,128)(2,1)}, u32[]{:S(2)}, u32[]{:S(2)}) collective-permute-start(bf16[32,7296]{1,0:T(8,128)(2,1)S(1)} %collective-permute-done.9.refs_10_), channel_id=1, source_target_pairs={{0,8},{8,0},{16,24},{24,16},{32,40},{40,32},{48,56},{56,48},{1,9},... | collective-permute-start | bytes 1400840 | tf_op jit(solution)/shard_map/ppermute | solution.py:151
  77.6 0.8 copy-start.3
  78.3 6.4 %collective-permute-start.8 = (bf16[32,7296]{1,0:T(8,128)(2,1)S(1)}, bf16[32,7296]{1,0:T(8,128)(2,1)}, u32[]{:S(2)}, u32[]{:S(2)}) collective-permute-start(bf16[32,7296]{1,0:T(8,128)(2,1)S(1)} %collective-permute-done.7.refs_8_), channel_id=1, source_target_pairs={{0,8},{8,0},{16,24},{24,16},{32,40},{40,32},{48,56},{56,48},{1,9},... | collective-permute-start | bytes 1400840 | tf_op jit(solution)/shard_map/ppermute | solution.py:151
  80.3 4.5 %collective-permute-start.14 = (bf16[32,7296]{1,0:T(8,128)(2,1)}, bf16[32,7296]{1,0:T(8,128)(2,1)}, u32[]{:S(2)}, u32[]{:S(2)}) collective-permute-start(bf16[32,7296]{1,0:T(8,128)(2,1)} %collective-permute-done.13.refs_14_), channel_id=1, source_target_pairs={{0,8},{8,0},{16,24},{24,16},{32,40},{40,32},{48,56},{56,48},{1,9},... | collective-permute-start | bytes 1400840 | tf_op jit(solution)/shard_map/ppermute | solution.py:151
  82.7 4.1 %collective-permute-start.12 = (bf16[32,7296]{1,0:T(8,128)(2,1)}, bf16[32,7296]{1,0:T(8,128)(2,1)}, u32[]{:S(2)}, u32[]{:S(2)}) collective-permute-start(bf16[32,7296]{1,0:T(8,128)(2,1)} %collective-permute-done.11.refs_12_), channel_id=1, source_target_pairs={{0,8},{8,0},{16,24},{24,16},{32,40},{40,32},{48,56},{56,48},{1,9},... | collective-permute-start | bytes 1400840 | tf_op jit(solution)/shard_map/ppermute | solution.py:151
  86.8 1.0 copy-start.2
  87.8 1.0 copy-start.4
  97.8 0.7 copy-start.5
  98.4 0.9 copy-start.6
  102.5 5.8 %collective-permute-start.15 = (bf16[256,3712]{1,0:T(8,128)(2,1)S(1)}, bf16[256,3712]{1,0:T(8,128)(2,1)S(1)}, u32[]{:S(2)}, u32[]{:S(2)}) collective-permute-start(bf16[256,3712]{1,0:T(8,128)(2,1)S(1)} %get-tuple-element.20), channel_id=1, source_target_pairs={{0,8},{8,0},{16,24},{24,16},{32,40},{40,32},{48,56},{56,48},{1,9},... | collective-permute-start | bytes 5701640 | tf_op jit(solution)/shard_map/ppermute | solution.py:198
  109.7 31.2 %all-to-all-start = ((bf16[8,32,1792]{2,1,0:T(8,128)(2,1)}), bf16[8,32,1792]{2,1,0:T(8,128)(2,1)S(1)}, u32[]{:S(2)}, u32[]{:S(2)}) async-start(bf16[8,32,1792]{2,1,0:T(8,128)(2,1)} %slice.17), calls=%async_computation.1 | async-start | bytes 1835008 | tf_op jit(solution)/shard_map/all_to_all | solution.py:202
  114.7 77.7 %all-gather.5.cloned.1.call-start = ((), (), s32[]{:S(2)}) async-start(), calls=%async_computation.6 | async-start | bytes 3096576 | tf_op jit(solution)/shard_map/all_gather | solution.py:204
  144.7 31.1 %all-to-all-start.1 = ((bf16[8,32,1920]{2,1,0:T(8,128)(2,1)}), bf16[8,32,1920]{2,1,0:T(8,128)(2,1)S(1)}, u32[]{:S(2)}, u32[]{:S(2)}) async-start(bf16[8,32,1920]{2,1,0:T(8,128)(2,1)} %slice.18), calls=%async_computation.2 | async-start | bytes 1966080 | tf_op jit(solution)/shard_map/all_to_all | solution.py:205
  152.0 34.3 %copy-start.7 = (s32[8,4]{0,1:T(4,128)S(1)}, s32[8,4]{0,1:T(4,128)}, u32[]{:S(2)}) copy-start(s32[8,4]{0,1:T(4,128)} %param.10) | copy-start | bytes 388
  192.5 1.8 copy-start
Sparse Core Ops, SparseCore 0:
  10.7 50.2 all-gather.2
  98.6 46.0 reduce-scatter.1
  147.0 45.4 all-gather.4

commit v3 on v2

--- a/solution.py
+++ b/solution.py
@@ -112,14 +112,29 @@
     other_ref[:, width:] = part_ref[half:]
 
 
-def unpack_kernel(sum_ref, gate_ref, up_ref, down_ref):
-    gate_ref[0] = sum_ref[:LANES, :].astype(jnp.float32).T.astype(jnp.bfloat16)
-    up_ref[0] = sum_ref[LANES : 2 * LANES, :].astype(jnp.float32).T.astype(jnp.bfloat16)
-    down_ref[0] = sum_ref[2 * LANES :, :]
+def unpack_kernel(sum_hbm, gate_hbm, up_hbm, down_hbm, held, turned, sems):
+    pieces = [pl.ds(n * LANES, LANES) for n in range(3)]
+    arrivals = [
+        pltpu.make_async_copy(sum_hbm.at[piece], held.at[piece], sems.at[n])
+        for n, piece in enumerate(pieces)
+    ]
+    for copy in arrivals:
+        copy.start()
+    leaving = []
+    for n, target in enumerate((gate_hbm, up_hbm)):
+        arrivals[n].wait()
+        turned[n] = held[pieces[n], :].astype(jnp.float32).T.astype(jnp.bfloat16)
+        leaving.append(pltpu.make_async_copy(turned.at[n], target.at[0], sems.at[3 + n]))
+        leaving[-1].start()
+    arrivals[2].wait()
+    leaving.append(pltpu.make_async_copy(held.at[pieces[2]], down_hbm.at[0], sems.at[5]))
+    leaving[-1].start()
+    for copy in leaving:
+        copy.wait()
 
 
 def params():
-    return pltpu.CompilerParams(vmem_limit_bytes=48 * 1024 * 1024)
+    return pltpu.CompilerParams(vmem_limit_bytes=60 * 1024 * 1024)
 
 
 def shards(tokens, grad_out, router_gates, groups, w_gate, w_up, w_down):
@@ -137,11 +152,18 @@
         jnp.where(hits, router_gates.astype(jnp.float32)[:, :, None], 0.0), axis=1
     ).astype(jnp.bfloat16)
     mine = jnp.concatenate([tokens, grad_out, table], axis=1)
-    packed = jnp.concatenate([w_gate[0], w_up[0], w_down[0].T], axis=1)
+    same_core = [[2 * x + core for x in range(columns)] for core in range(2)]
+    block = lax.all_to_all(
+        jnp.broadcast_to(mine, (columns, count, wide)),
+        "node",
+        0,
+        0,
+        tiled=True,
+        axis_index_groups=same_core,
+    ).reshape(columns * count, wide)
+    block, gate, up, down = lax.optimization_barrier((block, w_gate[0], w_up[0], w_down[0]))
+    packed = jnp.concatenate([gate, up, down.T], axis=1)
     weights = lax.all_gather(packed, "dp", axis=0, tiled=True)
-
-    same_core = [[2 * x + core for x in range(columns)] for core in range(2)]
-    block = lax.all_gather(mine, "node", axis=0, tiled=True, axis_index_groups=same_core)
     cores = [(i, i ^ 1) for i in range(nodes)]
     ring = [
         (n * places + z, n * places + (z + 1 - 2 * (n % 2)) % places)
@@ -149,7 +171,7 @@
         for z in range(places)
     ]
     swap = lambda piece: lax.ppermute(piece, "node", cores)
-    chains = [block, swap(block)]
+    chains = list(lax.optimization_barrier((block, swap(block))))
     blocks, plan = list(chains), [(0, 0), (0, 1)]
     for hop in range(1, places // 2 + 1):
         for which in range(1 if 2 * hop == places else 2):
@@ -226,8 +248,13 @@
             jax.ShapeDtypeStruct((1, width, LANES), jnp.bfloat16),
             jax.ShapeDtypeStruct((1, LANES, width), jnp.bfloat16),
         ),
-        in_specs=[vmem],
-        out_specs=(vmem, vmem, vmem),
+        in_specs=[anywhere],
+        out_specs=(anywhere, anywhere, anywhere),
+        scratch_shapes=[
+            pltpu.VMEM((3 * LANES, width), jnp.bfloat16),
+            pltpu.VMEM((2, width, LANES), jnp.bfloat16),
+            pltpu.SemaphoreType.DMA((6,)),
+        ],
         compiler_params=params(),
         name="unpack",
     )(summed)

time: 204 us -> 198 us (0.971)
  local copies, waits for them, and re-layouts: 9.56 us -> 3.35 us
  Pallas kernels: 13.9 us -> 18.5 us
  waiting for transfers between devices: 86.8 us -> 82.8 us
  other arithmetic: 5.63 us -> 8.09 us
    all_gather x1 -> x0, blocking collectives: 15.4 us -> none  [shards(): lax.all_gather(mine, 'node', axis=0, tiled=True, axis_index_groups=same_c...]
    all_to_all x0 -> x1, blocking collectives: none -> 14.6 us  [shards(): lax.all_to_all(jnp.broadcast_to(mine, (columns, count, wide)), 'node', 0,...]
    unnamed x16 -> x20, local copies, waits for them, and re-layouts: 6.88 us -> 0.04 us
    reduce_scatter x1, waiting for transfers between devices: 3.74 us -> 0.01 us  [shards(): share = lax.psum_scatter(grads, 'dp', scatter_dimension=0, tiled=True)]
    pallas_call x1, Pallas kernels: 3.15 us -> 5.21 us  [shards(): pl.pallas_call(input_kernel, out_shape=(jax.ShapeDtypeStruct((half, width...]
  transfers between devices with their start and end apart: 21 -> 21, of which waited for: 11 -> 11; matrix products, arithmetic and copies ran while one was open for 3% -> 3% of each run, Pallas kernels for 2% -> 3%
where the time goes in v3:
time: 198 us; the launch traced here: 197 us
  waiting for transfers between devices  82.8 us (42%)
  starting transfers between devices  46.4 us (23%)
  blocking collectives  24.1 us (12%)
  Pallas kernels  18.5 us (9%)
  between operations  14.1 us (7%)
  other arithmetic  8.09 us (4%)
  local copies, waits for them, and re-layouts  3.35 us (2%)
    all_to_all x1, waiting for transfers between devices, shards(): first = lax.all_to_all(chip[:, :, :cut], 'local', 0, 0, tiled=True)  25.1 us
    all_to_all x1, waiting for transfers between devices, shards(): rest = lax.all_to_all(rest, 'local', 0, 0, tiled=True)  24 us
    ppermute x7, waiting for transfers between devices, shards(): chains[which] = lax.ppermute(chains[which], ('node', 'local'), ring)  20.9 us
    ppermute x8, starting transfers between devices, shards(): swap = lambda piece: lax.ppermute(piece, 'node', cores)  17.5 us
    ppermute x7, starting transfers between devices, shards(): chains[which] = lax.ppermute(chains[which], ('node', 'local'), ring)  15.5 us
    all_to_all x1, blocking collectives, shards(): lax.all_to_all(jnp.broadcast_to(mine, (columns, count, wide)), 'node', 0,...  14.6 us
    pallas_call x1, Pallas kernels, shards(): pl.pallas_call(functools.partial(gradients_kernel, plan), out_shape=(jax....  10.2 us
    all_to_all x1, blocking collectives, shards(): lax.all_to_all(column.reshape(columns, count, width + LANES), 'node', 0,...  9.52 us
  transfers between devices with their start and end apart: 21, of which 11 were waited for; matrix products, arithmetic and copies ran while one was open for 3% of the time, Pallas kernels for 3%

profile of v3, /device:TPU:2, one launch (start us, length us, event | category | flops | bytes accessed | tf_op | source)
XLA Modules:
  0.0 197.3 jit_solution(10718486608799454943)
XLA Ops:
  9.6 14.6 %all_to_all.20 = bf16[4,8,7296]{2,1,0:T(8,128)(2,1)S(1)} all-to-all(bf16[4,8,7296]{2,1,0:T(8,128)(2,1)S(1)} %broadcast_in_dim.38), channel_id=1, replica_groups={{0,16,32,48},{8,24,40,56},{1,17,33,49},{9,25,41,57},{2,18,34,50},{10,26..., dimensions={0} | all-to-all | bytes 933888 | tf_op jit(solution)/shard_map/all_to_all | solution.py:156
  24.2 2.0 pad_maximum_fusion
  26.2 1.9 collective-permute-start
  29.9 1.9 collective-permute-start.1
  31.8 4.1 %collective-permute-start.3 = (bf16[32,7296]{1,0:T(8,128)(2,1)S(1)}, bf16[32,7296]{1,0:T(8,128)(2,1)S(1)}, u32[]{:S(2)}, u32[]{:S(2)}) collective-permute-start(bf16[32,7296]{1,0:T(8,128)(2,1)S(1)} %collective-permute-done.refs_1_), channel_id=1, source_target_pairs={{0,1},{1,2},{2,3},{3,4},{4,5},{5,6},{6,7},{7,0},{8,15},{9,8},{10,9... | collective-permute-start | bytes 1400840 | tf_op jit(solution)/shard_map/ppermute | solution.py:178
  35.9 8.9 %collective-permute-done.1.refs_2_ = bf16[32,7296]{1,0:T(8,128)(2,1)S(1)} collective-permute-done((bf16[32,7296]{1,0:T(8,128)(2,1)S(1)}, bf16[32,7296]{1,0:T(8,128)(2,1)S(1)}, u32[]{:S(2)}, u32[]{:S(2)}) %collective-permute-start.1) | collective-permute-done | bytes 466976 | tf_op jit(solution)/shard_map/ppermute | solution.py:178
  44.8 1.9 collective-permute-start.5
  46.7 3.1 %collective-permute-done.3.refs_4_ = bf16[32,7296]{1,0:T(8,128)(2,1)S(1)} collective-permute-done((bf16[32,7296]{1,0:T(8,128)(2,1)S(1)}, bf16[32,7296]{1,0:T(8,128)(2,1)S(1)}, u32[]{:S(2)}, u32[]{:S(2)}) %collective-permute-start.3) | collective-permute-done | bytes 466976 | tf_op jit(solution)/shard_map/ppermute | solution.py:178
  51.7 4.7 %collective-permute-done.5.refs_6_ = bf16[32,7296]{1,0:T(8,128)(2,1)S(1)} collective-permute-done((bf16[32,7296]{1,0:T(8,128)(2,1)S(1)}, bf16[32,7296]{1,0:T(8,128)(2,1)S(1)}, u32[]{:S(2)}, u32[]{:S(2)}) %collective-permute-start.5) | collective-permute-done | bytes 466976 | tf_op jit(solution)/shard_map/ppermute | solution.py:178
  56.5 1.9 collective-permute-start.9
  58.4 3.1 %collective-permute-start.2 = (bf16[32,7296]{1,0:T(8,128)(2,1)S(1)}, bf16[32,7296]{1,0:T(8,128)(2,1)S(1)}, u32[]{:S(2)}, u32[]{:S(2)}) collective-permute-start(bf16[32,7296]{1,0:T(8,128)(2,1)S(1)} %collective-permute-done.1.refs_2_), channel_id=1, source_target_pairs={{0,8},{8,0},{16,24},{24,16},{32,40},{40,32},{48,56},{56,48},{1,9},... | collective-permute-start | bytes 1400840 | tf_op jit(solution)/shard_map/ppermute | solution.py:173
  61.5 1.9 collective-permute-start.4
  63.4 1.9 collective-permute-start.11
  65.4 2.8 %collective-permute-done.9.refs_10_ = bf16[32,7296]{1,0:T(8,128)(2,1)S(1)} collective-permute-done((bf16[32,7296]{1,0:T(8,128)(2,1)S(1)}, bf16[32,7296]{1,0:T(8,128)(2,1)S(1)}, u32[]{:S(2)}, u32[]{:S(2)}) %collective-permute-start.9) | collective-permute-done | bytes 466976 | tf_op jit(solution)/shard_map/ppermute | solution.py:178
  68.1 1.9 collective-permute-start.13
  70.1 2.3 %collective-permute-start.6 = (bf16[32,7296]{1,0:T(8,128)(2,1)S(1)}, bf16[32,7296]{1,0:T(8,128)(2,1)}, u32[]{:S(2)}, u32[]{:S(2)}) collective-permute-start(bf16[32,7296]{1,0:T(8,128)(2,1)S(1)} %collective-permute-done.5.refs_6_), channel_id=1, source_target_pairs={{0,8},{8,0},{16,24},{24,16},{32,40},{40,32},{48,56},{56,48},{1,9},... | collective-permute-start | bytes 1400840 | tf_op jit(solution)/shard_map/ppermute | solution.py:173
  72.4 2.0 %collective-permute-start.8 = (bf16[32,7296]{1,0:T(8,128)(2,1)S(1)}, bf16[32,7296]{1,0:T(8,128)(2,1)}, u32[]{:S(2)}, u32[]{:S(2)}) collective-permute-start(bf16[32,7296]{1,0:T(8,128)(2,1)S(1)} %collective-permute-done.7.refs_8_), channel_id=1, source_target_pairs={{0,8},{8,0},{16,24},{24,16},{32,40},{40,32},{48,56},{56,48},{1,9},... | collective-permute-start | bytes 1400840 | tf_op jit(solution)/shard_map/ppermute | solution.py:173
  74.5 2.3 %collective-permute-start.10 = (bf16[32,7296]{1,0:T(8,128)(2,1)S(1)}, bf16[32,7296]{1,0:T(8,128)(2,1)}, u32[]{:S(2)}, u32[]{:S(2)}) collective-permute-start(bf16[32,7296]{1,0:T(8,128)(2,1)S(1)} %collective-permute-done.9.refs_10_), channel_id=1, source_target_pairs={{0,8},{8,0},{16,24},{24,16},{32,40},{40,32},{48,56},{56,48},{1,9},... | collective-permute-start | bytes 1400840 | tf_op jit(solution)/shard_map/ppermute | solution.py:173
  76.8 2.0 %collective-permute-start.12 = (bf16[32,7296]{1,0:T(8,128)(2,1)}, bf16[32,7296]{1,0:T(8,128)(2,1)}, u32[]{:S(2)}, u32[]{:S(2)}) collective-permute-start(bf16[32,7296]{1,0:T(8,128)(2,1)} %collective-permute-done.11.refs_12_), channel_id=1, source_target_pairs={{0,8},{8,0},{16,24},{24,16},{32,40},{40,32},{48,56},{56,48},{1,9},... | collective-permute-start | bytes 1400840 | tf_op jit(solution)/shard_map/ppermute | solution.py:173
  80.2 1.9 collective-permute-start.14
  84.9 10.2 %gradients.1 = (bf16[384,3584]{1,0:T(8,128)(2,1)}, bf16[512,256]{1,0:T(8,128)(2,1)}, bf16[512,128]{1,0:T(8,128)(2,1)}) custom-call(s32[2]{0:T(128)} %pad_add_fusion.z_ref, f32[8,128]{1,0:T(8,128)} %broadcast_in_dim.35.sel_ref, bf16[3584,384]{1,0:T(8,128)(2,1)} %all-gather.3.cloned.1.call-done.w_hbm.w_ref, bf16[32,7296]{1,0:T(8,128)(2,1)} %bitcast.14, ...), custom_call_target="tpu_custom_call" | custom-call | tf_op jit(solution)/shard_map/gradients/pallas_call | solution.py:188
  95.1 5.2 %input_part.1 = (bf16[256,3712]{1,0:T(8,128)(2,1)}, bf16[256,3712]{1,0:T(8,128)(2,1)}) custom-call(bf16[512,256]{1,0:T(8,128)(2,1)} %get-tuple-element.29.back_ref, bf16[512,128]{1,0:T(8,128)(2,1)} %get-tuple-element.30.part_ref, bf16[3584,384]{1,0:T(8,128)(2,1)} %all-gather.3.cloned.1.call-done.w_hbm.w_ref), custom_call_target="tpu_custom_call" | custom-call | tf_op jit(solution)/shard_map/input_part/pallas_call | solution.py:209
  100.4 2.0 %collective-permute-start.15 = (bf16[256,3712]{1,0:T(8,128)(2,1)}, bf16[256,3712]{1,0:T(8,128)(2,1)S(1)}, u32[]{:S(2)}, u32[]{:S(2)}) collective-permute-start(bf16[256,3712]{1,0:T(8,128)(2,1)} %get-tuple-element.32), channel_id=1, source_target_pairs={{0,8},{8,0},{16,24},{24,16},{32,40},{40,32},{48,56},{56,48},{1,9},... | collective-permute-start | bytes 5701640 | tf_op jit(solution)/shard_map/ppermute | solution.py:220
  102.4 3.9 %collective-permute-done.15 = bf16[256,3712]{1,0:T(8,128)(2,1)S(1)} collective-permute-done((bf16[256,3712]{1,0:T(8,128)(2,1)}, bf16[256,3712]{1,0:T(8,128)(2,1)S(1)}, u32[]{:S(2)}, u32[]{:S(2)}) %collective-permute-start.15) | collective-permute-done | bytes 1900576 | tf_op jit(solution)/shard_map/ppermute | solution.py:220
  106.3 2.2 %add_convert_fusion = bf16[256,3712]{1,0:T(8,128)(2,1)S(1)} fusion(bf16[256,3712]{1,0:T(8,128)(2,1)S(1)} %collective-permute-done.15, bf16[256,3712]{1,0:T(8,128)(2,1)} %get-tuple-element.31), kind=kLoop, calls=%fused_computation | loop fusion | flops 3801088 | bytes 5701632 | tf_op jit(solution)/shard_map/convert_element_type | solution.py:221
  109.5 4.0 %all-to-all-start.1 = ((bf16[8,32,1792]{2,1,0:T(8,128)(2,1)}), bf16[8,32,1792]{2,1,0:T(8,128)(2,1)S(1)}, u32[]{:S(2)}, u32[]{:S(2)}) async-start(bf16[8,32,1792]{2,1,0:T(8,128)(2,1)} %slice.17), calls=%async_computation.2 | async-start | bytes 1835008 | tf_op jit(solution)/shard_map/all_to_all | solution.py:224
  114.6 25.1 %all-to-all-done.1 = bf16[8,32,1792]{2,1,0:T(8,128)(2,1)S(1)} async-done(((bf16[8,32,1792]{2,1,0:T(8,128)(2,1)}), bf16[8,32,1792]{2,1,0:T(8,128)(2,1)S(1)}, u32[]{:S(2)}, u32[]{:S(2)}) %all-to-all-start.1) | async-done | bytes 917536 | tf_op jit(solution)/shard_map/all_to_all | solution.py:224
  139.8 7.2 %all-to-all-start.2 = ((bf16[8,32,1920]{2,1,0:T(8,128)(2,1)}), bf16[8,32,1920]{2,1,0:T(8,128)(2,1)S(1)}, u32[]{:S(2)}, u32[]{:S(2)}) async-start(bf16[8,32,1920]{2,1,0:T(8,128)(2,1)} %slice.18), calls=%async_computation.3 | async-start | bytes 1966080 | tf_op jit(solution)/shard_map/all_to_all | solution.py:227
  147.1 24.0 %all-to-all-done.2 = bf16[8,32,1920]{2,1,0:T(8,128)(2,1)S(1)} async-done(((bf16[8,32,1920]{2,1,0:T(8,128)(2,1)}), bf16[8,32,1920]{2,1,0:T(8,128)(2,1)S(1)}, u32[]{:S(2)}, u32[]{:S(2)}) %all-to-all-start.2) | async-done | bytes 983072 | tf_op jit(solution)/shard_map/all_to_all | solution.py:227
  171.3 9.5 %all_to_all.21 = bf16[4,8,3712]{2,1,0:T(8,128)(2,1)S(1)} all-to-all(bf16[4,8,3712]{2,1,0:T(8,128)(2,1)S(1)} %maximum_bitcast_fusion), channel_id=1, replica_groups={{0,16,32,48},{8,24,40,56},{1,17,33,49},{9,25,41,57},{2,18,34,50},{10,26..., dimensions={0} | all-to-all | bytes 475136 | tf_op jit(solution)/shard_map/all_to_all | solution.py:232
  182.2 5.5 %all-gather.5.cloned.1.call-done.sum_hbm = bf16[384,3584]{1,0:T(8,128)(2,1)} async-done(((bf16[48,3584]{1,0:T(8,128)(2,1)}), bf16[384,3584]{1,0:T(8,128)(2,1)}) %all-gather.5.cloned.1.call-update) | async-done | bytes 2752528 | tf_op jit(solution)/shard_map/all_gather | solution.py:226
  187.7 3.1 %unpack.1 = (bf16[1,3584,128]{2,1,0:T(8,128)(2,1)}, bf16[1,3584,128]{2,1,0:T(8,128)(2,1)}, bf16[1,128,3584]{2,1,0:T(8,128)(2,1)}) custom-call(bf16[384,3584]{1,0:T(8,128)(2,1)} %all-gather.5.cloned.1.call-done.sum_hbm), custom_call_target="tpu_custom_call" | custom-call | tf_op jit(solution)/shard_map/unpack/pallas_call | solution.py:244
  (56 shorter events, 14.1 us)
Async XLA Ops:
  7.2 77.1 %all-gather.3.cloned.1.call-start = ((), (), s32[]{:S(2)}) async-start(), calls=%async_computation.5 | async-start | bytes 3096576 | tf_op jit(solution)/shard_map/all_gather | solution.py:166
  24.2 60.7 %copy-start = (bf16[4,8,7296]{2,1,0:T(8,128)(2,1)}, bf16[4,8,7296]{2,1,0:T(8,128)(2,1)S(1)}, u32[]{:S(2)}) copy-start(bf16[4,8,7296]{2,1,0:T(8,128)(2,1)S(1)} %all_to_all.20) | copy-start | bytes 1400836
  26.1 113.6 %reduce-scatter.2.cloned.1.call-start = ((), (), s32[]{:S(2)}) async-start(), calls=%async_computation.6 | async-start | bytes 3096576 | tf_op jit(solution)/shard_map/reduce_scatter | solution.py:207
  26.2 3.7 %collective-permute-start = (bf16[32,7296]{1,0:T(8,128)(2,1)S(1)}, bf16[32,7296]{1,0:T(8,128)(2,1)S(1)}, u32[]{:S(2)}, u32[]{:S(2)}) collective-permute-start(bf16[32,7296]{1,0:T(8,128)(2,1)S(1)} %bitcast.12), channel_id=1, source_target_pairs={{0,8},{8,0},{16,24},{24,16},{32,40},{40,32},{48,56},{56,48},{1,9},... | collective-permute-start | bytes 1400840 | tf_op jit(solution)/shard_map/ppermute | solution.py:173
  29.9 55.0 %copy-start.1 = (bf16[32,7296]{1,0:T(8,128)(2,1)}, bf16[32,7296]{1,0:T(8,128)(2,1)S(1)}, u32[]{:S(2)}) copy-start(bf16[32,7296]{1,0:T(8,128)(2,1)S(1)} %collective-permute-done.refs_1_) | copy-start | bytes 1400836
  29.9 14.9 %collective-permute-start.1 = (bf16[32,7296]{1,0:T(8,128)(2,1)S(1)}, bf16[32,7296]{1,0:T(8,128)(2,1)S(1)}, u32[]{:S(2)}, u32[]{:S(2)}) collective-permute-start(bf16[32,7296]{1,0:T(8,128)(2,1)S(1)} %bitcast.13), channel_id=1, source_target_pairs={{0,1},{1,2},{2,3},{3,4},{4,5},{5,6},{6,7},{7,0},{8,15},{9,8},{10,9... | collective-permute-start | bytes 1400840 | tf_op jit(solution)/shard_map/ppermute | solution.py:178
  31.8 18.0 %collective-permute-start.3 = (bf16[32,7296]{1,0:T(8,128)(2,1)S(1)}, bf16[32,7296]{1,0:T(8,128)(2,1)S(1)}, u32[]{:S(2)}, u32[]{:S(2)}) collective-permute-start(bf16[32,7296]{1,0:T(8,128)(2,1)S(1)} %collective-permute-done.refs_1_), channel_id=1, source_target_pairs={{0,1},{1,2},{2,3},{3,4},{4,5},{5,6},{6,7},{7,0},{8,15},{9,8},{10,9... | collective-permute-start | bytes 1400840 | tf_op jit(solution)/shard_map/ppermute | solution.py:178
  44.8 40.1 %copy-start.2 = (bf16[32,7296]{1,0:T(8,128)(2,1)}, bf16[32,7296]{1,0:T(8,128)(2,1)S(1)}, u32[]{:S(2)}) copy-start(bf16[32,7296]{1,0:T(8,128)(2,1)S(1)} %collective-permute-done.1.refs_2_) | copy-start | bytes 1400836
  44.8 11.7 %collective-permute-start.5 = (bf16[32,7296]{1,0:T(8,128)(2,1)S(1)}, bf16[32,7296]{1,0:T(8,128)(2,1)S(1)}, u32[]{:S(2)}, u32[]{:S(2)}) collective-permute-start(bf16[32,7296]{1,0:T(8,128)(2,1)S(1)} %collective-permute-done.1.refs_2_), channel_id=1, source_target_pairs={{0,1},{1,2},{2,3},{3,4},{4,5},{5,6},{6,7},{7,0},{8,15},{9,8},{10,9... | collective-permute-start | bytes 1400840 | tf_op jit(solution)/shard_map/ppermute | solution.py:178
  49.8 35.1 %copy-start.3 = (bf16[32,7296]{1,0:T(8,128)(2,1)}, bf16[32,7296]{1,0:T(8,128)(2,1)S(1)}, u32[]{:S(2)}) copy-start(bf16[32,7296]{1,0:T(8,128)(2,1)S(1)} %collective-permute-done.3.refs_4_) | copy-start | bytes 1400836
  49.8 13.6 %collective-permute-start.7 = (bf16[32,7296]{1,0:T(8,128)(2,1)S(1)}, bf16[32,7296]{1,0:T(8,128)(2,1)S(1)}, u32[]{:S(2)}, u32[]{:S(2)}) collective-permute-start(bf16[32,7296]{1,0:T(8,128)(2,1)S(1)} %collective-permute-done.3.refs_4_), channel_id=1, source_target_pairs={{0,1},{1,2},{2,3},{3,4},{4,5},{5,6},{6,7},{7,0},{8,15},{9,8},{10,9... | collective-permute-start | bytes 1400840 | tf_op jit(solution)/shard_map/ppermute | solution.py:178
  56.5 28.4 %copy-start.4 = (bf16[32,7296]{1,0:T(8,128)(2,1)}, bf16[32,7296]{1,0:T(8,128)(2,1)S(1)}, u32[]{:S(2)}) copy-start(bf16[32,7296]{1,0:T(8,128)(2,1)S(1)} %collective-permute-done.5.refs_6_) | copy-start | bytes 1400836
  56.5 11.7 %collective-permute-start.9 = (bf16[32,7296]{1,0:T(8,128)(2,1)S(1)}, bf16[32,7296]{1,0:T(8,128)(2,1)S(1)}, u32[]{:S(2)}, u32[]{:S(2)}) collective-permute-start(bf16[32,7296]{1,0:T(8,128)(2,1)S(1)} %collective-permute-done.5.refs_6_), channel_id=1, source_target_pairs={{0,1},{1,2},{2,3},{3,4},{4,5},{5,6},{6,7},{7,0},{8,15},{9,8},{10,9... | collective-permute-start | bytes 1400840 | tf_op jit(solution)/shard_map/ppermute | solution.py:178
  58.4 14.0 %collective-permute-start.2 = (bf16[32,7296]{1,0:T(8,128)(2,1)S(1)}, bf16[32,7296]{1,0:T(8,128)(2,1)S(1)}, u32[]{:S(2)}, u32[]{:S(2)}) collective-permute-start(bf16[32,7296]{1,0:T(8,128)(2,1)S(1)} %collective-permute-done.1.refs_2_), channel_id=1, source_target_pairs={{0,8},{8,0},{16,24},{24,16},{32,40},{40,32},{48,56},{56,48},{1,9},... | collective-permute-start | bytes 1400840 | tf_op jit(solution)/shard_map/ppermute | solution.py:173
  61.5 12.9 %collective-permute-start.4 = (bf16[32,7296]{1,0:T(8,128)(2,1)S(1)}, bf16[32,7296]{1,0:T(8,128)(2,1)S(1)}, u32[]{:S(2)}, u32[]{:S(2)}) collective-permute-start(bf16[32,7296]{1,0:T(8,128)(2,1)S(1)} %collective-permute-done.3.refs_4_), channel_id=1, source_target_pairs={{0,8},{8,0},{16,24},{24,16},{32,40},{40,32},{48,56},{56,48},{1,9},... | collective-permute-start | bytes 1400840 | tf_op jit(solution)/shard_map/ppermute | solution.py:173
  63.4 21.5 %copy-start.5 = (bf16[32,7296]{1,0:T(8,128)(2,1)}, bf16[32,7296]{1,0:T(8,128)(2,1)S(1)}, u32[]{:S(2)}) copy-start(bf16[32,7296]{1,0:T(8,128)(2,1)S(1)} %collective-permute-done.7.refs_8_) | copy-start | bytes 1400836
  63.4 13.3 %collective-permute-start.11 = (bf16[32,7296]{1,0:T(8,128)(2,1)S(1)}, bf16[32,7296]{1,0:T(8,128)(2,1)}, u32[]{:S(2)}, u32[]{:S(2)}) collective-permute-start(bf16[32,7296]{1,0:T(8,128)(2,1)S(1)} %collective-permute-done.7.refs_8_), channel_id=1, source_target_pairs={{0,1},{1,2},{2,3},{3,4},{4,5},{5,6},{6,7},{7,0},{8,15},{9,8},{10,9... | collective-permute-start | bytes 1400840 | tf_op jit(solution)/shard_map/ppermute | solution.py:178
  68.1 16.8 %copy-start.6 = (bf16[32,7296]{1,0:T(8,128)(2,1)}, bf16[32,7296]{1,0:T(8,128)(2,1)S(1)}, u32[]{:S(2)}) copy-start(bf16[32,7296]{1,0:T(8,128)(2,1)S(1)} %collective-permute-done.9.refs_10_) | copy-start | bytes 1400836
  68.1 12.1 %collective-permute-start.13 = (bf16[32,7296]{1,0:T(8,128)(2,1)S(1)}, bf16[32,7296]{1,0:T(8,128)(2,1)}, u32[]{:S(2)}, u32[]{:S(2)}) collective-permute-start(bf16[32,7296]{1,0:T(8,128)(2,1)S(1)} %collective-permute-done.9.refs_10_), channel_id=1, source_target_pairs={{0,1},{1,2},{2,3},{3,4},{4,5},{5,6},{6,7},{7,0},{8,15},{9,8},{10,9... | collective-permute-start | bytes 1400840 | tf_op jit(solution)/shard_map/ppermute | solution.py:178
  70.1 12.7 %collective-permute-start.6 = (bf16[32,7296]{1,0:T(8,128)(2,1)S(1)}, bf16[32,7296]{1,0:T(8,128)(2,1)}, u32[]{:S(2)}, u32[]{:S(2)}) collective-permute-start(bf16[32,7296]{1,0:T(8,128)(2,1)S(1)} %collective-permute-done.5.refs_6_), channel_id=1, source_target_pairs={{0,8},{8,0},{16,24},{24,16},{32,40},{40,32},{48,56},{56,48},{1,9},... | collective-permute-start | bytes 1400840 | tf_op jit(solution)/shard_map/ppermute | solution.py:173
  72.4 7.8 %copy-start.7 = (bf16[32,7296]{1,0:T(8,128)(2,1)}, bf16[32,7296]{1,0:T(8,128)(2,1)S(1)}, u32[]{:S(2)}) copy-start(bf16[32,7296]{1,0:T(8,128)(2,1)S(1)} %collective-permute-done.2.refs_3_) | copy-start | bytes 1400836
  72.4 10.4 %collective-permute-start.8 = (bf16[32,7296]{1,0:T(8,128)(2,1)S(1)}, bf16[32,7296]{1,0:T(8,128)(2,1)}, u32[]{:S(2)}, u32[]{:S(2)}) collective-permute-start(bf16[32,7296]{1,0:T(8,128)(2,1)S(1)} %collective-permute-done.7.refs_8_), channel_id=1, source_target_pairs={{0,8},{8,0},{16,24},{24,16},{32,40},{40,32},{48,56},{56,48},{1,9},... | collective-permute-start | bytes 1400840 | tf_op jit(solution)/shard_map/ppermute | solution.py:173
  74.4 7.7 %copy-start.8 = (bf16[32,7296]{1,0:T(8,128)(2,1)}, bf16[32,7296]{1,0:T(8,128)(2,1)S(1)}, u32[]{:S(2)}) copy-start(bf16[32,7296]{1,0:T(8,128)(2,1)S(1)} %collective-permute-done.4.refs_5_) | copy-start | bytes 1400836
  74.5 8.3 %collective-permute-start.10 = (bf16[32,7296]{1,0:T(8,128)(2,1)S(1)}, bf16[32,7296]{1,0:T(8,128)(2,1)}, u32[]{:S(2)}, u32[]{:S(2)}) collective-permute-start(bf16[32,7296]{1,0:T(8,128)(2,1)S(1)} %collective-permute-done.9.refs_10_), channel_id=1, source_target_pairs={{0,8},{8,0},{16,24},{24,16},{32,40},{40,32},{48,56},{56,48},{1,9},... | collective-permute-start | bytes 1400840 | tf_op jit(solution)/shard_map/ppermute | solution.py:173
  76.8 6.0 %collective-permute-start.12 = (bf16[32,7296]{1,0:T(8,128)(2,1)}, bf16[32,7296]{1,0:T(8,128)(2,1)}, u32[]{:S(2)}, u32[]{:S(2)}) collective-permute-start(bf16[32,7296]{1,0:T(8,128)(2,1)} %collective-permute-done.11.refs_12_), channel_id=1, source_target_pairs={{0,8},{8,0},{16,24},{24,16},{32,40},{40,32},{48,56},{56,48},{1,9},... | collective-permute-start | bytes 1400840 | tf_op jit(solution)/shard_map/ppermute | solution.py:173
  80.2 4.1 %collective-permute-start.14 = (bf16[32,7296]{1,0:T(8,128)(2,1)}, bf16[32,7296]{1,0:T(8,128)(2,1)}, u32[]{:S(2)}, u32[]{:S(2)}) collective-permute-start(bf16[32,7296]{1,0:T(8,128)(2,1)} %collective-permute-done.13.refs_14_), channel_id=1, source_target_pairs={{0,8},{8,0},{16,24},{24,16},{32,40},{40,32},{48,56},{56,48},{1,9},... | collective-permute-start | bytes 1400840 | tf_op jit(solution)/shard_map/ppermute | solution.py:173
  100.4 6.0 %collective-permute-start.15 = (bf16[256,3712]{1,0:T(8,128)(2,1)}, bf16[256,3712]{1,0:T(8,128)(2,1)S(1)}, u32[]{:S(2)}, u32[]{:S(2)}) collective-permute-start(bf16[256,3712]{1,0:T(8,128)(2,1)} %get-tuple-element.32), channel_id=1, source_target_pairs={{0,8},{8,0},{16,24},{24,16},{32,40},{40,32},{48,56},{56,48},{1,9},... | collective-permute-start | bytes 5701640 | tf_op jit(solution)/shard_map/ppermute | solution.py:220
  109.5 30.2 %all-to-all-start.1 = ((bf16[8,32,1792]{2,1,0:T(8,128)(2,1)}), bf16[8,32,1792]{2,1,0:T(8,128)(2,1)S(1)}, u32[]{:S(2)}, u32[]{:S(2)}) async-start(bf16[8,32,1792]{2,1,0:T(8,128)(2,1)} %slice.17), calls=%async_computation.2 | async-start | bytes 1835008 | tf_op jit(solution)/shard_map/all_to_all | solution.py:224
  113.5 74.2 %all-gather.5.cloned.1.call-start = ((), (), s32[]{:S(2)}) async-start(), calls=%async_computation.7 | async-start | bytes 3096576 | tf_op jit(solution)/shard_map/all_gather | solution.py:226
  139.8 31.3 %all-to-all-start.2 = ((bf16[8,32,1920]{2,1,0:T(8,128)(2,1)}), bf16[8,32,1920]{2,1,0:T(8,128)(2,1)S(1)}, u32[]{:S(2)}, u32[]{:S(2)}) async-start(bf16[8,32,1920]{2,1,0:T(8,128)(2,1)} %slice.18), calls=%async_computation.3 | async-start | bytes 1966080 | tf_op jit(solution)/shard_map/all_to_all | solution.py:227
  147.0 34.5 %copy-start.9 = (s32[8,4]{0,1:T(4,128)S(1)}, s32[8,4]{0,1:T(4,128)}, u32[]{:S(2)}) copy-start(s32[8,4]{0,1:T(4,128)} %param.10) | copy-start | bytes 388
Sparse Core Ops, SparseCore 0:
  26.3 46.7 all-gather.2
  95.3 44.3 reduce-scatter.1
  142.0 45.6 all-gather.4

commit v4 on v3

--- a/solution.py
+++ b/solution.py
@@ -11,12 +11,13 @@
 STEP = 1792
 
 
-def gradients_kernel(plan, z_ref, sel_ref, w_hbm, *refs):
+def gradients_kernel(plan, w_hbm, *refs):
     blocks = refs[: len(plan)]
     grads_hbm, back_ref, part_ref, rows, weights, grads, sems = refs[len(plan) :]
     half = rows.shape[0] // 2
     width = (rows.shape[1] - LANES) // 2
-    here, towards = z_ref[0], z_ref[1]
+    node = lax.axis_index("node")
+    here, towards = lax.axis_index("local"), 2 * lax.rem(node, 2) - 1
     size = blocks[0].shape[0]
     places = half // size
     early = [pltpu.make_async_copy(w_hbm, weights, sems.at[0])]
@@ -57,7 +58,8 @@
         copy.wait()
     raw = lax.fori_loop(0, steps, project_back, jnp.zeros((2 * half, LANES), jnp.float32))
     pre_gate, pre_up = pre[:, :LANES], pre[:, LANES:]
-    sel = sel_ref[0:1, :]
+    lanes = lax.broadcasted_iota(jnp.int32, (1, LANES), 1)
+    sel = (lanes == node).astype(jnp.float32)
     weight = jnp.sum(rows[:, 2 * width :].astype(jnp.float32) * sel, axis=1, keepdims=True)
     sigmoid = jax.nn.sigmoid(pre_gate)
     activated = (pre_gate * sigmoid * pre_up).astype(jnp.bfloat16).astype(jnp.float32)
@@ -142,8 +144,6 @@
     places = lax.axis_size("local")
     count, width = tokens.shape
     columns = nodes // 2
-    node = lax.axis_index("node")
-    place = lax.axis_index("local")
     wide = 2 * width + LANES
 
     lanes = jnp.arange(LANES, dtype=jnp.int32)
@@ -180,9 +180,6 @@
             plan += [(hop, which), (-hop, 1 - which)]
 
     half = places * block.shape[0]
-    core = lax.rem(node, 2)
-    where = jnp.stack([place, 2 * core - 1]).astype(jnp.int32)
-    sel = jnp.broadcast_to((lanes == node).astype(jnp.float32)[None], (8, LANES))
     vmem = pl.BlockSpec(memory_space=pltpu.VMEM)
     anywhere = pl.BlockSpec(memory_space=pl.ANY)
     grads, back, part = pl.pallas_call(
@@ -192,7 +189,7 @@
             jax.ShapeDtypeStruct((2 * half, 2 * LANES), jnp.bfloat16),
             jax.ShapeDtypeStruct((2 * half, LANES), jnp.bfloat16),
         ),
-        in_specs=[pl.BlockSpec(memory_space=pltpu.SMEM), vmem] + [anywhere] * (1 + len(blocks)),
+        in_specs=[anywhere] * (1 + len(blocks)),
         out_specs=(anywhere, vmem, vmem),
         scratch_shapes=[
             pltpu.VMEM((2 * half, wide), jnp.bfloat16),
@@ -202,7 +199,7 @@
         ],
         compiler_params=params(),
         name="gradients",
-    )(where, sel, weights, *blocks)
+    )(weights, *blocks)
 
     share = lax.psum_scatter(grads, "dp", scatter_dimension=0, tiled=True)
 

time: 198 us -> 197 us (level)
  transfers between devices with their start and end apart: 21 -> 21, of which waited for: 11 -> 10; matrix products, arithmetic and copies ran while one was open for 3% -> 3% of each run, Pallas kernels for 3% -> 3%
where the time goes in v4:
time: 197 us; the launch traced here: 196 us
  waiting for transfers between devices  81.2 us (41%)
  starting transfers between devices  46.6 us (24%)
  blocking collectives  24.1 us (12%)
  Pallas kernels  17.8 us (9%)
  between operations  14.1 us (7%)
  other arithmetic  7.49 us (4%)
  local copies, waits for them, and re-layouts  4.52 us (2%)
    all_to_all x1, waiting for transfers between devices, shards(): first = lax.all_to_all(chip[:, :, :cut], 'local', 0, 0, tiled=True)  25.4 us
    all_to_all x1, waiting for transfers between devices, shards(): rest = lax.all_to_all(rest, 'local', 0, 0, tiled=True)  24.1 us
    ppermute x7, waiting for transfers between devices, shards(): chains[which] = lax.ppermute(chains[which], ('node', 'local'), ring)  20.8 us
    ppermute x8, starting transfers between devices, shards(): swap = lambda piece: lax.ppermute(piece, 'node', cores)  17.5 us
    ppermute x7, starting transfers between devices, shards(): chains[which] = lax.ppermute(chains[which], ('node', 'local'), ring)  15.5 us
    all_to_all x1, blocking collectives, shards(): lax.all_to_all(jnp.broadcast_to(mine, (columns, count, wide)), 'node', 0,...  14.6 us
    pallas_call x1, Pallas kernels, shards(): pl.pallas_call(functools.partial(gradients_kernel, plan), out_shape=(jax....  9.53 us
    all_to_all x1, blocking collectives, shards(): lax.all_to_all(column.reshape(columns, count, width + LANES), 'node', 0,...  9.49 us
  transfers between devices with their start and end apart: 21, of which 10 were waited for; matrix products, arithmetic and copies ran while one was open for 3% of the time, Pallas kernels for 3%

profile of v4, /device:TPU:2, one launch (start us, length us, event | category | flops | bytes accessed | tf_op | source)
XLA Modules:
  0.0 195.8 jit_solution(12048618955678242963)
XLA Ops:
  9.6 14.6 %all_to_all.20 = bf16[4,8,7296]{2,1,0:T(8,128)(2,1)S(1)} all-to-all(bf16[4,8,7296]{2,1,0:T(8,128)(2,1)S(1)} %broadcast_in_dim.31), channel_id=1, replica_groups={{0,16,32,48},{8,24,40,56},{1,17,33,49},{9,25,41,57},{2,18,34,50},{10,26..., dimensions={0} | all-to-all | bytes 933888 | tf_op jit(solution)/shard_map/all_to_all | solution.py:156
  24.2 2.0 %pad_maximum_fusion = bf16[448,384]{1,0:T(8,128)(2,1)} fusion(bf16[448,128]{1,0:T(8,128)(2,1)} %bitcast.13, bf16[448,128]{1,0:T(8,128)(2,1)} %bitcast.14, bf16[448,128]{1,0:T(8,128)(2,1)} %bitcast.15), kind=kLoop, calls=%fused_computation.2 | loop fusion | flops 1032192 | bytes 688128 | tf_op jit(solution)/shard_map/concatenate | solution.py:165
  26.2 1.9 collective-permute-start
  29.9 1.9 collective-permute-start.1
  31.8 4.1 %collective-permute-start.3 = (bf16[32,7296]{1,0:T(8,128)(2,1)S(1)}, bf16[32,7296]{1,0:T(8,128)(2,1)S(1)}, u32[]{:S(2)}, u32[]{:S(2)}) collective-permute-start(bf16[32,7296]{1,0:T(8,128)(2,1)S(1)} %collective-permute-done.refs_1_), channel_id=1, source_target_pairs={{0,1},{1,2},{2,3},{3,4},{4,5},{5,6},{6,7},{7,0},{8,15},{9,8},{10,9... | collective-permute-start | bytes 1400840 | tf_op jit(solution)/shard_map/ppermute | solution.py:178
  35.9 8.9 %collective-permute-done.1.refs_2_ = bf16[32,7296]{1,0:T(8,128)(2,1)S(1)} collective-permute-done((bf16[32,7296]{1,0:T(8,128)(2,1)S(1)}, bf16[32,7296]{1,0:T(8,128)(2,1)S(1)}, u32[]{:S(2)}, u32[]{:S(2)}) %collective-permute-start.1) | collective-permute-done | bytes 466976 | tf_op jit(solution)/shard_map/ppermute | solution.py:178
  44.8 1.9 collective-permute-start.5
  46.7 3.1 %collective-permute-done.3.refs_4_ = bf16[32,7296]{1,0:T(8,128)(2,1)S(1)} collective-permute-done((bf16[32,7296]{1,0:T(8,128)(2,1)S(1)}, bf16[32,7296]{1,0:T(8,128)(2,1)S(1)}, u32[]{:S(2)}, u32[]{:S(2)}) %collective-permute-start.3) | collective-permute-done | bytes 466976 | tf_op jit(solution)/shard_map/ppermute | solution.py:178
  49.8 1.9 collective-permute-start.7
  51.7 4.7 %collective-permute-done.5.refs_6_ = bf16[32,7296]{1,0:T(8,128)(2,1)S(1)} collective-permute-done((bf16[32,7296]{1,0:T(8,128)(2,1)S(1)}, bf16[32,7296]{1,0:T(8,128)(2,1)S(1)}, u32[]{:S(2)}, u32[]{:S(2)}) %collective-permute-start.5) | collective-permute-done | bytes 466976 | tf_op jit(solution)/shard_map/ppermute | solution.py:178
  56.5 1.9 collective-permute-start.9
  58.4 3.1 %collective-permute-start.2 = (bf16[32,7296]{1,0:T(8,128)(2,1)S(1)}, bf16[32,7296]{1,0:T(8,128)(2,1)S(1)}, u32[]{:S(2)}, u32[]{:S(2)}) collective-permute-start(bf16[32,7296]{1,0:T(8,128)(2,1)S(1)} %collective-permute-done.1.refs_2_), channel_id=1, source_target_pairs={{0,8},{8,0},{16,24},{24,16},{32,40},{40,32},{48,56},{56,48},{1,9},... | collective-permute-start | bytes 1400840 | tf_op jit(solution)/shard_map/ppermute | solution.py:173
  61.5 1.9 collective-permute-start.4
  63.4 1.9 collective-permute-start.11
  65.4 2.8 %collective-permute-done.9.refs_10_ = bf16[32,7296]{1,0:T(8,128)(2,1)S(1)} collective-permute-done((bf16[32,7296]{1,0:T(8,128)(2,1)S(1)}, bf16[32,7296]{1,0:T(8,128)(2,1)S(1)}, u32[]{:S(2)}, u32[]{:S(2)}) %collective-permute-start.9) | collective-permute-done | bytes 466976 | tf_op jit(solution)/shard_map/ppermute | solution.py:178
  70.1 2.3 %collective-permute-start.6 = (bf16[32,7296]{1,0:T(8,128)(2,1)S(1)}, bf16[32,7296]{1,0:T(8,128)(2,1)S(1)}, u32[]{:S(2)}, u32[]{:S(2)}) collective-permute-start(bf16[32,7296]{1,0:T(8,128)(2,1)S(1)} %collective-permute-done.5.refs_6_), channel_id=1, source_target_pairs={{0,8},{8,0},{16,24},{24,16},{32,40},{40,32},{48,56},{56,48},{1,9},... | collective-permute-start | bytes 1400840 | tf_op jit(solution)/shard_map/ppermute | solution.py:173
  72.4 2.0 %collective-permute-start.8 = (bf16[32,7296]{1,0:T(8,128)(2,1)S(1)}, bf16[32,7296]{1,0:T(8,128)(2,1)S(1)}, u32[]{:S(2)}, u32[]{:S(2)}) collective-permute-start(bf16[32,7296]{1,0:T(8,128)(2,1)S(1)} %collective-permute-done.7.refs_8_), channel_id=1, source_target_pairs={{0,8},{8,0},{16,24},{24,16},{32,40},{40,32},{48,56},{56,48},{1,9},... | collective-permute-start | bytes 1400840 | tf_op jit(solution)/shard_map/ppermute | solution.py:173
  74.4 2.3 %collective-permute-start.10 = (bf16[32,7296]{1,0:T(8,128)(2,1)S(1)}, bf16[32,7296]{1,0:T(8,128)(2,1)S(1)}, u32[]{:S(2)}, u32[]{:S(2)}) collective-permute-start(bf16[32,7296]{1,0:T(8,128)(2,1)S(1)} %collective-permute-done.9.refs_10_), channel_id=1, source_target_pairs={{0,8},{8,0},{16,24},{24,16},{32,40},{40,32},{48,56},{56,48},{1,9},... | collective-permute-start | bytes 1400840 | tf_op jit(solution)/shard_map/ppermute | solution.py:173
  76.8 2.0 %collective-permute-start.12 = (bf16[32,7296]{1,0:T(8,128)(2,1)S(1)}, bf16[32,7296]{1,0:T(8,128)(2,1)S(1)}, u32[]{:S(2)}, u32[]{:S(2)}) collective-permute-start(bf16[32,7296]{1,0:T(8,128)(2,1)S(1)} %collective-permute-done.11.refs_12_), channel_id=1, source_target_pairs={{0,8},{8,0},{16,24},{24,16},{32,40},{40,32},{48,56},{56,48},{1,9},... | collective-permute-start | bytes 1400840 | tf_op jit(solution)/shard_map/ppermute | solution.py:173
  80.1 1.9 collective-permute-start.14
  84.0 9.5 %gradients.1 = (bf16[384,3584]{1,0:T(8,128)(2,1)}, bf16[512,256]{1,0:T(8,128)(2,1)}, bf16[512,128]{1,0:T(8,128)(2,1)}) custom-call(bf16[3584,384]{1,0:T(8,128)(2,1)} %all-gather.3.cloned.1.call-done.w_hbm.w_ref, bf16[32,7296]{1,0:T(8,128)(2,1)} %bitcast.12, bf16[32,7296]{1,0:T(8,128)(2,1)} %copy-done.1, bf16[32,7296]{1,0:T(8,128)(2,1)} %copy-done.2, ...), custom_call_target="tpu_custom_call" | custom-call | tf_op jit(solution)/shard_map/gradients/pallas_call | solution.py:185
  93.6 5.2 %input_part.1 = (bf16[256,3712]{1,0:T(8,128)(2,1)}, bf16[256,3712]{1,0:T(8,128)(2,1)}) custom-call(bf16[512,256]{1,0:T(8,128)(2,1)} %get-tuple-element.29.back_ref, bf16[512,128]{1,0:T(8,128)(2,1)} %get-tuple-element.30.part_ref, bf16[3584,384]{1,0:T(8,128)(2,1)} %all-gather.3.cloned.1.call-done.w_hbm.w_ref), custom_call_target="tpu_custom_call" | custom-call | tf_op jit(solution)/shard_map/input_part/pallas_call | solution.py:206
  98.8 2.4 %collective-permute-start.15 = (bf16[256,3712]{1,0:T(8,128)(2,1)}, bf16[256,3712]{1,0:T(8,128)(2,1)S(1)}, u32[]{:S(2)}, u32[]{:S(2)}) collective-permute-start(bf16[256,3712]{1,0:T(8,128)(2,1)} %get-tuple-element.32), channel_id=1, source_target_pairs={{0,8},{8,0},{16,24},{24,16},{32,40},{40,32},{48,56},{56,48},{1,9},... | collective-permute-start | bytes 5701640 | tf_op jit(solution)/shard_map/ppermute | solution.py:217
  101.2 3.7 %collective-permute-done.15 = bf16[256,3712]{1,0:T(8,128)(2,1)S(1)} collective-permute-done((bf16[256,3712]{1,0:T(8,128)(2,1)}, bf16[256,3712]{1,0:T(8,128)(2,1)S(1)}, u32[]{:S(2)}, u32[]{:S(2)}) %collective-permute-start.15) | collective-permute-done | bytes 1900576 | tf_op jit(solution)/shard_map/ppermute | solution.py:217
  104.8 2.2 %add_convert_fusion = bf16[256,3712]{1,0:T(8,128)(2,1)S(1)} fusion(bf16[256,3712]{1,0:T(8,128)(2,1)S(1)} %collective-permute-done.15, bf16[256,3712]{1,0:T(8,128)(2,1)} %get-tuple-element.31), kind=kLoop, calls=%fused_computation | loop fusion | flops 3801088 | bytes 5701632 | tf_op jit(solution)/shard_map/convert_element_type | solution.py:218
  108.0 4.0 %all-to-all-start.1 = ((bf16[8,32,1792]{2,1,0:T(8,128)(2,1)}), bf16[8,32,1792]{2,1,0:T(8,128)(2,1)S(1)}, u32[]{:S(2)}, u32[]{:S(2)}) async-start(bf16[8,32,1792]{2,1,0:T(8,128)(2,1)} %slice.17), calls=%async_computation.2 | async-start | bytes 1835008 | tf_op jit(solution)/shard_map/all_to_all | solution.py:221
  113.1 25.4 %all-to-all-done.1 = bf16[8,32,1792]{2,1,0:T(8,128)(2,1)S(1)} async-done(((bf16[8,32,1792]{2,1,0:T(8,128)(2,1)}), bf16[8,32,1792]{2,1,0:T(8,128)(2,1)S(1)}, u32[]{:S(2)}, u32[]{:S(2)}) %all-to-all-start.1) | async-done | bytes 917536 | tf_op jit(solution)/shard_map/all_to_all | solution.py:221
  138.5 7.0 %all-to-all-start.2 = ((bf16[8,32,1920]{2,1,0:T(8,128)(2,1)}), bf16[8,32,1920]{2,1,0:T(8,128)(2,1)S(1)}, u32[]{:S(2)}, u32[]{:S(2)}) async-start(bf16[8,32,1920]{2,1,0:T(8,128)(2,1)} %slice.18), calls=%async_computation.3 | async-start | bytes 1966080 | tf_op jit(solution)/shard_map/all_to_all | solution.py:224
  145.7 24.1 %all-to-all-done.2 = bf16[8,32,1920]{2,1,0:T(8,128)(2,1)S(1)} async-done(((bf16[8,32,1920]{2,1,0:T(8,128)(2,1)}), bf16[8,32,1920]{2,1,0:T(8,128)(2,1)S(1)}, u32[]{:S(2)}, u32[]{:S(2)}) %all-to-all-start.2) | async-done | bytes 983072 | tf_op jit(solution)/shard_map/all_to_all | solution.py:224
  170.0 9.5 %all_to_all.21 = bf16[4,8,3712]{2,1,0:T(8,128)(2,1)S(1)} all-to-all(bf16[4,8,3712]{2,1,0:T(8,128)(2,1)S(1)} %maximum_bitcast_fusion), channel_id=1, replica_groups={{0,16,32,48},{8,24,40,56},{1,17,33,49},{9,25,41,57},{2,18,34,50},{10,26..., dimensions={0} | all-to-all | bytes 475136 | tf_op jit(solution)/shard_map/all_to_all | solution.py:229
  180.9 5.3 %all-gather.5.cloned.1.call-done.sum_hbm = bf16[384,3584]{1,0:T(8,128)(2,1)} async-done(((bf16[48,3584]{1,0:T(8,128)(2,1)}), bf16[384,3584]{1,0:T(8,128)(2,1)}) %all-gather.5.cloned.1.call-update) | async-done | bytes 2752528 | tf_op jit(solution)/shard_map/all_gather | solution.py:223
  186.2 3.1 %unpack.1 = (bf16[1,3584,128]{2,1,0:T(8,128)(2,1)}, bf16[1,3584,128]{2,1,0:T(8,128)(2,1)}, bf16[1,128,3584]{2,1,0:T(8,128)(2,1)}) custom-call(bf16[384,3584]{1,0:T(8,128)(2,1)} %all-gather.5.cloned.1.call-done.sum_hbm), custom_call_target="tpu_custom_call" | custom-call | tf_op jit(solution)/shard_map/unpack/pallas_call | solution.py:241
  (65 shorter events, 13.1 us)
Async XLA Ops:
  7.2 76.8 %all-gather.3.cloned.1.call-start = ((), (), s32[]{:S(2)}) async-start(), calls=%async_computation.5 | async-start | bytes 3096576 | tf_op jit(solution)/shard_map/all_gather | solution.py:166
  24.2 59.8 %copy-start = (bf16[4,8,7296]{2,1,0:T(8,128)(2,1)}, bf16[4,8,7296]{2,1,0:T(8,128)(2,1)S(1)}, u32[]{:S(2)}) copy-start(bf16[4,8,7296]{2,1,0:T(8,128)(2,1)S(1)} %all_to_all.20) | copy-start | bytes 1400836
  26.1 112.4 %reduce-scatter.2.cloned.1.call-start = ((), (), s32[]{:S(2)}) async-start(), calls=%async_computation.6 | async-start | bytes 3096576 | tf_op jit(solution)/shard_map/reduce_scatter | solution.py:204
  26.2 3.7 %collective-permute-start = (bf16[32,7296]{1,0:T(8,128)(2,1)S(1)}, bf16[32,7296]{1,0:T(8,128)(2,1)S(1)}, u32[]{:S(2)}, u32[]{:S(2)}) collective-permute-start(bf16[32,7296]{1,0:T(8,128)(2,1)S(1)} %bitcast.10), channel_id=1, source_target_pairs={{0,8},{8,0},{16,24},{24,16},{32,40},{40,32},{48,56},{56,48},{1,9},... | collective-permute-start | bytes 1400840 | tf_op jit(solution)/shard_map/ppermute | solution.py:173
  29.9 54.0 %copy-start.1 = (bf16[32,7296]{1,0:T(8,128)(2,1)}, bf16[32,7296]{1,0:T(8,128)(2,1)S(1)}, u32[]{:S(2)}) copy-start(bf16[32,7296]{1,0:T(8,128)(2,1)S(1)} %collective-permute-done.refs_1_) | copy-start | bytes 1400836
  29.9 14.9 %collective-permute-start.1 = (bf16[32,7296]{1,0:T(8,128)(2,1)S(1)}, bf16[32,7296]{1,0:T(8,128)(2,1)S(1)}, u32[]{:S(2)}, u32[]{:S(2)}) collective-permute-start(bf16[32,7296]{1,0:T(8,128)(2,1)S(1)} %bitcast.11), channel_id=1, source_target_pairs={{0,1},{1,2},{2,3},{3,4},{4,5},{5,6},{6,7},{7,0},{8,15},{9,8},{10,9... | collective-permute-start | bytes 1400840 | tf_op jit(solution)/shard_map/ppermute | solution.py:178
  31.8 18.0 %collective-permute-start.3 = (bf16[32,7296]{1,0:T(8,128)(2,1)S(1)}, bf16[32,7296]{1,0:T(8,128)(2,1)S(1)}, u32[]{:S(2)}, u32[]{:S(2)}) collective-permute-start(bf16[32,7296]{1,0:T(8,128)(2,1)S(1)} %collective-permute-done.refs_1_), channel_id=1, source_target_pairs={{0,1},{1,2},{2,3},{3,4},{4,5},{5,6},{6,7},{7,0},{8,15},{9,8},{10,9... | collective-permute-start | bytes 1400840 | tf_op jit(solution)/shard_map/ppermute | solution.py:178
  44.8 39.1 %copy-start.2 = (bf16[32,7296]{1,0:T(8,128)(2,1)}, bf16[32,7296]{1,0:T(8,128)(2,1)S(1)}, u32[]{:S(2)}) copy-start(bf16[32,7296]{1,0:T(8,128)(2,1)S(1)} %collective-permute-done.1.refs_2_) | copy-start | bytes 1400836
  44.8 11.7 %collective-permute-start.5 = (bf16[32,7296]{1,0:T(8,128)(2,1)S(1)}, bf16[32,7296]{1,0:T(8,128)(2,1)S(1)}, u32[]{:S(2)}, u32[]{:S(2)}) collective-permute-start(bf16[32,7296]{1,0:T(8,128)(2,1)S(1)} %collective-permute-done.1.refs_2_), channel_id=1, source_target_pairs={{0,1},{1,2},{2,3},{3,4},{4,5},{5,6},{6,7},{7,0},{8,15},{9,8},{10,9... | collective-permute-start | bytes 1400840 | tf_op jit(solution)/shard_map/ppermute | solution.py:178
  49.8 34.1 %copy-start.3 = (bf16[32,7296]{1,0:T(8,128)(2,1)}, bf16[32,7296]{1,0:T(8,128)(2,1)S(1)}, u32[]{:S(2)}) copy-start(bf16[32,7296]{1,0:T(8,128)(2,1)S(1)} %collective-permute-done.3.refs_4_) | copy-start | bytes 1400836
  49.8 13.6 %collective-permute-start.7 = (bf16[32,7296]{1,0:T(8,128)(2,1)S(1)}, bf16[32,7296]{1,0:T(8,128)(2,1)S(1)}, u32[]{:S(2)}, u32[]{:S(2)}) collective-permute-start(bf16[32,7296]{1,0:T(8,128)(2,1)S(1)} %collective-permute-done.3.refs_4_), channel_id=1, source_target_pairs={{0,1},{1,2},{2,3},{3,4},{4,5},{5,6},{6,7},{7,0},{8,15},{9,8},{10,9... | collective-permute-start | bytes 1400840 | tf_op jit(solution)/shard_map/ppermute | solution.py:178
  56.5 27.5 %copy-start.4 = (bf16[32,7296]{1,0:T(8,128)(2,1)}, bf16[32,7296]{1,0:T(8,128)(2,1)S(1)}, u32[]{:S(2)}) copy-start(bf16[32,7296]{1,0:T(8,128)(2,1)S(1)} %collective-permute-done.5.refs_6_) | copy-start | bytes 1400836
  56.5 11.7 %collective-permute-start.9 = (bf16[32,7296]{1,0:T(8,128)(2,1)S(1)}, bf16[32,7296]{1,0:T(8,128)(2,1)S(1)}, u32[]{:S(2)}, u32[]{:S(2)}) collective-permute-start(bf16[32,7296]{1,0:T(8,128)(2,1)S(1)} %collective-permute-done.5.refs_6_), channel_id=1, source_target_pairs={{0,1},{1,2},{2,3},{3,4},{4,5},{5,6},{6,7},{7,0},{8,15},{9,8},{10,9... | collective-permute-start | bytes 1400840 | tf_op jit(solution)/shard_map/ppermute | solution.py:178
  58.4 14.0 %collective-permute-start.2 = (bf16[32,7296]{1,0:T(8,128)(2,1)S(1)}, bf16[32,7296]{1,0:T(8,128)(2,1)S(1)}, u32[]{:S(2)}, u32[]{:S(2)}) collective-permute-start(bf16[32,7296]{1,0:T(8,128)(2,1)S(1)} %collective-permute-done.1.refs_2_), channel_id=1, source_target_pairs={{0,8},{8,0},{16,24},{24,16},{32,40},{40,32},{48,56},{56,48},{1,9},... | collective-permute-start | bytes 1400840 | tf_op jit(solution)/shard_map/ppermute | solution.py:173
  61.5 12.9 %collective-permute-start.4 = (bf16[32,7296]{1,0:T(8,128)(2,1)S(1)}, bf16[32,7296]{1,0:T(8,128)(2,1)S(1)}, u32[]{:S(2)}, u32[]{:S(2)}) collective-permute-start(bf16[32,7296]{1,0:T(8,128)(2,1)S(1)} %collective-permute-done.3.refs_4_), channel_id=1, source_target_pairs={{0,8},{8,0},{16,24},{24,16},{32,40},{40,32},{48,56},{56,48},{1,9},... | collective-permute-start | bytes 1400840 | tf_op jit(solution)/shard_map/ppermute | solution.py:173
  63.4 20.6 %copy-start.5 = (bf16[32,7296]{1,0:T(8,128)(2,1)}, bf16[32,7296]{1,0:T(8,128)(2,1)S(1)}, u32[]{:S(2)}) copy-start(bf16[32,7296]{1,0:T(8,128)(2,1)S(1)} %collective-permute-done.7.refs_8_) | copy-start | bytes 1400836
  63.4 13.3 %collective-permute-start.11 = (bf16[32,7296]{1,0:T(8,128)(2,1)S(1)}, bf16[32,7296]{1,0:T(8,128)(2,1)S(1)}, u32[]{:S(2)}, u32[]{:S(2)}) collective-permute-start(bf16[32,7296]{1,0:T(8,128)(2,1)S(1)} %collective-permute-done.7.refs_8_), channel_id=1, source_target_pairs={{0,1},{1,2},{2,3},{3,4},{4,5},{5,6},{6,7},{7,0},{8,15},{9,8},{10,9... | collective-permute-start | bytes 1400840 | tf_op jit(solution)/shard_map/ppermute | solution.py:178
  68.1 15.9 %copy-start.6 = (bf16[32,7296]{1,0:T(8,128)(2,1)}, bf16[32,7296]{1,0:T(8,128)(2,1)S(1)}, u32[]{:S(2)}) copy-start(bf16[32,7296]{1,0:T(8,128)(2,1)S(1)} %collective-permute-done.9.refs_10_) | copy-start | bytes 1400836
  68.1 12.0 %collective-permute-start.13 = (bf16[32,7296]{1,0:T(8,128)(2,1)S(1)}, bf16[32,7296]{1,0:T(8,128)(2,1)S(1)}, u32[]{:S(2)}, u32[]{:S(2)}) collective-permute-start(bf16[32,7296]{1,0:T(8,128)(2,1)S(1)} %collective-permute-done.9.refs_10_), channel_id=1, source_target_pairs={{0,1},{1,2},{2,3},{3,4},{4,5},{5,6},{6,7},{7,0},{8,15},{9,8},{10,9... | collective-permute-start | bytes 1400840 | tf_op jit(solution)/shard_map/ppermute | solution.py:178
  70.1 12.0 %collective-permute-start.6 = (bf16[32,7296]{1,0:T(8,128)(2,1)S(1)}, bf16[32,7296]{1,0:T(8,128)(2,1)S(1)}, u32[]{:S(2)}, u32[]{:S(2)}) collective-permute-start(bf16[32,7296]{1,0:T(8,128)(2,1)S(1)} %collective-permute-done.5.refs_6_), channel_id=1, source_target_pairs={{0,8},{8,0},{16,24},{24,16},{32,40},{40,32},{48,56},{56,48},{1,9},... | collective-permute-start | bytes 1400840 | tf_op jit(solution)/shard_map/ppermute | solution.py:173
  72.4 9.7 %copy-start.7 = (bf16[32,7296]{1,0:T(8,128)(2,1)}, bf16[32,7296]{1,0:T(8,128)(2,1)S(1)}, u32[]{:S(2)}) copy-start(bf16[32,7296]{1,0:T(8,128)(2,1)S(1)} %collective-permute-done.2.refs_3_) | copy-start | bytes 1400836
  72.4 9.7 %collective-permute-start.8 = (bf16[32,7296]{1,0:T(8,128)(2,1)S(1)}, bf16[32,7296]{1,0:T(8,128)(2,1)S(1)}, u32[]{:S(2)}, u32[]{:S(2)}) collective-permute-start(bf16[32,7296]{1,0:T(8,128)(2,1)S(1)} %collective-permute-done.7.refs_8_), channel_id=1, source_target_pairs={{0,8},{8,0},{16,24},{24,16},{32,40},{40,32},{48,56},{56,48},{1,9},... | collective-permute-start | bytes 1400840 | tf_op jit(solution)/shard_map/ppermute | solution.py:173
  74.4 7.7 %copy-start.8 = (bf16[32,7296]{1,0:T(8,128)(2,1)}, bf16[32,7296]{1,0:T(8,128)(2,1)S(1)}, u32[]{:S(2)}) copy-start(bf16[32,7296]{1,0:T(8,128)(2,1)S(1)} %collective-permute-done.4.refs_5_) | copy-start | bytes 1400836
  74.4 7.6 %collective-permute-start.10 = (bf16[32,7296]{1,0:T(8,128)(2,1)S(1)}, bf16[32,7296]{1,0:T(8,128)(2,1)S(1)}, u32[]{:S(2)}, u32[]{:S(2)}) collective-permute-start(bf16[32,7296]{1,0:T(8,128)(2,1)S(1)} %collective-permute-done.9.refs_10_), channel_id=1, source_target_pairs={{0,8},{8,0},{16,24},{24,16},{32,40},{40,32},{48,56},{56,48},{1,9},... | collective-permute-start | bytes 1400840 | tf_op jit(solution)/shard_map/ppermute | solution.py:173
  76.8 5.4 %copy-start.9 = (bf16[32,7296]{1,0:T(8,128)(2,1)}, bf16[32,7296]{1,0:T(8,128)(2,1)S(1)}, u32[]{:S(2)}) copy-start(bf16[32,7296]{1,0:T(8,128)(2,1)S(1)} %collective-permute-done.11.refs_12_) | copy-start | bytes 1400836
  76.8 5.3 %collective-permute-start.12 = (bf16[32,7296]{1,0:T(8,128)(2,1)S(1)}, bf16[32,7296]{1,0:T(8,128)(2,1)S(1)}, u32[]{:S(2)}, u32[]{:S(2)}) collective-permute-start(bf16[32,7296]{1,0:T(8,128)(2,1)S(1)} %collective-permute-done.11.refs_12_), channel_id=1, source_target_pairs={{0,8},{8,0},{16,24},{24,16},{32,40},{40,32},{48,56},{56,48},{1,9},... | collective-permute-start | bytes 1400840 | tf_op jit(solution)/shard_map/ppermute | solution.py:173
  80.1 3.8 %collective-permute-start.14 = (bf16[32,7296]{1,0:T(8,128)(2,1)S(1)}, bf16[32,7296]{1,0:T(8,128)(2,1)}, u32[]{:S(2)}, u32[]{:S(2)}) collective-permute-start(bf16[32,7296]{1,0:T(8,128)(2,1)S(1)} %collective-permute-done.13.refs_14_), channel_id=1, source_target_pairs={{0,8},{8,0},{16,24},{24,16},{32,40},{40,32},{48,56},{56,48},{1,9},... | collective-permute-start | bytes 1400840 | tf_op jit(solution)/shard_map/ppermute | solution.py:173
  98.8 6.1 %collective-permute-start.15 = (bf16[256,3712]{1,0:T(8,128)(2,1)}, bf16[256,3712]{1,0:T(8,128)(2,1)S(1)}, u32[]{:S(2)}, u32[]{:S(2)}) collective-permute-start(bf16[256,3712]{1,0:T(8,128)(2,1)} %get-tuple-element.32), channel_id=1, source_target_pairs={{0,8},{8,0},{16,24},{24,16},{32,40},{40,32},{48,56},{56,48},{1,9},... | collective-permute-start | bytes 5701640 | tf_op jit(solution)/shard_map/ppermute | solution.py:217
  108.0 30.5 %all-to-all-start.1 = ((bf16[8,32,1792]{2,1,0:T(8,128)(2,1)}), bf16[8,32,1792]{2,1,0:T(8,128)(2,1)S(1)}, u32[]{:S(2)}, u32[]{:S(2)}) async-start(bf16[8,32,1792]{2,1,0:T(8,128)(2,1)} %slice.17), calls=%async_computation.2 | async-start | bytes 1835008 | tf_op jit(solution)/shard_map/all_to_all | solution.py:221
  112.1 74.1 %all-gather.5.cloned.1.call-start = ((), (), s32[]{:S(2)}) async-start(), calls=%async_computation.7 | async-start | bytes 3096576 | tf_op jit(solution)/shard_map/all_gather | solution.py:223
  138.5 31.3 %all-to-all-start.2 = ((bf16[8,32,1920]{2,1,0:T(8,128)(2,1)}), bf16[8,32,1920]{2,1,0:T(8,128)(2,1)S(1)}, u32[]{:S(2)}, u32[]{:S(2)}) async-start(bf16[8,32,1920]{2,1,0:T(8,128)(2,1)} %slice.18), calls=%async_computation.3 | async-start | bytes 1966080 | tf_op jit(solution)/shard_map/all_to_all | solution.py:224
  145.6 34.6 %copy-start.15 = (s32[8,4]{0,1:T(4,128)S(1)}, s32[8,4]{0,1:T(4,128)}, u32[]{:S(2)}) copy-start(s32[8,4]{0,1:T(4,128)} %param.10) | copy-start | bytes 388
  (5 other events, 5.6 us)
Sparse Core Ops, SparseCore 0:
  26.3 46.7 all-gather.2
  93.7 44.4 reduce-scatter.1
  140.5 45.6 all-gather.4

commit v5 on v4

--- a/solution.py
+++ b/solution.py
@@ -115,22 +115,38 @@
 
 
 def unpack_kernel(sum_hbm, gate_hbm, up_hbm, down_hbm, held, turned, sems):
-    pieces = [pl.ds(n * LANES, LANES) for n in range(3)]
+    width = held.shape[1]
+    tiles = [
+        (n, target, pl.ds(first, STEP))
+        for n, target in enumerate((gate_hbm, up_hbm))
+        for first in range(0, width, STEP)
+    ]
+    total = len(tiles)
     arrivals = [
-        pltpu.make_async_copy(sum_hbm.at[piece], held.at[piece], sems.at[n])
-        for n, piece in enumerate(pieces)
+        pltpu.make_async_copy(
+            sum_hbm.at[pl.ds(n * LANES, LANES), span],
+            held.at[pl.ds(n * LANES, LANES), span],
+            sems.at[k],
+        )
+        for k, (n, _, span) in enumerate(tiles)
     ]
     for copy in arrivals:
         copy.start()
-    leaving = []
-    for n, target in enumerate((gate_hbm, up_hbm)):
-        arrivals[n].wait()
-        turned[n] = held[pieces[n], :].astype(jnp.float32).T.astype(jnp.bfloat16)
-        leaving.append(pltpu.make_async_copy(turned.at[n], target.at[0], sems.at[3 + n]))
+    leaving = [
+        pltpu.make_async_copy(
+            sum_hbm.at[pl.ds(2 * LANES, LANES)], down_hbm.at[0], sems.at[2 * total]
+        )
+    ]
+    leaving[0].start()
+    for k, (n, target, span) in enumerate(tiles):
+        arrivals[k].wait()
+        turned[n, span, :] = (
+            held[n * LANES : (n + 1) * LANES, span].astype(jnp.float32).T.astype(jnp.bfloat16)
+        )
+        leaving.append(
+            pltpu.make_async_copy(turned.at[n, span], target.at[0, span], sems.at[total + k])
+        )
         leaving[-1].start()
-    arrivals[2].wait()
-    leaving.append(pltpu.make_async_copy(held.at[pieces[2]], down_hbm.at[0], sems.at[5]))
-    leaving[-1].start()
     for copy in leaving:
         copy.wait()
 
@@ -248,9 +264,9 @@
         in_specs=[anywhere],
         out_specs=(anywhere, anywhere, anywhere),
         scratch_shapes=[
-            pltpu.VMEM((3 * LANES, width), jnp.bfloat16),
+            pltpu.VMEM((2 * LANES, width), jnp.bfloat16),
             pltpu.VMEM((2, width, LANES), jnp.bfloat16),
-            pltpu.SemaphoreType.DMA((6,)),
+            pltpu.SemaphoreType.DMA((4 * width // STEP + 1,)),
         ],
         compiler_params=params(),
         name="unpack",

time: 197 us -> 223 us (1.13)
  Pallas kernels: 17.8 us -> 43.7 us
    pallas_call x1, Pallas kernels: 3.07 us -> 29 us  [shards(): pl.pallas_call(unpack_kernel, out_shape=(jax.ShapeDtypeStruct((1, width,...]
  transfers between devices with their start and end apart: 21 -> 21, of which waited for: 10 -> 10; matrix products, arithmetic and copies ran while one was open for 3% -> 3% of each run, Pallas kernels for 3% -> 2%
where the time goes in v5:
time: 223 us; the launch traced here: 222 us
  waiting for transfers between devices  81.2 us (36%)
  starting transfers between devices  46.6 us (21%)
  Pallas kernels  43.7 us (20%)
  blocking collectives  24.1 us (11%)
  between operations  14.1 us (6%)
  other arithmetic  7.49 us (3%)
  local copies, waits for them, and re-layouts  4.52 us (2%)
    pallas_call x1, Pallas kernels, shards(): pl.pallas_call(unpack_kernel, out_shape=(jax.ShapeDtypeStruct((1, width,...  29 us
    all_to_all x1, waiting for transfers between devices, shards(): first = lax.all_to_all(chip[:, :, :cut], 'local', 0, 0, tiled=True)  25.4 us
    all_to_all x1, waiting for transfers between devices, shards(): rest = lax.all_to_all(rest, 'local', 0, 0, tiled=True)  24.1 us
    ppermute x7, waiting for transfers between devices, shards(): chains[which] = lax.ppermute(chains[which], ('node', 'local'), ring)  20.8 us
    ppermute x8, starting transfers between devices, shards(): swap = lambda piece: lax.ppermute(piece, 'node', cores)  17.5 us
    ppermute x7, starting transfers between devices, shards(): chains[which] = lax.ppermute(chains[which], ('node', 'local'), ring)  15.5 us
    all_to_all x1, blocking collectives, shards(): lax.all_to_all(jnp.broadcast_to(mine, (columns, count, wide)), 'node', 0,...  14.6 us
    pallas_call x1, Pallas kernels, shards(): pl.pallas_call(functools.partial(gradients_kernel, plan), out_shape=(jax....  9.53 us
  transfers between devices with their start and end apart: 21, of which 10 were waited for; matrix products, arithmetic and copies ran while one was open for 3% of the time, Pallas kernels for 2%

profile of v5, /device:TPU:2, one launch (start us, length us, event | category | flops | bytes accessed | tf_op | source)
XLA Modules:
  0.0 221.7 jit_solution(16834597024614627490)
XLA Ops:
  9.6 14.6 %all_to_all.20 = bf16[4,8,7296]{2,1,0:T(8,128)(2,1)S(1)} all-to-all(bf16[4,8,7296]{2,1,0:T(8,128)(2,1)S(1)} %broadcast_in_dim.31), channel_id=1, replica_groups={{0,16,32,48},{8,24,40,56},{1,17,33,49},{9,25,41,57},{2,18,34,50},{10,26..., dimensions={0} | all-to-all | bytes 933888 | tf_op jit(solution)/shard_map/all_to_all | solution.py:172
  24.2 2.0 pad_maximum_fusion
  26.2 1.9 collective-permute-start
  29.9 1.9 collective-permute-start.1
  31.8 4.1 %collective-permute-start.3 = (bf16[32,7296]{1,0:T(8,128)(2,1)S(1)}, bf16[32,7296]{1,0:T(8,128)(2,1)S(1)}, u32[]{:S(2)}, u32[]{:S(2)}) collective-permute-start(bf16[32,7296]{1,0:T(8,128)(2,1)S(1)} %collective-permute-done.refs_1_), channel_id=1, source_target_pairs={{0,1},{1,2},{2,3},{3,4},{4,5},{5,6},{6,7},{7,0},{8,15},{9,8},{10,9... | collective-permute-start | bytes 1400840 | tf_op jit(solution)/shard_map/ppermute | solution.py:194
  35.9 8.9 %collective-permute-done.1.refs_2_ = bf16[32,7296]{1,0:T(8,128)(2,1)S(1)} collective-permute-done((bf16[32,7296]{1,0:T(8,128)(2,1)S(1)}, bf16[32,7296]{1,0:T(8,128)(2,1)S(1)}, u32[]{:S(2)}, u32[]{:S(2)}) %collective-permute-start.1) | collective-permute-done | bytes 466976 | tf_op jit(solution)/shard_map/ppermute | solution.py:194
  44.8 1.9 collective-permute-start.5
  46.7 3.1 %collective-permute-done.3.refs_4_ = bf16[32,7296]{1,0:T(8,128)(2,1)S(1)} collective-permute-done((bf16[32,7296]{1,0:T(8,128)(2,1)S(1)}, bf16[32,7296]{1,0:T(8,128)(2,1)S(1)}, u32[]{:S(2)}, u32[]{:S(2)}) %collective-permute-start.3) | collective-permute-done | bytes 466976 | tf_op jit(solution)/shard_map/ppermute | solution.py:194
  49.8 1.9 collective-permute-start.7
  51.7 4.7 %collective-permute-done.5.refs_6_ = bf16[32,7296]{1,0:T(8,128)(2,1)S(1)} collective-permute-done((bf16[32,7296]{1,0:T(8,128)(2,1)S(1)}, bf16[32,7296]{1,0:T(8,128)(2,1)S(1)}, u32[]{:S(2)}, u32[]{:S(2)}) %collective-permute-start.5) | collective-permute-done | bytes 466976 | tf_op jit(solution)/shard_map/ppermute | solution.py:194
  56.5 1.9 collective-permute-start.9
  58.4 3.1 %collective-permute-start.2 = (bf16[32,7296]{1,0:T(8,128)(2,1)S(1)}, bf16[32,7296]{1,0:T(8,128)(2,1)S(1)}, u32[]{:S(2)}, u32[]{:S(2)}) collective-permute-start(bf16[32,7296]{1,0:T(8,128)(2,1)S(1)} %collective-permute-done.1.refs_2_), channel_id=1, source_target_pairs={{0,8},{8,0},{16,24},{24,16},{32,40},{40,32},{48,56},{56,48},{1,9},... | collective-permute-start | bytes 1400840 | tf_op jit(solution)/shard_map/ppermute | solution.py:189
  61.5 1.9 collective-permute-start.4
  63.4 1.9 collective-permute-start.11
  65.4 2.8 %collective-permute-done.9.refs_10_ = bf16[32,7296]{1,0:T(8,128)(2,1)S(1)} collective-permute-done((bf16[32,7296]{1,0:T(8,128)(2,1)S(1)}, bf16[32,7296]{1,0:T(8,128)(2,1)S(1)}, u32[]{:S(2)}, u32[]{:S(2)}) %collective-permute-start.9) | collective-permute-done | bytes 466976 | tf_op jit(solution)/shard_map/ppermute | solution.py:194
  70.1 2.3 %collective-permute-start.6 = (bf16[32,7296]{1,0:T(8,128)(2,1)S(1)}, bf16[32,7296]{1,0:T(8,128)(2,1)S(1)}, u32[]{:S(2)}, u32[]{:S(2)}) collective-permute-start(bf16[32,7296]{1,0:T(8,128)(2,1)S(1)} %collective-permute-done.5.refs_6_), channel_id=1, source_target_pairs={{0,8},{8,0},{16,24},{24,16},{32,40},{40,32},{48,56},{56,48},{1,9},... | collective-permute-start | bytes 1400840 | tf_op jit(solution)/shard_map/ppermute | solution.py:189
  72.4 2.0 collective-permute-start.8
  74.4 2.3 %collective-permute-start.10 = (bf16[32,7296]{1,0:T(8,128)(2,1)S(1)}, bf16[32,7296]{1,0:T(8,128)(2,1)S(1)}, u32[]{:S(2)}, u32[]{:S(2)}) collective-permute-start(bf16[32,7296]{1,0:T(8,128)(2,1)S(1)} %collective-permute-done.9.refs_10_), channel_id=1, source_target_pairs={{0,8},{8,0},{16,24},{24,16},{32,40},{40,32},{48,56},{56,48},{1,9},... | collective-permute-start | bytes 1400840 | tf_op jit(solution)/shard_map/ppermute | solution.py:189
  76.8 2.0 collective-permute-start.12
  80.1 1.9 collective-permute-start.14
  84.0 9.5 %gradients.1 = (bf16[384,3584]{1,0:T(8,128)(2,1)}, bf16[512,256]{1,0:T(8,128)(2,1)}, bf16[512,128]{1,0:T(8,128)(2,1)}) custom-call(bf16[3584,384]{1,0:T(8,128)(2,1)} %all-gather.3.cloned.1.call-done.w_hbm.w_ref, bf16[32,7296]{1,0:T(8,128)(2,1)} %bitcast.12, bf16[32,7296]{1,0:T(8,128)(2,1)} %copy-done.1, bf16[32,7296]{1,0:T(8,128)(2,1)} %copy-done.2, ...), custom_call_target="tpu_custom_call" | custom-call | tf_op jit(solution)/shard_map/gradients/pallas_call | solution.py:201
  93.6 5.2 %input_part.1 = (bf16[256,3712]{1,0:T(8,128)(2,1)}, bf16[256,3712]{1,0:T(8,128)(2,1)}) custom-call(bf16[512,256]{1,0:T(8,128)(2,1)} %get-tuple-element.29.back_ref, bf16[512,128]{1,0:T(8,128)(2,1)} %get-tuple-element.30.part_ref, bf16[3584,384]{1,0:T(8,128)(2,1)} %all-gather.3.cloned.1.call-done.w_hbm.w_ref), custom_call_target="tpu_custom_call" | custom-call | tf_op jit(solution)/shard_map/input_part/pallas_call | solution.py:222
  98.8 2.4 %collective-permute-start.15 = (bf16[256,3712]{1,0:T(8,128)(2,1)}, bf16[256,3712]{1,0:T(8,128)(2,1)S(1)}, u32[]{:S(2)}, u32[]{:S(2)}) collective-permute-start(bf16[256,3712]{1,0:T(8,128)(2,1)} %get-tuple-element.32), channel_id=1, source_target_pairs={{0,8},{8,0},{16,24},{24,16},{32,40},{40,32},{48,56},{56,48},{1,9},... | collective-permute-start | bytes 5701640 | tf_op jit(solution)/shard_map/ppermute | solution.py:233
  101.2 3.7 %collective-permute-done.15 = bf16[256,3712]{1,0:T(8,128)(2,1)S(1)} collective-permute-done((bf16[256,3712]{1,0:T(8,128)(2,1)}, bf16[256,3712]{1,0:T(8,128)(2,1)S(1)}, u32[]{:S(2)}, u32[]{:S(2)}) %collective-permute-start.15) | collective-permute-done | bytes 1900576 | tf_op jit(solution)/shard_map/ppermute | solution.py:233
  104.8 2.2 add_convert_fusion
  108.0 4.0 %all-to-all-start.1 = ((bf16[8,32,1792]{2,1,0:T(8,128)(2,1)}), bf16[8,32,1792]{2,1,0:T(8,128)(2,1)S(1)}, u32[]{:S(2)}, u32[]{:S(2)}) async-start(bf16[8,32,1792]{2,1,0:T(8,128)(2,1)} %slice.17), calls=%async_computation.2 | async-start | bytes 1835008 | tf_op jit(solution)/shard_map/all_to_all | solution.py:237
  113.1 25.4 %all-to-all-done.1 = bf16[8,32,1792]{2,1,0:T(8,128)(2,1)S(1)} async-done(((bf16[8,32,1792]{2,1,0:T(8,128)(2,1)}), bf16[8,32,1792]{2,1,0:T(8,128)(2,1)S(1)}, u32[]{:S(2)}, u32[]{:S(2)}) %all-to-all-start.1) | async-done | bytes 917536 | tf_op jit(solution)/shard_map/all_to_all | solution.py:237
  138.5 7.0 %all-to-all-start.2 = ((bf16[8,32,1920]{2,1,0:T(8,128)(2,1)}), bf16[8,32,1920]{2,1,0:T(8,128)(2,1)S(1)}, u32[]{:S(2)}, u32[]{:S(2)}) async-start(bf16[8,32,1920]{2,1,0:T(8,128)(2,1)} %slice.18), calls=%async_computation.3 | async-start | bytes 1966080 | tf_op jit(solution)/shard_map/all_to_all | solution.py:240
  145.7 24.1 %all-to-all-done.2 = bf16[8,32,1920]{2,1,0:T(8,128)(2,1)S(1)} async-done(((bf16[8,32,1920]{2,1,0:T(8,128)(2,1)}), bf16[8,32,1920]{2,1,0:T(8,128)(2,1)S(1)}, u32[]{:S(2)}, u32[]{:S(2)}) %all-to-all-start.2) | async-done | bytes 983072 | tf_op jit(solution)/shard_map/all_to_all | solution.py:240
  170.0 9.5 %all_to_all.21 = bf16[4,8,3712]{2,1,0:T(8,128)(2,1)S(1)} all-to-all(bf16[4,8,3712]{2,1,0:T(8,128)(2,1)S(1)} %maximum_bitcast_fusion), channel_id=1, replica_groups={{0,16,32,48},{8,24,40,56},{1,17,33,49},{9,25,41,57},{2,18,34,50},{10,26..., dimensions={0} | all-to-all | bytes 475136 | tf_op jit(solution)/shard_map/all_to_all | solution.py:245
  180.9 5.3 %all-gather.5.cloned.1.call-done.sum_hbm = bf16[384,3584]{1,0:T(8,128)(2,1)} async-done(((bf16[48,3584]{1,0:T(8,128)(2,1)}), bf16[384,3584]{1,0:T(8,128)(2,1)}) %all-gather.5.cloned.1.call-update) | async-done | bytes 2752528 | tf_op jit(solution)/shard_map/all_gather | solution.py:239
  186.2 29.0 %unpack.1 = (bf16[1,3584,128]{2,1,0:T(8,128)(2,1)}, bf16[1,3584,128]{2,1,0:T(8,128)(2,1)}, bf16[1,128,3584]{2,1,0:T(8,128)(2,1)}) custom-call(bf16[384,3584]{1,0:T(8,128)(2,1)} %all-gather.5.cloned.1.call-done.sum_hbm), custom_call_target="tpu_custom_call" | custom-call | tf_op jit(solution)/shard_map/unpack/pallas_call | solution.py:257
  (65 shorter events, 13.1 us)
Async XLA Ops:
  7.2 76.8 %all-gather.3.cloned.1.call-start = ((), (), s32[]{:S(2)}) async-start(), calls=%async_computation.5 | async-start | bytes 3096576 | tf_op jit(solution)/shard_map/all_gather | solution.py:182
  24.2 59.8 %copy-start = (bf16[4,8,7296]{2,1,0:T(8,128)(2,1)}, bf16[4,8,7296]{2,1,0:T(8,128)(2,1)S(1)}, u32[]{:S(2)}) copy-start(bf16[4,8,7296]{2,1,0:T(8,128)(2,1)S(1)} %all_to_all.20) | copy-start | bytes 1400836
  26.1 112.4 %reduce-scatter.2.cloned.1.call-start = ((), (), s32[]{:S(2)}) async-start(), calls=%async_computation.6 | async-start | bytes 3096576 | tf_op jit(solution)/shard_map/reduce_scatter | solution.py:220
  26.2 3.7 %collective-permute-start = (bf16[32,7296]{1,0:T(8,128)(2,1)S(1)}, bf16[32,7296]{1,0:T(8,128)(2,1)S(1)}, u32[]{:S(2)}, u32[]{:S(2)}) collective-permute-start(bf16[32,7296]{1,0:T(8,128)(2,1)S(1)} %bitcast.10), channel_id=1, source_target_pairs={{0,8},{8,0},{16,24},{24,16},{32,40},{40,32},{48,56},{56,48},{1,9},... | collective-permute-start | bytes 1400840 | tf_op jit(solution)/shard_map/ppermute | solution.py:189
  29.9 54.0 %copy-start.1 = (bf16[32,7296]{1,0:T(8,128)(2,1)}, bf16[32,7296]{1,0:T(8,128)(2,1)S(1)}, u32[]{:S(2)}) copy-start(bf16[32,7296]{1,0:T(8,128)(2,1)S(1)} %collective-permute-done.refs_1_) | copy-start | bytes 1400836
  29.9 14.9 %collective-permute-start.1 = (bf16[32,7296]{1,0:T(8,128)(2,1)S(1)}, bf16[32,7296]{1,0:T(8,128)(2,1)S(1)}, u32[]{:S(2)}, u32[]{:S(2)}) collective-permute-start(bf16[32,7296]{1,0:T(8,128)(2,1)S(1)} %bitcast.11), channel_id=1, source_target_pairs={{0,1},{1,2},{2,3},{3,4},{4,5},{5,6},{6,7},{7,0},{8,15},{9,8},{10,9... | collective-permute-start | bytes 1400840 | tf_op jit(solution)/shard_map/ppermute | solution.py:194
  31.8 18.0 %collective-permute-start.3 = (bf16[32,7296]{1,0:T(8,128)(2,1)S(1)}, bf16[32,7296]{1,0:T(8,128)(2,1)S(1)}, u32[]{:S(2)}, u32[]{:S(2)}) collective-permute-start(bf16[32,7296]{1,0:T(8,128)(2,1)S(1)} %collective-permute-done.refs_1_), channel_id=1, source_target_pairs={{0,1},{1,2},{2,3},{3,4},{4,5},{5,6},{6,7},{7,0},{8,15},{9,8},{10,9... | collective-permute-start | bytes 1400840 | tf_op jit(solution)/shard_map/ppermute | solution.py:194
  44.8 39.1 %copy-start.2 = (bf16[32,7296]{1,0:T(8,128)(2,1)}, bf16[32,7296]{1,0:T(8,128)(2,1)S(1)}, u32[]{:S(2)}) copy-start(bf16[32,7296]{1,0:T(8,128)(2,1)S(1)} %collective-permute-done.1.refs_2_) | copy-start | bytes 1400836
  44.8 11.7 %collective-permute-start.5 = (bf16[32,7296]{1,0:T(8,128)(2,1)S(1)}, bf16[32,7296]{1,0:T(8,128)(2,1)S(1)}, u32[]{:S(2)}, u32[]{:S(2)}) collective-permute-start(bf16[32,7296]{1,0:T(8,128)(2,1)S(1)} %collective-permute-done.1.refs_2_), channel_id=1, source_target_pairs={{0,1},{1,2},{2,3},{3,4},{4,5},{5,6},{6,7},{7,0},{8,15},{9,8},{10,9... | collective-permute-start | bytes 1400840 | tf_op jit(solution)/shard_map/ppermute | solution.py:194
  49.8 34.1 %copy-start.3 = (bf16[32,7296]{1,0:T(8,128)(2,1)}, bf16[32,7296]{1,0:T(8,128)(2,1)S(1)}, u32[]{:S(2)}) copy-start(bf16[32,7296]{1,0:T(8,128)(2,1)S(1)} %collective-permute-done.3.refs_4_) | copy-start | bytes 1400836
  49.8 13.6 %collective-permute-start.7 = (bf16[32,7296]{1,0:T(8,128)(2,1)S(1)}, bf16[32,7296]{1,0:T(8,128)(2,1)S(1)}, u32[]{:S(2)}, u32[]{:S(2)}) collective-permute-start(bf16[32,7296]{1,0:T(8,128)(2,1)S(1)} %collective-permute-done.3.refs_4_), channel_id=1, source_target_pairs={{0,1},{1,2},{2,3},{3,4},{4,5},{5,6},{6,7},{7,0},{8,15},{9,8},{10,9... | collective-permute-start | bytes 1400840 | tf_op jit(solution)/shard_map/ppermute | solution.py:194
  56.5 27.5 %copy-start.4 = (bf16[32,7296]{1,0:T(8,128)(2,1)}, bf16[32,7296]{1,0:T(8,128)(2,1)S(1)}, u32[]{:S(2)}) copy-start(bf16[32,7296]{1,0:T(8,128)(2,1)S(1)} %collective-permute-done.5.refs_6_) | copy-start | bytes 1400836
  56.5 11.7 %collective-permute-start.9 = (bf16[32,7296]{1,0:T(8,128)(2,1)S(1)}, bf16[32,7296]{1,0:T(8,128)(2,1)S(1)}, u32[]{:S(2)}, u32[]{:S(2)}) collective-permute-start(bf16[32,7296]{1,0:T(8,128)(2,1)S(1)} %collective-permute-done.5.refs_6_), channel_id=1, source_target_pairs={{0,1},{1,2},{2,3},{3,4},{4,5},{5,6},{6,7},{7,0},{8,15},{9,8},{10,9... | collective-permute-start | bytes 1400840 | tf_op jit(solution)/shard_map/ppermute | solution.py:194
  58.4 14.0 %collective-permute-start.2 = (bf16[32,7296]{1,0:T(8,128)(2,1)S(1)}, bf16[32,7296]{1,0:T(8,128)(2,1)S(1)}, u32[]{:S(2)}, u32[]{:S(2)}) collective-permute-start(bf16[32,7296]{1,0:T(8,128)(2,1)S(1)} %collective-permute-done.1.refs_2_), channel_id=1, source_target_pairs={{0,8},{8,0},{16,24},{24,16},{32,40},{40,32},{48,56},{56,48},{1,9},... | collective-permute-start | bytes 1400840 | tf_op jit(solution)/shard_map/ppermute | solution.py:189
  61.5 12.9 %collective-permute-start.4 = (bf16[32,7296]{1,0:T(8,128)(2,1)S(1)}, bf16[32,7296]{1,0:T(8,128)(2,1)S(1)}, u32[]{:S(2)}, u32[]{:S(2)}) collective-permute-start(bf16[32,7296]{1,0:T(8,128)(2,1)S(1)} %collective-permute-done.3.refs_4_), channel_id=1, source_target_pairs={{0,8},{8,0},{16,24},{24,16},{32,40},{40,32},{48,56},{56,48},{1,9},... | collective-permute-start | bytes 1400840 | tf_op jit(solution)/shard_map/ppermute | solution.py:189
  63.4 20.6 %copy-start.5 = (bf16[32,7296]{1,0:T(8,128)(2,1)}, bf16[32,7296]{1,0:T(8,128)(2,1)S(1)}, u32[]{:S(2)}) copy-start(bf16[32,7296]{1,0:T(8,128)(2,1)S(1)} %collective-permute-done.7.refs_8_) | copy-start | bytes 1400836
  63.4 13.3 %collective-permute-start.11 = (bf16[32,7296]{1,0:T(8,128)(2,1)S(1)}, bf16[32,7296]{1,0:T(8,128)(2,1)S(1)}, u32[]{:S(2)}, u32[]{:S(2)}) collective-permute-start(bf16[32,7296]{1,0:T(8,128)(2,1)S(1)} %collective-permute-done.7.refs_8_), channel_id=1, source_target_pairs={{0,1},{1,2},{2,3},{3,4},{4,5},{5,6},{6,7},{7,0},{8,15},{9,8},{10,9... | collective-permute-start | bytes 1400840 | tf_op jit(solution)/shard_map/ppermute | solution.py:194
  68.1 15.9 %copy-start.6 = (bf16[32,7296]{1,0:T(8,128)(2,1)}, bf16[32,7296]{1,0:T(8,128)(2,1)S(1)}, u32[]{:S(2)}) copy-start(bf16[32,7296]{1,0:T(8,128)(2,1)S(1)} %collective-permute-done.9.refs_10_) | copy-start | bytes 1400836
  68.1 12.0 %collective-permute-start.13 = (bf16[32,7296]{1,0:T(8,128)(2,1)S(1)}, bf16[32,7296]{1,0:T(8,128)(2,1)S(1)}, u32[]{:S(2)}, u32[]{:S(2)}) collective-permute-start(bf16[32,7296]{1,0:T(8,128)(2,1)S(1)} %collective-permute-done.9.refs_10_), channel_id=1, source_target_pairs={{0,1},{1,2},{2,3},{3,4},{4,5},{5,6},{6,7},{7,0},{8,15},{9,8},{10,9... | collective-permute-start | bytes 1400840 | tf_op jit(solution)/shard_map/ppermute | solution.py:194
  70.1 12.0 %collective-permute-start.6 = (bf16[32,7296]{1,0:T(8,128)(2,1)S(1)}, bf16[32,7296]{1,0:T(8,128)(2,1)S(1)}, u32[]{:S(2)}, u32[]{:S(2)}) collective-permute-start(bf16[32,7296]{1,0:T(8,128)(2,1)S(1)} %collective-permute-done.5.refs_6_), channel_id=1, source_target_pairs={{0,8},{8,0},{16,24},{24,16},{32,40},{40,32},{48,56},{56,48},{1,9},... | collective-permute-start | bytes 1400840 | tf_op jit(solution)/shard_map/ppermute | solution.py:189
  72.4 9.7 %copy-start.7 = (bf16[32,7296]{1,0:T(8,128)(2,1)}, bf16[32,7296]{1,0:T(8,128)(2,1)S(1)}, u32[]{:S(2)}) copy-start(bf16[32,7296]{1,0:T(8,128)(2,1)S(1)} %collective-permute-done.2.refs_3_) | copy-start | bytes 1400836
  72.4 9.7 %collective-permute-start.8 = (bf16[32,7296]{1,0:T(8,128)(2,1)S(1)}, bf16[32,7296]{1,0:T(8,128)(2,1)S(1)}, u32[]{:S(2)}, u32[]{:S(2)}) collective-permute-start(bf16[32,7296]{1,0:T(8,128)(2,1)S(1)} %collective-permute-done.7.refs_8_), channel_id=1, source_target_pairs={{0,8},{8,0},{16,24},{24,16},{32,40},{40,32},{48,56},{56,48},{1,9},... | collective-permute-start | bytes 1400840 | tf_op jit(solution)/shard_map/ppermute | solution.py:189
  74.4 7.7 %copy-start.8 = (bf16[32,7296]{1,0:T(8,128)(2,1)}, bf16[32,7296]{1,0:T(8,128)(2,1)S(1)}, u32[]{:S(2)}) copy-start(bf16[32,7296]{1,0:T(8,128)(2,1)S(1)} %collective-permute-done.4.refs_5_) | copy-start | bytes 1400836
  74.4 7.6 %collective-permute-start.10 = (bf16[32,7296]{1,0:T(8,128)(2,1)S(1)}, bf16[32,7296]{1,0:T(8,128)(2,1)S(1)}, u32[]{:S(2)}, u32[]{:S(2)}) collective-permute-start(bf16[32,7296]{1,0:T(8,128)(2,1)S(1)} %collective-permute-done.9.refs_10_), channel_id=1, source_target_pairs={{0,8},{8,0},{16,24},{24,16},{32,40},{40,32},{48,56},{56,48},{1,9},... | collective-permute-start | bytes 1400840 | tf_op jit(solution)/shard_map/ppermute | solution.py:189
  76.8 5.4 %copy-start.9 = (bf16[32,7296]{1,0:T(8,128)(2,1)}, bf16[32,7296]{1,0:T(8,128)(2,1)S(1)}, u32[]{:S(2)}) copy-start(bf16[32,7296]{1,0:T(8,128)(2,1)S(1)} %collective-permute-done.11.refs_12_) | copy-start | bytes 1400836
  76.8 5.3 %collective-permute-start.12 = (bf16[32,7296]{1,0:T(8,128)(2,1)S(1)}, bf16[32,7296]{1,0:T(8,128)(2,1)S(1)}, u32[]{:S(2)}, u32[]{:S(2)}) collective-permute-start(bf16[32,7296]{1,0:T(8,128)(2,1)S(1)} %collective-permute-done.11.refs_12_), channel_id=1, source_target_pairs={{0,8},{8,0},{16,24},{24,16},{32,40},{40,32},{48,56},{56,48},{1,9},... | collective-permute-start | bytes 1400840 | tf_op jit(solution)/shard_map/ppermute | solution.py:189
  80.1 3.8 %collective-permute-start.14 = (bf16[32,7296]{1,0:T(8,128)(2,1)S(1)}, bf16[32,7296]{1,0:T(8,128)(2,1)}, u32[]{:S(2)}, u32[]{:S(2)}) collective-permute-start(bf16[32,7296]{1,0:T(8,128)(2,1)S(1)} %collective-permute-done.13.refs_14_), channel_id=1, source_target_pairs={{0,8},{8,0},{16,24},{24,16},{32,40},{40,32},{48,56},{56,48},{1,9},... | collective-permute-start | bytes 1400840 | tf_op jit(solution)/shard_map/ppermute | solution.py:189
  98.8 6.1 %collective-permute-start.15 = (bf16[256,3712]{1,0:T(8,128)(2,1)}, bf16[256,3712]{1,0:T(8,128)(2,1)S(1)}, u32[]{:S(2)}, u32[]{:S(2)}) collective-permute-start(bf16[256,3712]{1,0:T(8,128)(2,1)} %get-tuple-element.32), channel_id=1, source_target_pairs={{0,8},{8,0},{16,24},{24,16},{32,40},{40,32},{48,56},{56,48},{1,9},... | collective-permute-start | bytes 5701640 | tf_op jit(solution)/shard_map/ppermute | solution.py:233
  108.0 30.5 %all-to-all-start.1 = ((bf16[8,32,1792]{2,1,0:T(8,128)(2,1)}), bf16[8,32,1792]{2,1,0:T(8,128)(2,1)S(1)}, u32[]{:S(2)}, u32[]{:S(2)}) async-start(bf16[8,32,1792]{2,1,0:T(8,128)(2,1)} %slice.17), calls=%async_computation.2 | async-start | bytes 1835008 | tf_op jit(solution)/shard_map/all_to_all | solution.py:237
  112.1 74.1 %all-gather.5.cloned.1.call-start = ((), (), s32[]{:S(2)}) async-start(), calls=%async_computation.7 | async-start | bytes 3096576 | tf_op jit(solution)/shard_map/all_gather | solution.py:239
  138.5 31.3 %all-to-all-start.2 = ((bf16[8,32,1920]{2,1,0:T(8,128)(2,1)}), bf16[8,32,1920]{2,1,0:T(8,128)(2,1)S(1)}, u32[]{:S(2)}, u32[]{:S(2)}) async-start(bf16[8,32,1920]{2,1,0:T(8,128)(2,1)} %slice.18), calls=%async_computation.3 | async-start | bytes 1966080 | tf_op jit(solution)/shard_map/all_to_all | solution.py:240
  145.6 34.6 %copy-start.15 = (s32[8,4]{0,1:T(4,128)S(1)}, s32[8,4]{0,1:T(4,128)}, u32[]{:S(2)}) copy-start(s32[8,4]{0,1:T(4,128)} %param.10) | copy-start | bytes 388
  (5 other events, 5.6 us)
Sparse Core Ops, SparseCore 0:
  26.3 46.7 all-gather.2
  93.7 44.4 reduce-scatter.1
  140.5 45.6 all-gather.4
